TPU v7x, 32 devices: a whole 2x2x4 slice. The times are simulated.
32 devices in a mesh: dp: 8 (over z, y), seq: 4 (over x, core).
Axes of the slice: x: 2, y: 2, z: 4, core: 2. Of those that a mesh axis runs over, the one named last changes fastest.
Arguments:
- inputs: bfloat16 [24, 2048, 512], P('dp', 'seq'), may hold values from -6 to 6
- gains: float32 [1, 2, 512], replicated, may hold values from 0.5 to 1.5
- w_qkv: bfloat16 [1, 512, 1536], replicated, may hold values from -0.125 to 0.125
- w_out: bfloat16 [1, 512, 512], replicated, may hold values from -1 to 1
- ffn_weight: bfloat16 [1, 2, 2048, 512], P(None, None, ('dp', 'seq')), may hold values from -0.25 to 0.25
- omega: bfloat16 [1, 8, 256, 64], replicated, may hold values from -5 to 5
- cotangent: bfloat16 [24, 2048, 512], P('dp', 'seq'), may hold values from -6 to 6
Outputs:
- outputs: bfloat16 [24, 2048, 512], P('dp', 'seq')
- grad_inputs: float32 [24, 2048, 512], P('dp', 'seq')
- grad_gains: float32 [1, 2, 512], replicated
- grad_w_qkv: float32 [1, 512, 1536], replicated
- grad_w_out: float32 [1, 512, 512], replicated
- grad_ffn: float32 [1, 2, 2048, 512], P(None, None, ('dp', 'seq'))
All inputs are finite; a program needn't handle non-finite values.
Results may differ from a plain program's by a relative error of at most 0.017.
Values may be sent and summed in bfloat16 or wider, within the bound.
No kernel may reach another device: no remote copies, remote signals or barrier semaphores. Data moves between devices by JAX's collectives and lax.ppermute only.
A program may use at most 320 MiB of HBM per device.

v0:
```python
import math

import jax
import jax.numpy as jnp
from jax import lax
from jax.sharding import PartitionSpec as P

epsilon = 1e-05
highest = lax.Precision.HIGHEST


def prefix(part, axis, combine, identity):
    place = lax.axis_index(axis)
    gathered = jax.tree.map(lambda a: lax.all_gather(a, axis), part)
    state = jax.tree.map(lambda a, e: jnp.zeros_like(a) + jnp.asarray(e, a.dtype), part, identity)

    def one(step, state):
        return combine(
            state, jax.tree.map(lambda a: lax.dynamic_index_in_dim(a, step, 0, False), gathered)
        )

    return lax.fori_loop(0, place, one, state)


def entering(array, axis, combine, identity):
    count, place = (lax.axis_size(axis), lax.axis_index(axis))
    everything = jax.tree.map(
        lambda part, kind: lax.all_gather(part.astype(kind), axis),
        array,
        jax.tree.map(lambda a: jnp.bfloat16 if a.dtype == jnp.float32 else a.dtype, array),
    )
    start = jax.tree.map(
        lambda part, zero: jnp.broadcast_to(jnp.asarray(zero, part.dtype), part.shape),
        array,
        identity,
    )

    def step(k, before):
        at = count - 1 - k
        reached = at > place
        new = combine(
            before, jax.tree.map(lambda part, own: part[at].astype(own.dtype), everything, array)
        )
        return jax.tree.map(lambda a, b: jnp.where(reached, a, b), new, before)

    return lax.fori_loop(0, count, step, start)


def layer_norm(values, gain_row):
    center = values - jnp.mean(values, axis=-1, keepdims=True)
    spread = jnp.mean(center * center, axis=-1, keepdims=True)
    return center * lax.rsqrt(spread + epsilon) * gain_row


def feature_map(projected, queries):
    head_dim = queries.shape[-1]
    feature_scale = head_dim ** (-0.25)
    energy = jnp.sum(queries * queries, axis=-1, keepdims=True)
    return jnp.exp(
        feature_scale * projected - 0.5 * feature_scale * feature_scale * energy
    ) / math.sqrt(projected.shape[-1])


def gelu_exact(values):
    return jax.nn.gelu(values, approximate=False)


def divide_heads(numerator, denominator):
    return numerator / denominator[:, :, None]


def add_states(earlier, later):
    return (earlier[0] + later[0], earlier[1] + later[1])


def contract_rows(left, right):
    return lax.dot_general(
        left, right, (((0,), (0,)), ((), ())), preferred_element_type=jnp.float32
    )


def contract_cols(left, right):
    return lax.dot_general(
        left, right, (((1,), (1,)), ((), ())), preferred_element_type=jnp.float32
    )


def causal_mask(block_len):
    positions = jnp.arange(block_len)
    return (positions[:, None] >= positions[None, :]).astype(jnp.float32)


def attention_forward(stream, gain_row, w_qkv, w_out, omega_layer):
    row_count, model_width = stream.shape
    head_count, feature_count, head_dim = omega_layer.shape
    hidden_low = layer_norm(stream, gain_row).astype(jnp.bfloat16)
    qkv_low = jnp.dot(hidden_low, w_qkv, preferred_element_type=jnp.float32).astype(jnp.bfloat16)
    queries = qkv_low[:, :model_width].reshape(row_count, head_count, head_dim)
    key_rows = qkv_low[:, model_width : 2 * model_width].reshape(row_count, head_count, head_dim)
    value_rows = qkv_low[:, 2 * model_width :].reshape(row_count, head_count, head_dim)
    proj_q = jnp.einsum("thd,hfd->thf", queries, omega_layer, preferred_element_type=jnp.float32)
    proj_k = jnp.einsum("thd,hfd->thf", key_rows, omega_layer, preferred_element_type=jnp.float32)
    phi_q = feature_map(proj_q, queries.astype(jnp.float32)).astype(jnp.bfloat16)
    phi_k = feature_map(proj_k, key_rows.astype(jnp.float32)).astype(jnp.bfloat16)
    causal = causal_mask(row_count)
    scores = (
        jnp.einsum("thf,shf->hts", phi_q, phi_k, preferred_element_type=jnp.float32) * causal[None]
    )
    local_state = jnp.einsum("thf,thd->hfd", phi_k, value_rows, preferred_element_type=jnp.float32)
    local_norm = jnp.sum(phi_k.astype(jnp.float32), axis=0)
    empty = (
        jnp.zeros((head_count, feature_count, head_dim), jnp.float32),
        jnp.zeros((head_count, feature_count), jnp.float32),
    )
    prev_state, prev_norm = prefix((local_state, local_norm), "seq", add_states, empty)
    phi_q_full = phi_q.astype(jnp.float32)
    numerator = jnp.einsum(
        "hts,shd->thd", scores.astype(jnp.bfloat16), value_rows, preferred_element_type=jnp.float32
    ) + jnp.einsum("thf,hfd->thd", phi_q_full, prev_state, precision=highest)
    denominator = jnp.sum(scores, axis=-1).T + jnp.einsum(
        "thf,hf->th", phi_q_full, prev_norm, precision=highest
    )
    mixed_low = (
        divide_heads(numerator, denominator).reshape(row_count, model_width).astype(jnp.bfloat16)
    )
    branch = jnp.dot(mixed_low, w_out, preferred_element_type=jnp.float32)
    saved_forward = (
        stream,
        hidden_low,
        qkv_low,
        proj_q,
        proj_k,
        phi_q,
        phi_k,
        scores,
        prev_state,
        prev_norm,
        numerator,
        denominator,
        mixed_low,
    )
    return (stream + branch, saved_forward)


def attention_backward(grad_out, gain_row, w_qkv, w_out, omega_layer, saved_forward):
    (
        stream,
        hidden_low,
        qkv_low,
        proj_q,
        proj_k,
        phi_q,
        phi_k,
        scores,
        prev_state,
        prev_norm,
        numerator,
        denominator,
        mixed_low,
    ) = saved_forward
    row_count, model_width = stream.shape
    head_count, feature_count, head_dim = omega_layer.shape
    grad_low = grad_out.astype(jnp.bfloat16)
    grad_wout = contract_rows(mixed_low, grad_low)
    grad_mixed = contract_cols(grad_low, w_out).reshape(row_count, head_count, head_dim)
    _, divide_back = jax.vjp(divide_heads, numerator, denominator)
    grad_numer, grad_denom = divide_back(grad_mixed)
    grad_numer_low = grad_numer.astype(jnp.bfloat16)
    value_rows = qkv_low[:, 2 * model_width :].reshape(row_count, head_count, head_dim)
    causal = causal_mask(row_count)
    grad_scores = (
        jnp.einsum("thd,shd->hts", grad_numer_low, value_rows, preferred_element_type=jnp.float32)
        + grad_denom.T[:, :, None]
    )
    grad_scores_low = (grad_scores * causal[None]).astype(jnp.bfloat16)
    grad_values = jnp.einsum(
        "hts,thd->shd",
        scores.astype(jnp.bfloat16),
        grad_numer_low,
        preferred_element_type=jnp.float32,
    )
    grad_prev_state = jnp.einsum(
        "thf,thd->hfd", phi_q, grad_numer_low, preferred_element_type=jnp.float32
    )
    grad_prev_norm = jnp.einsum(
        "th,thf->hf", grad_denom, phi_q.astype(jnp.float32), precision=highest
    )
    grad_phi_q = (
        jnp.einsum(
            "thd,hfd->thf", grad_numer_low.astype(jnp.float32), prev_state, precision=highest
        )
        + grad_denom[:, :, None] * prev_norm[None]
        + jnp.einsum("hts,shf->thf", grad_scores_low, phi_k, preferred_element_type=jnp.float32)
    )
    empty = (
        jnp.zeros((head_count, feature_count, head_dim), jnp.float32),
        jnp.zeros((head_count, feature_count), jnp.float32),
    )
    later_state, later_norm = entering((grad_prev_state, grad_prev_norm), "seq", add_states, empty)
    grad_phi_k = (
        jnp.einsum("hts,thf->shf", grad_scores_low, phi_q, preferred_element_type=jnp.float32)
        + jnp.einsum("thd,hfd->thf", value_rows.astype(jnp.float32), later_state, precision=highest)
        + later_norm[None]
    )
    grad_values = grad_values + jnp.einsum(
        "thf,hfd->thd", phi_k.astype(jnp.float32), later_state, precision=highest
    )

    def feature_back(projected, point_vals, grad_phi):
        _, pullback = jax.vjp(feature_map, projected, point_vals)
        grad_proj, grad_point = pullback(grad_phi)
        return (
            jnp.einsum(
                "thf,hfd->thd",
                grad_proj.astype(jnp.bfloat16),
                omega_layer,
                preferred_element_type=jnp.float32,
            )
            + grad_point
        )

    grad_query = feature_back(
        proj_q,
        qkv_low[:, :model_width].reshape(row_count, head_count, head_dim).astype(jnp.float32),
        grad_phi_q,
    )
    grad_key = feature_back(
        proj_k,
        qkv_low[:, model_width : 2 * model_width]
        .reshape(row_count, head_count, head_dim)
        .astype(jnp.float32),
        grad_phi_k,
    )
    grad_qkv = jnp.concatenate(
        [
            grad_query.reshape(row_count, model_width),
            grad_key.reshape(row_count, model_width),
            grad_values.reshape(row_count, model_width),
        ],
        axis=1,
    ).astype(jnp.bfloat16)
    grad_wqkv = contract_rows(hidden_low, grad_qkv)
    grad_hidden = contract_cols(grad_qkv, w_qkv)
    _, norm_back = jax.vjp(layer_norm, stream, gain_row)
    grad_stream, grad_gain = norm_back(grad_hidden)
    return (grad_out + grad_stream, grad_gain, grad_wqkv, grad_wout)


def fetch_rows(weight_pair):
    return lax.all_gather(weight_pair, "dp", axis=1, tiled=True)


def mlp_forward(stream, gain_row, weight_pair):
    hidden_low = layer_norm(stream, gain_row).astype(jnp.bfloat16)
    pair_rows = fetch_rows(weight_pair)
    rows_in = lax.all_gather(hidden_low, "seq", axis=0, tiled=True)
    pre_act = contract_cols(rows_in, pair_rows[0])
    act_low = gelu_exact(pre_act).astype(jnp.bfloat16)
    partial_value = jnp.dot(act_low, pair_rows[1], preferred_element_type=jnp.float32)
    branch = lax.psum_scatter(
        partial_value.astype(jnp.bfloat16), "seq", scatter_dimension=0, tiled=True
    ).astype(jnp.float32)
    return (stream + branch, rows_in)


def mlp_backward(grad_out, stream, gain_row, weight_pair, rows_in):
    grad_low = grad_out.astype(jnp.bfloat16)
    pair_rows = fetch_rows(weight_pair)
    grad_rows = lax.all_gather(grad_low, "seq", axis=0, tiled=True)
    pre_act = contract_cols(rows_in, pair_rows[0])
    act_vals, gelu_back = jax.vjp(gelu_exact, pre_act)
    act_low = act_vals.astype(jnp.bfloat16)
    grad_act = contract_cols(grad_rows, pair_rows[1])
    grad_pre = gelu_back(grad_act)[0].astype(jnp.bfloat16)
    grad_down = contract_rows(act_low, grad_rows)
    grad_up = contract_rows(grad_pre, rows_in)
    partial_value = jnp.dot(grad_pre, pair_rows[0], preferred_element_type=jnp.float32)
    grad_hidden = lax.psum_scatter(partial_value, "seq", scatter_dimension=0, tiled=True)
    _, norm_back = jax.vjp(layer_norm, stream, gain_row)
    grad_stream, grad_gain = norm_back(grad_hidden)
    return (grad_out + grad_stream, grad_gain, jnp.stack([grad_up, grad_down]))


def on_device(inputs, gains, w_qkv, w_out, ffn_weight, omega, cotangent):
    batch_count = inputs.shape[0]
    layer_count = w_qkv.shape[0]
    model_width = inputs.shape[2]
    unit_count = ffn_weight.shape[2] * lax.axis_size("dp")
    outputs = []
    stored = []
    for batch_index in range(batch_count):
        stream = inputs[batch_index].astype(jnp.float32)
        layer_index = 0
        stream, attn_saved = attention_forward(
            stream,
            gains[layer_index, 0],
            w_qkv[layer_index],
            w_out[layer_index],
            omega[layer_index],
        )
        mlp_input = stream
        stream, rows_in = mlp_forward(stream, gains[layer_index, 1], ffn_weight[layer_index])
        layer_saves = [(attn_saved, mlp_input, rows_in)]
        outputs.append(stream.astype(jnp.bfloat16))
        stored.append(layer_saves)
    acc_gain = jnp.zeros(gains.shape, jnp.float32)
    acc_qkv = jnp.zeros(w_qkv.shape, jnp.float32)
    acc_out = jnp.zeros(w_out.shape, jnp.float32)
    acc_ffn = jnp.zeros((layer_count, 2, unit_count, model_width), jnp.float32)
    grads_in = []
    for batch_index in range(batch_count):
        grad_stream = cotangent[batch_index].astype(jnp.float32)
        for layer_index in reversed(range(layer_count)):
            attn_saved, mlp_input, rows_in = stored[batch_index][layer_index]
            grad_stream, gain_mlp, grad_pair = mlp_backward(
                grad_stream, mlp_input, gains[layer_index, 1], ffn_weight[layer_index], rows_in
            )
            grad_stream, gain_attn, grad_wqkv, grad_wout = attention_backward(
                grad_stream,
                gains[layer_index, 0],
                w_qkv[layer_index],
                w_out[layer_index],
                omega[layer_index],
                attn_saved,
            )
            acc_gain = acc_gain.at[layer_index, 0].add(gain_attn).at[layer_index, 1].add(gain_mlp)
            acc_qkv = acc_qkv.at[layer_index].add(grad_wqkv)
            acc_out = acc_out.at[layer_index].add(grad_wout)
            acc_ffn = acc_ffn.at[layer_index].add(grad_pair)
        grads_in.append(grad_stream)
    grad_ffn = lax.psum_scatter(
        acc_ffn.astype(jnp.bfloat16), "dp", scatter_dimension=2, tiled=True
    ).astype(jnp.float32)
    sum_gain, sum_qkv, sum_out = lax.psum((acc_gain, acc_qkv, acc_out), ("dp", "seq"))
    return (jnp.stack(outputs), jnp.stack(grads_in), sum_gain, sum_qkv, sum_out, grad_ffn)


def solution(mesh):
    in_specs = (
        P("dp", "seq", None),
        P(),
        P(),
        P(),
        P(None, None, ("dp", "seq"), None),
        P(),
        P("dp", "seq", None),
    )
    out_specs = (
        P("dp", "seq", None),
        P("dp", "seq", None),
        P(),
        P(),
        P(),
        P(None, None, ("dp", "seq"), None),
    )
    return jax.shard_map(
        on_device, mesh=mesh, in_specs=in_specs, out_specs=out_specs, check_vma=False
    )
```

profile of v0, /device:TPU:0, one launch (start us, length us, event | category | flops | bytes accessed | tf_op | source)
XLA Modules:
  0.0 905.2 jit_solution(15864796164400052898)
XLA Ops:
  40.9 3.8 convert_reduce_fusion
  58.7 6.2 all-gather.4
  64.9 5.7 all-gather.1
  70.6 5.4 all-gather.6
  76.0 4.0 multiply_convert_fusion.14
  92.2 8.6 multiply_reduce_fusion.2
  100.7 5.4 fusion.128
  117.4 4.5 divide_convert_fusion.5
  134.2 5.0 all-gather.38.cloned.1.call-done
  139.2 58.2 %all-gather.32.cloned.1.call-done = bf16[2048,512]{0,1:T(8,128)(2,1)} async-done(((bf16[512,512]{0,1:T(8,128)(2,1)}), bf16[2048,512]{0,1:T(8,128)(2,1)}) %all-gather.32.cloned.1.call-update) | async-done | bytes 2097168 | tf_op jit(solution)/shard_map/all_gather | solution.py:256
  197.4 13.4 %multiply_convert_fusion.15 = (bf16[2048,512]{1,0:T(8,128)(2,1)}, f32[2048,512]{1,0:T(8,128)}, f32[2048,512]{1,0:T(8,128)}) fusion(bf16[2048,512]{0,1:T(8,128)(2,1)} %all-gather.32.cloned.1.call-done, bf16[1,2,512,512]{3,2,1,0:T(8,128)(2,1)} %all-gather.38.cloned.1.call-done), kind=kOutput, calls=%fused_computation.85 | convolution fusion | flops 1141899264 | bytes 13107200 | tf_op jit(solution)/shard_map/dot_general | solution.py:83
  210.8 10.6 %all-gather.48.cloned.1.call-done = bf16[1,2048,512]{1,2,0:T(8,128)(2,1)} async-done(((bf16[1,512,512]{1,2,0:T(8,128)(2,1)}), bf16[1,2048,512]{1,2,0:T(8,128)(2,1)}) %all-gather.48.cloned.1.call-update) | async-done | bytes 2097168 | tf_op jit(solution)/shard_map/all_gather | solution.py:269
  221.4 6.9 add_convert_fusion.1
  233.3 12.3 %all-gather.30.cloned.1.call-done = bf16[2048,512]{0,1:T(8,128)(2,1)} async-done(((bf16[512,512]{0,1:T(8,128)(2,1)}), bf16[2048,512]{0,1:T(8,128)(2,1)}) %all-gather.30.cloned.1.call-update) | async-done | bytes 2097168 | tf_op jit(solution)/shard_map/all_gather | solution.py:256
  245.6 13.5 %multiply_convert_fusion.18 = (bf16[2048,512]{1,0:T(8,128)(2,1)}, f32[2048,512]{1,0:T(8,128)}, f32[2048,512]{1,0:T(8,128)}) fusion(bf16[2048,512]{0,1:T(8,128)(2,1)} %all-gather.30.cloned.1.call-done, bf16[1,2,512,512]{3,2,1,0:T(8,128)(2,1)} %all-gather.38.cloned.1.call-done), kind=kOutput, calls=%fused_computation.101 | convolution fusion | flops 1141899264 | bytes 13107200 | tf_op jit(solution)/shard_map/dot_general | solution.py:83
  259.1 10.7 %all-gather.44.cloned.1.call-done = bf16[1,2048,512]{1,2,0:T(8,128)(2,1)} async-done(((bf16[1,512,512]{1,2,0:T(8,128)(2,1)}), bf16[1,2048,512]{1,2,0:T(8,128)(2,1)}) %all-gather.44.cloned.1.call-update) | async-done | bytes 2097168 | tf_op jit(solution)/shard_map/all_gather | solution.py:269
  269.8 6.9 add_convert_fusion.2
  281.9 4.5 convolution_convert_fusion.4
  286.4 4.4 convolution_convert_fusion.5
  291.4 4.5 fusion.132
  299.9 17.0 %reduce-scatter.16.cloned.1.call-done = f32[512,512]{0,1:T(8,128)} async-done(((f32[2048,512]{0,1:T(8,128)}), f32[512,512]{0,1:T(8,128)}) %reduce-scatter.16.cloned.1.call-update) | async-done | bytes 1048592 | tf_op jit(solution)/shard_map/reduce_scatter | solution.py:278
  316.9 47.1 %reduce-scatter.14.cloned.1.call-done = f32[512,512]{0,1:T(8,128)} async-done(((f32[2048,512]{0,1:T(8,128)}), f32[512,512]{0,1:T(8,128)}) %reduce-scatter.14.cloned.1.call-update) | async-done | bytes 1048592 | tf_op jit(solution)/shard_map/reduce_scatter | solution.py:278
  367.3 30.6 %reduce-scatter.10.cloned.1.call-done = bf16[512,512]{0,1:T(8,128)(2,1)} async-done(((bf16[2048,512]{0,1:T(8,128)(2,1)}), bf16[512,512]{0,1:T(8,128)(2,1)}) %reduce-scatter.10.cloned.1.call-update) | async-done | bytes 524304 | tf_op jit(solution)/shard_map/reduce_scatter | solution.py:260
  397.9 34.0 %reduce-scatter.8.cloned.1.call-done = bf16[512,512]{0,1:T(8,128)(2,1)} async-done(((bf16[2048,512]{0,1:T(8,128)(2,1)}), bf16[512,512]{0,1:T(8,128)(2,1)}) %reduce-scatter.8.cloned.1.call-update) | async-done | bytes 524304 | tf_op jit(solution)/shard_map/reduce_scatter | solution.py:260
  431.9 5.4 fusion.271
  440.2 4.8 fusion.81
  470.8 5.2 fusion.304
  479.4 9.1 %fusion.296 = (f32[512,8]{0,1:T(8,128)S(1)}, f32[512,8,256]{0,2,1:T(8,128)}) fusion(f32[512,8]{0,1:T(8,128)S(1)} %copy-done.138, f32[8,512,256]{1,2,0:T(8,128)} %get-tuple-element.1121, bf16[512,8,256]{0,2,1:T(8,128)(2,1)} %copy-done.22, bf16[8,512,512]{1,2,0:T(8,128)(2,1)} %multiply_convert_fusion.1, f32[8,256]{1,0:T(8,128)S(1)} %get-tuple-element.756, ...), kind=kOutput, calls=%fused_computation.509 | convolution fusion | flops 1082126336 | bytes 18931712 | tf_op jit(solution)/shard_map/hts,shf->thf/dot_general | solution.py:193
  488.5 13.5 %multiply_convert_fusion.12 = (bf16[2048,512]{1,0:T(8,128)(2,1)}, f32[2048,512]{1,0:T(8,128)}, f32[2048,512]{1,0:T(8,128)}) fusion(bf16[2048,512]{0,1:T(8,128)(2,1)} %all-gather.34.cloned.1.call-done, bf16[1,2,512,512]{3,2,1,0:T(8,128)(2,1)} %all-gather.38.cloned.1.call-done), kind=kOutput, calls=%fused_computation.69 | convolution fusion | flops 1141899264 | bytes 13107200 | tf_op jit(solution)/shard_map/dot_general | solution.py:83
  506.4 4.7 add_convert_fusion
  534.2 5.2 all-gather.9
  539.4 5.2 all-gather.12
  544.5 6.3 fusion.303
  554.2 6.0 fusion.127
  562.8 19.8 %while.108 = (s32[]{:T(128)}, f32[8,256,64]{2,1,0:T(8,128)}, f32[8,256]{1,0:T(8,128)S(1)}, s32[]{:T(128)}, bf16[4,8,256,64]{2,3,1,0:T(8,128)(2,1)}, /*index=5*/b...) while((s32[]{:T(128)}, f32[8,256,64]{2,1,0:T(8,128)}, ...), condition=%wide.region_39.40_spmd.clone, body=%wide.region_38.39_spmd.clone.sunk | while | flops 532488 | bytes 2379961 | solution.py:46
  582.6 4.3 fusion.118
  586.9 6.6 fusion.293
  593.5 20.3 %while.109 = (s32[]{:T(128)}, f32[8,256,64]{2,1,0:T(8,128)}, f32[8,256]{1,0:T(8,128)S(1)}, s32[]{:T(128)}, bf16[4,8,256,64]{2,3,1,0:T(8,128)(2,1)}, /*index=5*/b...) while((s32[]{:T(128)}, f32[8,256,64]{2,1,0:T(8,128)}, ...), condition=%wide.region_49.50_spmd.clone, body=%wide.region_48.49_spmd.clone.sunk | while | flops 532488 | bytes 2379961 | solution.py:46
  613.8 4.3 convolution_convert_fusion.3
  639.6 28.4 %reduce-scatter.12.cloned.1.call-done = bf16[512,512]{0,1:T(8,128)(2,1)} async-done(((bf16[2048,512]{0,1:T(8,128)(2,1)}), bf16[512,512]{0,1:T(8,128)(2,1)}) %reduce-scatter.12.cloned.1.call-update) | async-done | bytes 524304 | tf_op jit(solution)/shard_map/reduce_scatter | solution.py:260
  675.2 5.3 fusion.306
  685.7 6.1 fusion.292
  693.1 5.2 all-gather.15
  713.7 13.2 %while.110 = (s32[]{:T(128)}, f32[8,256,64]{2,1,0:T(8,128)}, f32[8,256]{1,0:T(8,128)S(1)}, s32[]{:T(128)}, bf16[4,8,256,64]{2,3,1,0:T(8,128)(2,1)}, /*index=5*/b...) while((s32[]{:T(128)}, f32[8,256,64]{2,1,0:T(8,128)}, ...), condition=%wide.region_59.60_spmd.clone, body=%wide.region_58.59_spmd.clone.sunk | while | flops 532488 | bytes 2379961 | solution.py:46
  730.5 5.4 fusion.291
  741.0 4.4 fusion.133
  765.9 39.8 %psum.21 = f32[1,2,512]{2,1,0:T(2,128)} all-reduce(f32[1,2,512]{2,1,0:T(2,128)S(1)} %scatter-add.35), channel_id=1, replica_groups=mesh['dp'=8,'seq'=4] {'dp','seq'}, use_global_device_ids=true, to_apply=%region_69.70 | all-reduce | flops 1024 | bytes 8192 | tf_op jit(solution)/shard_map/psum | solution.py:334
  805.7 87.4 %all-reduce.4.cloned.1.call-done = (f32[1,512,1536]{2,1,0:T(8,128)}, f32[1,512,512]{2,1,0:T(8,128)}) async-done(((f32[1,512,1536]{2,1,0:T(8,128)}, f32[1,512,512]{2,1,0:T(8,128)}), (f32[1,512,1536]{2,1,0:T(8,128)}, f32[1,512,512]{2,1,0:T(8,128)})) %all-reduce.4.cloned.1.call-update) | async-done | bytes 4194320 | tf_op jit(solution)/shard_map/psum | solution.py:334
  (647 shorter events, 302.6 us)
Async XLA Ops:
  7.2 98.9 %all-gather.40.cloned.1.call-start = ((), (), s32[]{:S(2)}) async-start(), calls=%async_computation.19 | async-start | bytes 2621440 | tf_op jit(solution)/shard_map/all_gather | solution.py:14
  8.0 27.7 %copy-start.127 = (f32[1,1,512]{2,1,0:T(1,128)}, f32[1,1,512]{2,1,0:T(1,128)S(1)}, u32[]{:S(2)}) copy-start(f32[1,1,512]{2,1,0:T(1,128)S(1)} %get-tuple-element.1103) | copy-start | bytes 6148
  14.5 75.1 %copy-start.56 = (bf16[512,512]{0,1:T(8,128)(2,1)}, bf16[512,512]{0,1:T(8,128)(2,1)S(1)}, u32[]{:S(2)}) copy-start(bf16[512,512]{0,1:T(8,128)(2,1)S(1)} %copy.214) | copy-start | bytes 1572868
  15.9 6.8 copy-start.76
  22.8 86.9 %all-gather.36.cloned.1.call-start = ((), (), s32[]{:S(2)}) async-start(), calls=%async_computation.17 | async-start | bytes 2621440 | tf_op jit(solution)/shard_map/all_gather | solution.py:14
  27.3 6.8 copy-start.78
  34.1 79.6 %all-gather.42.cloned.1.call-start = ((), (), s32[]{:S(2)}) async-start(), calls=%async_computation.20 | async-start | bytes 2621440 | tf_op jit(solution)/shard_map/all_gather | solution.py:14
  40.7 6.9 copy-start.53
  47.7 91.5 %all-gather.38.cloned.1.call-start = ((), (), s32[]{:S(2)}) async-start(), calls=%async_computation.18 | async-start | bytes 1179648 | tf_op jit(solution)/shard_map/all_gather | solution.py:250
  48.3 149.1 %all-gather.32.cloned.1.call-start = ((), (), s32[]{:S(2)}) async-start(), calls=%async_computation.9 | async-start | bytes 2621440 | tf_op jit(solution)/shard_map/all_gather | solution.py:256
  52.0 28.0 %copy-start.133 = (f32[512,8]{0,1:T(8,128)}, f32[512,8]{0,1:T(8,128)S(1)}, u32[]{:S(2)}) copy-start(f32[512,8]{0,1:T(8,128)S(1)} %broadcast_multiply_fusion.1) | copy-start | bytes 49156
  55.2 30.6 %copy-start.139 = (f32[512,8]{0,1:T(8,128)}, f32[512,8]{0,1:T(8,128)S(1)}, u32[]{:S(2)}) copy-start(f32[512,8]{0,1:T(8,128)S(1)} %broadcast_multiply_fusion.5) | copy-start | bytes 49156
  57.3 22.7 %copy-start.20 = (bf16[512,8,256]{0,2,1:T(8,128)(2,1)S(1)}, bf16[512,8,256]{0,2,1:T(8,128)(2,1)}, u32[]{:S(2)}) copy-start(bf16[512,8,256]{0,2,1:T(8,128)(2,1)} %copy-done.19) | copy-start | bytes 6291460
  58.7 22.6 %copy-start.137 = (f32[512,8]{0,1:T(8,128)}, f32[512,8]{0,1:T(8,128)S(1)}, u32[]{:S(2)}) copy-start(f32[512,8]{0,1:T(8,128)S(1)} %broadcast_multiply_fusion.3) | copy-start | bytes 49156
  81.3 10.5 %copy-start.1 = (f32[8,512,512]{1,2,0:T(8,128)}, f32[8,512,512]{1,2,0:T(8,128)S(1)}, u32[]{:S(2)}) copy-start(f32[8,512,512]{1,2,0:T(8,128)S(1)} %fusion.300) | copy-start | bytes 25165828
  92.2 8.6 copy-start.60
  114.7 7.7 copy-start.122
  114.7 7.2 copy-start.50
  114.7 7.2 copy-start.92
  127.6 93.9 %all-gather.48.cloned.1.call-start = ((), (), s32[]{:S(2)}) async-start(), calls=%async_computation.23 | async-start | bytes 2621440 | tf_op jit(solution)/shard_map/all_gather | solution.py:269
  132.2 113.5 %all-gather.30.cloned.1.call-start = ((), (), s32[]{:S(2)}) async-start(), calls=%async_computation.7 | async-start | bytes 2621440 | tf_op jit(solution)/shard_map/all_gather | solution.py:256
  132.9 136.9 %all-gather.44.cloned.1.call-start = ((), (), s32[]{:S(2)}) async-start(), calls=%async_computation.21 | async-start | bytes 2621440 | tf_op jit(solution)/shard_map/all_gather | solution.py:269
  134.0 182.9 %reduce-scatter.16.cloned.1.call-start = ((), (), s32[]{:S(2)}) async-start(), calls=%async_computation.14 | async-start | bytes 5242880 | tf_op jit(solution)/shard_map/reduce_scatter | solution.py:278
  221.4 8.3 copy-start.101
  233.0 130.9 %reduce-scatter.14.cloned.1.call-start = ((), (), s32[]{:S(2)}) async-start(), calls=%async_computation.13 | async-start | bytes 5242880 | tf_op jit(solution)/shard_map/reduce_scatter | solution.py:278
  269.8 8.3 copy-start.102
  281.9 116.1 %reduce-scatter.10.cloned.1.call-start = ((), (), s32[]{:S(2)}) async-start(), calls=%async_computation.10 | async-start | bytes 2621440 | tf_op jit(solution)/shard_map/reduce_scatter | solution.py:260
  286.4 145.6 %reduce-scatter.8.cloned.1.call-start = ((), (), s32[]{:S(2)}) async-start(), calls=%async_computation.8 | async-start | bytes 2621440 | tf_op jit(solution)/shard_map/reduce_scatter | solution.py:260
  290.9 197.7 %all-gather.34.cloned.1.call-start = ((), (), s32[]{:S(2)}) async-start(), calls=%async_computation.11 | async-start | bytes 2621440 | tf_op jit(solution)/shard_map/all_gather | solution.py:256
  437.4 64.6 %all-gather.52.cloned.1.call-start = ((), (), s32[]{:S(2)}) async-start(), calls=%async_computation.25 | async-start | bytes 2621440 | tf_op jit(solution)/shard_map/all_gather | solution.py:269
  439.5 123.3 %all-gather.46.cloned.1.call-start = ((), (), s32[]{:S(2)}) async-start(), calls=%async_computation.22 | async-start | bytes 1310720 | tf_op jit(solution)/shard_map/all_gather | solution.py:28
  452.2 12.6 %copy-start.151 = (f32[512]{0:T(512)}, f32[512]{0:T(512)S(1)}, u32[]{:S(2)}) copy-start(f32[512]{0:T(512)S(1)} %negate_multiply_fusion.12) | copy-start | bytes 6148
  452.9 10.1 %copy-start.79 = (bf16[512,8,64]{0,2,1:T(8,128)(2,1)}, bf16[512,8,64]{0,2,1:T(8,128)(2,1)S(1)}, u32[]{:S(2)}) copy-start(bf16[512,8,64]{0,2,1:T(8,128)(2,1)S(1)} %get-tuple-element.1088) | copy-start | bytes 1572868
  464.5 129.0 %all-gather.50.cloned.1.call-start = ((), (), s32[]{:S(2)}) async-start(), calls=%async_computation.24 | async-start | bytes 1310720 | tf_op jit(solution)/shard_map/all_gather | solution.py:28
  469.3 6.7 copy-start.57
  479.3 156.7 %reduce-scatter.20.cloned.1.call-start = ((), (), s32[]{:S(2)}) async-start(), calls=%async_computation.16 | async-start | bytes 1179648 | tf_op jit(solution)/shard_map/reduce_scatter | solution.py:331
  516.2 8.5 copy-start.33
  516.2 8.5 copy-start.71
  516.2 121.4 %reduce-scatter.18.cloned.1.call-start = ((), (), s32[]{:S(2)}) async-start(), calls=%async_computation.15 | async-start | bytes 5242880 | tf_op jit(solution)/shard_map/reduce_scatter | solution.py:278
  516.7 8.0 copy-start.47
  530.7 137.2 %reduce-scatter.12.cloned.1.call-start = ((), (), s32[]{:S(2)}) async-start(), calls=%async_computation.12 | async-start | bytes 2621440 | tf_op jit(solution)/shard_map/reduce_scatter | solution.py:260
  550.8 9.4 %slice-start.2 = ((s8[8388608]{0:T(1024)(128)(4,1)}), s8[4194304]{0:T(1024)(128)(4,1)S(1)}, s32[]{:S(2)}) async-start(s8[8388608]{0:T(1024)(128)(4,1)} %bitcast.675), calls=%async_computation.30 | async-start | bytes 8388608
  618.1 95.6 %all-gather.54.cloned.1.call-start = ((), (), s32[]{:S(2)}) async-start(), calls=%async_computation.26 | async-start | bytes 1310720 | tf_op jit(solution)/shard_map/all_gather | solution.py:28
  637.7 34.4 %copy-start.161 = (f32[512,8]{0,1:T(8,128)S(1)}, f32[512,8]{0,1:T(8,128)}, u32[]{:S(2)}) copy-start(f32[512,8]{0,1:T(8,128)} %get-tuple-element.1053) | copy-start | bytes 49156
  682.3 210.8 %all-reduce.4.cloned.1.call-start = ((), (), s32[]{:S(2)}) async-start(), calls=%async_computation.27 | async-start | bytes 8388608 | tf_op jit(solution)/shard_map/psum | solution.py:334
  700.9 6.9 copy-start.7
  700.9 6.9 copy-start.31
  704.1 7.0 slice-start
  (150 other events, 484.0 us)
Sparse Core Ops, SparseCore 0:
  22.9 25.2 all-gather.39
  49.8 22.9 all-gather.35
  74.3 22.5 all-gather.41
  99.0 40.1 all-gather.37
  140.7 56.7 all-gather.31
  198.8 22.5 all-gather.47
  223.0 22.5 all-gather.29
  247.2 22.5 all-gather.43
  272.3 44.4 reduce-scatter.15
  319.4 44.4 reduce-scatter.13
  366.5 31.4 reduce-scatter.9
  400.5 31.4 reduce-scatter.7
  437.5 22.5 all-gather.33
  461.5 22.5 all-gather.51
  486.2 16.7 all-gather.45
  504.4 16.7 all-gather.49
  524.4 63.4 reduce-scatter.19
  590.5 43.4 reduce-scatter.17
  636.5 31.4 reduce-scatter.11
  682.4 16.8 all-gather.53
  750.9 142.1 all-reduce.3
where the time goes:
time: 917 us; the launch traced here: 905 us
  waiting for transfers between devices  343 us (37%)
  matrix products  304 us (33%)
  local copies, waits for them, and re-layouts  97.9 us (11%)
  blocking collectives  72.6 us (8%)
  other arithmetic  67.4 us (7%)
  between operations  16.8 us (2%)
    reduce_scatter x3, waiting for transfers between devices, mlp_forward(): lax.psum_scatter(partial_value.astype(jnp.bfloat16), 'seq', scatter_dimen...  93 us
    psum x1, waiting for transfers between devices, on_device(): lax.psum((acc_gain, acc_qkv, acc_out), ('dp', 'seq'))  87.4 us
    all_gather x3, waiting for transfers between devices, mlp_forward(): rows_in = lax.all_gather(hidden_low, 'seq', axis=0, tiled=True)  70.5 us
    dot_general x12, matrix products, contract_cols(): lax.dot_general(left, right, (((1,), (1,)), ((), ())), preferred_element_...  70.4 us
    reduce_scatter x3, waiting for transfers between devices, mlp_backward(): lax.psum_scatter(partial_value, 'seq', scatter_dimension=0, tiled=True)  64 us
    unnamed x364, local copies, waits for them, and re-layouts  41.3 us
    psum x1, blocking collectives, on_device(): lax.psum((acc_gain, acc_qkv, acc_out), ('dp', 'seq'))  39.8 us
    dot_general x12, matrix products, contract_rows(): lax.dot_general(left, right, (((0,), (0,)), ((), ())), preferred_element_...  30.9 us
  transfers between devices with their start and end apart: 21, of which 11 were waited for; matrix products, arithmetic and copies ran while one was open for 41% of the time, Pallas kernels for 0%

commit v1 on v0

v1 whole, which is shorter than its diff:
```python
import functools
import math

import jax
import jax.numpy as jnp
from jax import lax
from jax.experimental import pallas as pl
from jax.experimental.pallas import tpu as pltpu
from jax.sharding import PartitionSpec as P

epsilon = 1e-05
bf16 = jnp.bfloat16
f32 = jnp.float32
AXES = ("dp", "seq")
MIB = 2**20
A_ROWS = 48


def nn(a, b):
    return lax.dot_general(a, b, (((1,), (0,)), ((), ())), preferred_element_type=f32)


def nt(a, b):
    return lax.dot_general(a, b, (((1,), (1,)), ((), ())), preferred_element_type=f32)


def tn(a, b):
    return lax.dot_general(a, b, (((0,), (0,)), ((), ())), preferred_element_type=f32)


def lanes_of(shape):
    return lax.broadcasted_iota(jnp.int32, shape, len(shape) - 1)


def params(mib=56):
    return pltpu.CompilerParams(vmem_limit_bytes=mib * MIB)


def cost(flops, nbytes, trans=0):
    return pl.CostEstimate(flops=int(flops), bytes_accessed=int(nbytes), transcendentals=int(trans))


def const_block(shape):
    return pl.BlockSpec(shape, lambda *_: (0,) * len(shape))


def stacked_call(kernel, grid, in_specs, out_specs, out_shapes, stacked, before, args, scratch, estimate):
    n_in = len(args)
    aliases = {}
    extra = []
    if before is not None:
        for at, (flag, buffer) in enumerate(zip(stacked, before)):
            if flag:
                aliases[n_in + len(extra)] = at
                extra.append(buffer)
    n_extra = len(extra)

    def body(*refs):
        kernel(*refs[:n_in], *refs[n_in + n_extra :])

    return pl.pallas_call(
        body,
        grid=grid,
        in_specs=list(in_specs) + [pl.BlockSpec(memory_space=pl.ANY)] * n_extra,
        out_specs=out_specs,
        out_shape=out_shapes,
        scratch_shapes=scratch,
        input_output_aliases=aliases,
        compiler_params=params(),
        cost_estimate=estimate,
    )(*args, *extra)


def normed(values):
    center = values - jnp.mean(values, axis=-1, keepdims=True)
    spread = jnp.mean(center * center, axis=-1, keepdims=True)
    scale = lax.rsqrt(spread + epsilon)
    return center * scale, scale


def norm_back(grad, xhat, scale, gain):
    gy = grad * gain
    return scale * (
        gy - jnp.mean(gy, axis=-1, keepdims=True) - xhat * jnp.mean(gy * xhat, axis=-1, keepdims=True)
    )


def causal_tile(rows):
    return lax.broadcasted_iota(jnp.int32, (rows, rows), 0) >= lax.broadcasted_iota(
        jnp.int32, (rows, rows), 1
    )


def feature_weights(omega):
    heads, feats, hd = omega.shape
    pairs = omega.reshape(heads // 2, 2, feats, hd)
    ones = jnp.full((heads // 2, feats, hd), -1.0, omega.dtype)
    zeros = jnp.zeros_like(ones)
    even = jnp.concatenate([pairs[:, 0], ones, ones, zeros], axis=-1)
    odd = jnp.concatenate([ones, pairs[:, 1], zeros, ones], axis=-1)
    return jnp.stack([even, odd], axis=1).reshape(heads, feats, 4 * hd)


def features_kernel(hd, x_ref, gains_ref, w_ref, wf_ref, qkv_ref, phiq_ref, phik_ref, h1_ref, state_ref, qkv_scr):
    pair = pl.program_id(0)
    width = 2 * hd
    model = x_ref.shape[-1]
    s = hd ** (-0.25)
    feats = wf_ref.shape[1]

    @pl.when(pair == 0)
    def _():
        xhat, _ = normed(x_ref[0].astype(f32))
        hidden = (xhat * gains_ref[0:1, :]).astype(bf16)
        h1_ref[0] = hidden
        for part in range(3):
            cols = slice(part * model, (part + 1) * model)
            made = nn(hidden, w_ref[:, cols]).astype(bf16)
            qkv_ref[0, :, cols] = made
            qkv_scr[part] = made

    column = pl.ds(pl.multiple_of(pair * width, width), width)
    rows = x_ref.shape[1]
    low = lanes_of((rows, width)) < hd

    def phi_pair(part, out_ref):
        points = qkv_scr[part, :, column].astype(f32)
        energy = points * points * (0.5 * s)
        high = energy.astype(bf16).astype(f32)
        rest = (energy - high).astype(bf16)
        turned = pltpu.roll(high, hd, 1)
        made = []
        for odd in range(2):
            first = jnp.where(low, turned, points) if odd else jnp.where(low, points, turned)
            left = jnp.concatenate([first.astype(bf16), rest], axis=1)
            proj = nt(left, wf_ref[odd])
            phi = jnp.exp2(proj * (s * math.log2(math.e)) - 0.5 * math.log2(feats))
            phi_low = phi.astype(bf16)
            out_ref[0, :, odd * feats : (odd + 1) * feats] = phi_low
            made.append(phi_low)
        return made

    phi_pair(0, phiq_ref)
    even_k, odd_k = phi_pair(1, phik_ref)
    values = qkv_scr[2, :, column]
    state_ref[0, 0:hd, :] = tn(values, even_k)[0:hd].astype(bf16)
    state_ref[0, hd:width, :] = tn(values, odd_k)[hd:width].astype(bf16)
    sums = jnp.concatenate(
        [
            jnp.sum(even_k.astype(f32), axis=0, keepdims=True),
            jnp.sum(odd_k.astype(f32), axis=0, keepdims=True),
            jnp.zeros((14, feats), f32),
        ],
        axis=0,
    )
    state_ref[0, width : width + 16, :] = sums.astype(bf16)


def features_call(index, inputs, gains, w_qkv, wf, before, hd):
    batch, rows, model = inputs.shape
    heads, feats, _ = wf.shape
    pairs = heads // 2
    width = 2 * hd
    n_rows = width + 16
    return stacked_call(
        functools.partial(features_kernel, hd),
        (pairs,),
        [
            pl.BlockSpec((1, rows, model), lambda p: (index, 0, 0)),
            const_block(gains.shape),
            const_block(w_qkv.shape),
            pl.BlockSpec((2, feats, 4 * hd), lambda p: (p, 0, 0)),
        ],
        [
            pl.BlockSpec((1, rows, 3 * model), lambda p: (index, 0, 0)),
            pl.BlockSpec((1, rows, 2 * feats), lambda p: (index, 0, p)),
            pl.BlockSpec((1, rows, 2 * feats), lambda p: (index, 0, p)),
            pl.BlockSpec((1, rows, model), lambda p: (index, 0, 0)),
            pl.BlockSpec((1, n_rows, feats), lambda p: (p, 0, 0)),
        ],
        [
            jax.ShapeDtypeStruct((batch, rows, 3 * model), bf16),
            jax.ShapeDtypeStruct((batch, rows, heads * feats), bf16),
            jax.ShapeDtypeStruct((batch, rows, heads * feats), bf16),
            jax.ShapeDtypeStruct((batch, rows, model), bf16),
            jax.ShapeDtypeStruct((pairs, n_rows, feats), bf16),
        ],
        (True, True, True, True, False),
        before,
        (inputs, gains, w_qkv, wf),
        [pltpu.VMEM((3, rows, model), bf16)],
        cost(2 * rows * model * 3 * model + 4 * heads * rows * 256 * feats, 8 * MIB, 2 * rows * heads * feats),
    )


def state_block(state_refs, place, pair, hd):
    if len(state_refs) == 1:
        total = state_refs[0][0].astype(f32)
    else:
        near, got, other = state_refs
        mine = jnp.where(pair // got.half == place["core"], 1.0, 0.0)
        total = (
            got.ref[0].astype(f32) * mine
            + other.ref[0].astype(f32) * (1.0 - mine)
            + near[0].astype(f32) * place["near"]
        )
    feats = total.shape[-1]
    width = 2 * hd
    zeros = jnp.zeros((hd, feats), bf16)
    low = total.astype(bf16)
    even_norm = jnp.broadcast_to(total[width : width + 1], (hd, feats)).astype(bf16)
    odd_norm = jnp.broadcast_to(total[width + 1 : width + 2], (hd, feats)).astype(bf16)
    even = jnp.concatenate([low[0:hd], zeros, even_norm, zeros], axis=0)
    odd = jnp.concatenate([zeros, low[hd:width], zeros, odd_norm], axis=0)
    return even, odd


class Half:
    def __init__(self, ref, half):
        self.ref = ref
        self.half = half


def state_refs_of(refs, pairs):
    if len(refs) == 1:
        return refs
    return refs[0], Half(refs[1], pairs // 2), Half(refs[2], pairs // 2)


def place_of(backward):
    seq = lax.axis_index("seq")
    core = lax.rem(seq, 2)
    near = jnp.where(core == (0 if backward else 1), 1.0, 0.0)
    return {"core": core, "near": near}


def state_specs(states, pairs):
    shape = (1,) + states[0].shape[1:]
    specs = [pl.BlockSpec(shape, lambda p: (p, 0, 0))]
    if len(states) > 1:
        specs += [pl.BlockSpec(shape, lambda p: (lax.rem(p, pairs // 2), 0, 0))] * 2
    return specs


def mix_kernel(hd, n_states, tile, *refs):
    x_ref, gains_ref, wout_ref, phiq_ref, phik_ref, v_ref = refs[:6]
    state_refs = refs[6 : 6 + n_states]
    scores_ref, mixed_ref, rden_ref, x1_ref, h2_ref, mixed_scr = refs[6 + n_states :]
    pair = pl.program_id(0)
    pairs = pl.num_programs(0)
    width = 2 * hd
    rows = x_ref.shape[1]
    feats = phiq_ref.shape[-1] // 2
    tiles = rows // tile
    column = pl.ds(pl.multiple_of(pair * width, width), width)
    even_state, odd_state = state_block(
        state_refs_of(state_refs, wout_ref.shape[0] // width), place_of(False), pair, hd
    )
    both_state = jnp.concatenate([even_state, odd_state], axis=1)
    low = lanes_of((rows, width)) < hd
    values = v_ref[0].astype(f32)
    ones = jnp.where(low, 1.0, 0.0)
    sides = [
        jnp.concatenate([jnp.where(low, values, 0.0), ones], axis=1).astype(bf16),
        jnp.concatenate([jnp.where(low, 0.0, values), 1.0 - ones], axis=1).astype(bf16),
    ]
    causal = causal_tile(tile)
    for at in range(tiles):
        here = slice(at * tile, (at + 1) * tile)
        end = (at + 1) * tile
        total = nt(phiq_ref[0, here, :], both_state)
        for odd in range(2):
            cols = slice(odd * feats, (odd + 1) * feats)
            made = nt(phiq_ref[0, here, cols], phik_ref[0, 0:end, cols])
            last = jnp.where(causal, made[:, at * tile : end], 0.0)
            made = last if at == 0 else jnp.concatenate([made[:, : at * tile], last], axis=1)
            made = made.astype(bf16)
            scores_ref[0, odd, here, 0:end] = made
            total = total + nn(made, sides[odd][0:end])
        rden = 1.0 / total[:, width:]
        mixed = (total[:, :width] * rden).astype(bf16)
        rden_ref[0, here, :] = rden
        mixed_ref[0, here, :] = mixed
        mixed_scr[here, column] = mixed

    @pl.when(pair == pairs - 1)
    def _():
        x1 = x_ref[0].astype(f32) + nn(mixed_scr[...], wout_ref[...])
        x1_ref[0] = x1
        xhat, _ = normed(x1)
        h2_ref[0] = (xhat * gains_ref[1:2, :]).astype(bf16)


def mix_call(index, inputs, gains, w_out, phi_q, phi_k, qkv, states, before, hd):
    batch, rows, model = inputs.shape
    width = 2 * hd
    pairs = model // width
    heads = 2 * pairs
    feats = phi_q.shape[-1] // heads
    tile = min(256, rows)
    return stacked_call(
        functools.partial(mix_kernel, hd, len(states), tile),
        (pairs,),
        [
            pl.BlockSpec((1, rows, model), lambda p: (index, 0, 0)),
            const_block(gains.shape),
            const_block(w_out.shape),
            pl.BlockSpec((1, rows, 2 * feats), lambda p: (index, 0, p)),
            pl.BlockSpec((1, rows, 2 * feats), lambda p: (index, 0, p)),
            pl.BlockSpec((1, rows, width), lambda p: (index, 0, 2 * pairs + p)),
        ]
        + state_specs(states, pairs),
        [
            pl.BlockSpec((1, 2, rows, rows), lambda p: (index, p, 0, 0)),
            pl.BlockSpec((1, rows, width), lambda p: (index, 0, p)),
            pl.BlockSpec((1, rows, width), lambda p: (index, 0, p)),
            pl.BlockSpec((1, rows, model), lambda p: (index, 0, 0)),
            pl.BlockSpec((1, rows, model), lambda p: (index, 0, 0)),
        ],
        [
            jax.ShapeDtypeStruct((batch, heads, rows, rows), bf16),
            jax.ShapeDtypeStruct((batch, rows, model), bf16),
            jax.ShapeDtypeStruct((batch, rows, model), f32),
            jax.ShapeDtypeStruct((batch, rows, model), f32),
            jax.ShapeDtypeStruct((batch, rows, model), bf16),
        ],
        (True,) * 5,
        before,
        (inputs, gains, w_out, phi_q, phi_k, qkv) + tuple(states),
        [pltpu.VMEM((rows, model), bf16)],
        cost(heads * 2 * rows * rows * 512 + 2 * rows * model * model, 12 * MIB),
    )


def ffn_kernel(n_weights, copies, groups, batch, split_out, *refs):
    h2_ref, gf_ref, x1_ref = refs[:3]
    weights = refs[3 : 3 + n_weights]
    n_out = 6 if split_out else 4
    outs = refs[3 + n_weights : 3 + n_weights + n_out]
    out_ref, gh2_ref = outs[:2]
    up_scr, down_scr, act_scr, pre_scr, sems = refs[3 + n_weights + n_out :]
    step = pl.program_id(0)
    n_blocks = pl.num_programs(0) - batch
    block = act_scr.shape[-1] // n_blocks
    rows = h2_ref.shape[1]
    model = h2_ref.shape[2]
    started = [
        pltpu.make_async_copy(src(weights), dst(up_scr, down_scr), sems.at[at])
        for at, (src, dst, _) in enumerate(copies)
    ]

    @pl.when(step == 0)
    def _():
        for copy in started:
            copy.start()

    for group in range(groups):

        @pl.when(step == group * (n_blocks // groups))
        def _():
            for copy, (_, _, own) in zip(started, copies):
                if own == group:
                    copy.wait()

    @pl.when(step < n_blocks)
    def _():
        if split_out:
            up = up_scr[step // 4, lax.rem(step, 4)].reshape(block, model)
            down = down_scr[step // 4, lax.rem(step, 4)].reshape(block, model)
        else:
            up = up_scr[step]
            down = down_scr[step]
        cols = pl.ds(pl.multiple_of(step * block, block), block)
        grad_up = jnp.zeros((block, model), f32)
        grad_down = jnp.zeros((block, model), f32)
        for b in range(batch):
            pre = nt(h2_ref[b], up)
            part = 0.5 * lax.erf(pre * math.sqrt(0.5)) + 0.5
            act = (pre * part).astype(bf16)
            act_scr[b, :, cols] = act
            slope = part + pre * (
                jnp.exp2(pre * pre * (-0.5 * math.log2(math.e))) * (1.0 / math.sqrt(2.0 * math.pi))
            )
            grad_pre = (nt(gf_ref[b], down) * slope).astype(bf16)
            pre_scr[b, :, cols] = grad_pre
            grad_down = grad_down + tn(act, gf_ref[b])
            grad_up = grad_up + tn(grad_pre, h2_ref[b])
        if split_out:
            up_low = grad_up.astype(bf16).reshape(4, block // 4, model)
            down_low = grad_down.astype(bf16).reshape(4, block // 4, model)
            for half in range(2):

                @pl.when(step // 4 == half)
                def _():
                    a_ref, b_ref = outs[2 + 2 * half : 4 + 2 * half]
                    a_ref[0] = up_low[:, :A_ROWS]
                    b_ref[:, 0, 0 : block // 4 - A_ROWS] = up_low[:, A_ROWS:]
                    b_ref[:, 0, block // 4 - A_ROWS :] = down_low
        else:
            outs[2][0] = grad_up.astype(bf16)
            outs[3][0] = grad_down.astype(bf16)

    @pl.when(step >= n_blocks)
    def _():
        b = step - n_blocks
        hidden = n_blocks * block
        down = down_scr[...].reshape(hidden, model)
        out_ref[0] = (x1_ref[0] + nn(act_scr[b], down)).astype(bf16)
        up = up_scr[...].reshape(hidden, model)
        gh2_ref[0] = nn(pre_scr[b], up)


def ffn_call(h2, gf, x1, weights, copies, groups, scratch_dims, split_out):
    batch, rows, model = h2.shape
    hidden = math.prod(scratch_dims)
    block = min(256, hidden)
    n_blocks = hidden // block
    late = lambda j: (jnp.clip(j - n_blocks, 0, batch - 1), 0, 0)
    out_specs = [pl.BlockSpec((1, rows, model), late), pl.BlockSpec((1, rows, model), late)]
    out_shapes = [
        jax.ShapeDtypeStruct((batch, rows, model), bf16),
        jax.ShapeDtypeStruct((batch, rows, model), f32),
    ]
    if split_out:
        unit = scratch_dims[-1]
        b_rows = 2 * unit - A_ROWS
        for half in range(2):
            out_specs.append(
                pl.BlockSpec((1, 4, A_ROWS, model), lambda j, h=half: (jnp.clip(j - 4 * h, 0, 3), 0, 0, 0))
            )
            out_shapes.append(jax.ShapeDtypeStruct((4, 4, A_ROWS, model), bf16))
            out_specs.append(
                pl.BlockSpec((4, 1, b_rows, model), lambda j, h=half: (0, jnp.clip(j - 4 * h, 0, 3), 0, 0))
            )
            out_shapes.append(jax.ShapeDtypeStruct((4, 4, b_rows, model), bf16))
    else:
        for _ in range(2):
            out_specs.append(pl.BlockSpec((1, block, model), lambda j: (jnp.minimum(j, n_blocks - 1), 0, 0)))
            out_shapes.append(jax.ShapeDtypeStruct((n_blocks, block, model), bf16))
    return pl.pallas_call(
        functools.partial(ffn_kernel, len(weights), copies, groups, batch, split_out),
        grid=(n_blocks + batch,),
        in_specs=[
            const_block(h2.shape),
            const_block(gf.shape),
            pl.BlockSpec((1, rows, model), late),
        ]
        + [pl.BlockSpec(memory_space=pl.ANY)] * len(weights),
        out_specs=out_specs,
        out_shape=out_shapes,
        scratch_shapes=[
            pltpu.VMEM(scratch_dims + (model,), bf16),
            pltpu.VMEM(scratch_dims + (model,), bf16),
            pltpu.VMEM((batch, rows, hidden), bf16),
            pltpu.VMEM((batch, rows, hidden), bf16),
            pltpu.SemaphoreType.DMA((len(copies),)),
        ],
        compiler_params=params(),
        cost_estimate=cost(12 * batch * rows * hidden * model, 18 * MIB, 2 * batch * rows * hidden),
    )(h2, gf, x1, *weights)


def query_back_kernel(hd, n_states, tile, *refs):
    (
        gh2_ref,
        x1_ref,
        cot_ref,
        mixed_ref,
        rden_ref,
        wout_ref,
        gains_ref,
        phiq_ref,
        phik_ref,
        q_ref,
        v_ref,
        wf_ref,
    ) = refs[:12]
    state_refs = refs[12 : 12 + n_states]
    g1_ref, ga_ref, gcol_ref, gn_ref, gs_ref, gq_ref, gstate_ref, side_scr = refs[12 + n_states :]
    pair = pl.program_id(0)
    width = 2 * hd
    rows = x1_ref.shape[1]
    model = x1_ref.shape[2]
    pairs = model // width
    feats = phiq_ref.shape[-1] // 2
    s = hd ** (-0.25)
    low = lanes_of((rows, width)) < hd
    inner = lax.rem(lanes_of((rows, width)), hd)

    @pl.when(pair == 0)
    def _():
        xhat, scale = normed(x1_ref[0])
        grad = gh2_ref[0]
        g1 = cot_ref[0].astype(f32) + norm_back(grad, xhat, scale, gains_ref[1:2, :])
        g1_ref[0] = g1
        gcol_ref[0] = tn((grad * xhat).astype(bf16), jnp.ones((rows, 128), bf16))
        ga = g1.astype(bf16)
        ga_ref[0] = ga
        gn_full = nt(ga, wout_ref[...]) * rden_ref[0]
        gn_low = gn_full.astype(bf16)
        gn_ref[0] = gn_low
        product = gn_full * mixed_ref[0].astype(f32)
        high = product.astype(bf16)
        rest = (product - high.astype(f32)).astype(bf16)
        same = lax.div(lax.rem(lax.broadcasted_iota(jnp.int32, (2 * width, width), 0), width), hd) == lax.div(
            lax.broadcasted_iota(jnp.int32, (2 * width, width), 1), hd
        )
        minus = jnp.where(same, -1.0, 0.0).astype(bf16)
        for at in range(pairs):
            cols = slice(at * width, (at + 1) * width)
            gd = nn(jnp.concatenate([high[:, cols], rest[:, cols]], axis=1), minus)
            gd_high = gd.astype(bf16).astype(f32)
            gdx = jnp.where(inner == 0, gd_high, jnp.where(inner == 1, gd - gd_high, 0.0))
            side_scr[at] = jnp.concatenate([gn_low[:, cols], gdx.astype(bf16)], axis=1)

    side = side_scr[pair]
    even_state, odd_state = state_block(state_refs_of(state_refs, pairs), place_of(False), pair, hd)
    states = [even_state, odd_state]
    values = v_ref[0].astype(f32)
    ones = jnp.where(inner < 2, 1.0, 0.0)
    sides = [
        jnp.concatenate([jnp.where(low, values, 0.0), jnp.where(low, ones, 0.0)], axis=1).astype(bf16),
        jnp.concatenate([jnp.where(low, 0.0, values), jnp.where(low, 0.0, ones)], axis=1).astype(bf16),
    ]
    causal = causal_tile(tile)
    low_tile = low[0:tile]
    for at in range(rows // tile):
        here = slice(at * tile, (at + 1) * tile)
        end = (at + 1) * tile
        back = []
        for odd in range(2):
            cols = slice(odd * feats, (odd + 1) * feats)
            made = nt(side[here], sides[odd][0:end])
            last = jnp.where(causal, made[:, at * tile : end], 0.0)
            made = last if at == 0 else jnp.concatenate([made[:, : at * tile], last], axis=1)
            made = made.astype(bf16)
            gs_ref[0, odd, here, 0:end] = made
            grad_phi = nn(side[here], states[odd]) + nn(made, phik_ref[0, 0:end, cols])
            grad_proj = (grad_phi * phiq_ref[0, here, cols].astype(f32)).astype(bf16)
            back.append(nn(grad_proj, wf_ref[odd]))
        along = jnp.where(low_tile, back[0][:, :width], back[1][:, :width])
        total = jnp.where(low_tile, back[0][:, width:], back[1][:, width:])
        gq_ref[0, here, :] = (s * along + (s * s) * q_ref[0, here, :].astype(f32) * total).astype(bf16)
    even = tn(side, phiq_ref[0, :, :feats])
    odd = tn(side, phiq_ref[0, :, feats:])
    gstate_ref[0, 0:hd] = even[0:hd].astype(bf16)
    gstate_ref[0, hd:width] = odd[hd:width].astype(bf16)
    norms = jnp.concatenate(
        [
            even[width : width + 1] + even[width + 1 : width + 2],
            odd[width + hd : width + hd + 1] + odd[width + hd + 1 : width + hd + 2],
            jnp.zeros((14, feats), f32),
        ],
        axis=0,
    )
    gstate_ref[0, width : width + 16] = norms.astype(bf16)


def query_back_call(index, gh2, x1, cot, mixed, rden, w_out, gains, phi_q, phi_k, qkv, wf, states, before, hd):
    batch, rows, model = x1.shape
    width = 2 * hd
    pairs = model // width
    heads = 2 * pairs
    feats = phi_q.shape[-1] // heads
    tile = min(256, rows)
    whole = pl.BlockSpec((1, rows, model), lambda p: (index, 0, 0))
    phi_spec = pl.BlockSpec((1, rows, 2 * feats), lambda p: (index, 0, p))
    n_rows = width + 16
    return stacked_call(
        functools.partial(query_back_kernel, hd, len(states), tile),
        (pairs,),
        [
            whole,
            whole,
            whole,
            whole,
            whole,
            const_block(w_out.shape),
            const_block(gains.shape),
            phi_spec,
            phi_spec,
            pl.BlockSpec((1, rows, width), lambda p: (index, 0, p)),
            pl.BlockSpec((1, rows, width), lambda p: (index, 0, 2 * pairs + p)),
            pl.BlockSpec((2, feats, 4 * hd), lambda p: (p, 0, 0)),
        ]
        + state_specs(states, pairs),
        [
            whole,
            whole,
            pl.BlockSpec((1, model, 128), lambda p: (index, 0, 0)),
            whole,
            pl.BlockSpec((1, 2, rows, rows), lambda p: (index, p, 0, 0)),
            pl.BlockSpec((1, rows, width), lambda p: (index, 0, p)),
            pl.BlockSpec((1, n_rows, feats), lambda p: (p, 0, 0)),
        ],
        [
            jax.ShapeDtypeStruct((batch, rows, model), f32),
            jax.ShapeDtypeStruct((batch, rows, model), bf16),
            jax.ShapeDtypeStruct((batch, model, 128), f32),
            jax.ShapeDtypeStruct((batch, rows, model), bf16),
            jax.ShapeDtypeStruct((batch, heads, rows, rows), bf16),
            jax.ShapeDtypeStruct((batch, rows, model), bf16),
            jax.ShapeDtypeStruct((pairs, n_rows, feats), bf16),
        ],
        (True,) * 6 + (False,),
        before,
        (gh2, x1, cot, mixed, rden, w_out, gains, phi_q, phi_k, qkv, qkv, wf) + tuple(states),
        [pltpu.VMEM((pairs, rows, 2 * width), bf16)],
        cost(heads * 2 * rows * (rows * 512 + 4 * 65536), 18 * MIB),
    )


def key_back_kernel(hd, n_states, tile, *refs):
    gs_ref, scores_ref, phiq_ref, phik_ref, gn_ref, k_ref, v_ref, wf_ref = refs[:8]
    state_refs = refs[8 : 8 + n_states]
    gk_ref, gv_ref = refs[8 + n_states :]
    pair = pl.program_id(0)
    width = 2 * hd
    rows = k_ref.shape[1]
    feats = phiq_ref.shape[-1] // 2
    tiles = rows // tile
    s = hd ** (-0.25)
    states = state_block(state_refs_of(state_refs, pl.num_programs(0)), place_of(True), pair, hd)
    both = jnp.concatenate([states[0][0:width], states[1][0:width]], axis=1)
    low = lanes_of((tile, width)) < hd
    inner = lax.rem(lanes_of((tile, width)), hd)
    one = jnp.where(inner == 0, 1.0, 0.0).astype(bf16)
    gn_pair = gn_ref[0].astype(f32)
    low_all = lanes_of((rows, width)) < hd
    gn_sides = [
        jnp.where(low_all, gn_pair, 0.0).astype(bf16),
        jnp.where(low_all, 0.0, gn_pair).astype(bf16),
    ]
    for at in range(tiles):
        here = slice(at * tile, (at + 1) * tile)
        start = at * tile
        side = jnp.concatenate([v_ref[0, here, :], one], axis=1)
        grad_v = nt(phik_ref[0, here, :], both)
        back = []
        for odd in range(2):
            cols = slice(odd * feats, (odd + 1) * feats)
            grad_phi = nn(side, states[odd]) + tn(gs_ref[0, odd, start:, here], phiq_ref[0, start:, cols])
            grad_proj = (grad_phi * phik_ref[0, here, cols].astype(f32)).astype(bf16)
            back.append(nn(grad_proj, wf_ref[odd]))
            grad_v = grad_v + tn(scores_ref[0, odd, start:, here], gn_sides[odd][start:])
        along = jnp.where(low, back[0][:, :width], back[1][:, :width])
        total = jnp.where(low, back[0][:, width:], back[1][:, width:])
        gk_ref[0, here, :] = (s * along + (s * s) * k_ref[0, here, :].astype(f32) * total).astype(bf16)
        gv_ref[0, here, :] = grad_v.astype(bf16)


def key_back_call(index, gs, scores, phi_q, phi_k, gn, qkv, wf, states, before, hd):
    batch, rows, model = gn.shape
    width = 2 * hd
    pairs = model // width
    heads = 2 * pairs
    feats = phi_q.shape[-1] // heads
    tile = min(256, rows)
    square = pl.BlockSpec((1, 2, rows, rows), lambda p: (index, p, 0, 0))
    phi_spec = pl.BlockSpec((1, rows, 2 * feats), lambda p: (index, 0, p))
    narrow = pl.BlockSpec((1, rows, width), lambda p: (index, 0, p))
    return stacked_call(
        functools.partial(key_back_kernel, hd, len(states), tile),
        (pairs,),
        [
            square,
            square,
            phi_spec,
            phi_spec,
            narrow,
            pl.BlockSpec((1, rows, width), lambda p: (index, 0, pairs + p)),
            pl.BlockSpec((1, rows, width), lambda p: (index, 0, 2 * pairs + p)),
            pl.BlockSpec((2, feats, 4 * hd), lambda p: (p, 0, 0)),
        ]
        + state_specs(states, pairs),
        [narrow, narrow],
        [jax.ShapeDtypeStruct((batch, rows, model), bf16)] * 2,
        (True, True),
        before,
        (gs, scores, phi_q, phi_k, gn, qkv, qkv, wf) + tuple(states),
        [],
        cost(heads * 2 * rows * (rows * 512 + 4 * 65536), 14 * MIB),
    )


def inputs_back_kernel(gq_ref, gk_ref, gv_ref, w_ref, x_ref, g1_ref, gains_ref, out_ref):
    model = gq_ref.shape[2]
    grad = nt(gq_ref[0], w_ref[:, :model])
    grad = grad + nt(gk_ref[0], w_ref[:, model : 2 * model])
    grad = grad + nt(gv_ref[0], w_ref[:, 2 * model :])
    xhat, scale = normed(x_ref[0].astype(f32))
    out_ref[0] = g1_ref[0] + norm_back(grad, xhat, scale, gains_ref[0:1, :])


def inputs_back_call(gq, gk, gv, w_qkv, inputs, g1, gains):
    batch, rows, model = gq.shape
    whole = pl.BlockSpec((1, rows, model), lambda b: (b, 0, 0))
    return pl.pallas_call(
        inputs_back_kernel,
        grid=(batch,),
        in_specs=[whole, whole, whole, const_block(w_qkv.shape), whole, whole, const_block(gains.shape)],
        out_specs=whole,
        out_shape=jax.ShapeDtypeStruct((batch, rows, model), f32),
        compiler_params=params(),
        cost_estimate=cost(6 * batch * rows * model * model, 14 * MIB),
    )(gq, gk, gv, w_qkv, inputs, g1, gains)


def position():
    dp = lax.axis_index("dp")
    seq = lax.axis_index("seq")
    z, y = dp // 2, lax.rem(dp, 2)
    x, core = seq // 2, lax.rem(seq, 2)
    return core * 16 + z * 4 + y * 2 + x


def weight_kernel(n_products, has_column, pieces, *refs):
    n_in = 2 * n_products + has_column
    ins = refs[:n_in]
    outs = refs[n_in:-1]
    acc = refs[-1]
    step = pl.program_id(0)
    model = acc.shape[0]
    parts = [tn(ins[2 * at][0], ins[2 * at + 1][0]) for at in range(n_products)]
    if has_column:
        parts.append(ins[-1][0])

    @pl.when(step == 0)
    def _():
        for at, part in enumerate(parts):
            acc[:, at * model : at * model + part.shape[1]] = part

    @pl.when(step > 0)
    def _():
        for at, part in enumerate(parts):
            acc[:, at * model : at * model + part.shape[1]] += part

    @pl.when(step == pl.num_programs(0) - 1)
    def _():
        if not pieces:
            outs[0][...] = acc[...]
            return
        rows = model // 32
        cut = 3 * 128
        here = position()
        for half in range(2):
            a_ref, b_ref = outs[2 * half : 2 * half + 2]
            for z in range(4):
                for plane in range(4):
                    owner = here ^ (half * 16 + z * 4 + plane)
                    taken = acc[pl.ds(pl.multiple_of(owner * rows, rows), rows), :].astype(bf16)
                    a_ref[z, plane] = taken[:, :cut]
                    b_ref[plane, z] = taken[:, cut:]


def weight_call(products, column, pieces):
    batch, rows, model = products[0][0].shape
    whole = pl.BlockSpec((1, rows, model), lambda b: (b, 0, 0))
    args = [a for pair in products for a in pair]
    in_specs = [whole] * len(args)
    total = model * len(products)
    if column is not None:
        args.append(column)
        in_specs.append(pl.BlockSpec((1,) + column.shape[1:], lambda b: (b, 0, 0)))
        total += column.shape[2]
    if pieces:
        shapes = [(4, 4, model // 32, 384), (4, 4, model // 32, total - 384)] * 2
        kind = bf16
    else:
        shapes = [(model, total)]
        kind = f32
    return pl.pallas_call(
        functools.partial(weight_kernel, len(products), int(column is not None), pieces),
        grid=(batch,),
        in_specs=in_specs,
        out_specs=[const_block(shape) for shape in shapes],
        out_shape=[jax.ShapeDtypeStruct(shape, kind) for shape in shapes],
        scratch_shapes=[pltpu.VMEM((model, total), f32)],
        compiler_params=params(),
        cost_estimate=cost(2 * batch * rows * model * total, 10 * MIB),
    )(*args)


def swap(array, core=0, z=0, plane=0):
    mask = z * 8 + (plane // 2) * 4 + (plane % 2) * 2 + core
    return lax.ppermute(array, AXES, [(i, i ^ mask) for i in range(32)])


def gather_pieces(a_own, b_own):
    a_plane = jnp.stack([a_own] + [swap(a_own, plane=p) for p in (1, 2, 3)])
    b_line = jnp.stack([b_own] + [swap(b_own, z=z) for z in (1, 2, 3)])
    a_all = [a_plane] + [swap(a_plane, z=z) for z in (1, 2, 3)]
    b_all = [b_line] + [swap(b_line, plane=p) for p in (1, 2, 3)]
    return a_all, b_all


def summed(*arrays):
    return functools.reduce(lambda a, b: a + b, [a.astype(f32) for a in arrays])


def scatter_pieces(a_near, b_near, a_far, b_far):
    a_got, b_got = swap(a_far, core=1), swap(b_far, core=1)
    a_sum = [summed(a_near[z], a_got[z]).astype(bf16) for z in range(4)]
    b_sum = [summed(b_near[p], b_got[p]).astype(bf16) for p in range(4)]
    a_line = summed(a_sum[0], *[swap(a_sum[z], z=z) for z in (1, 2, 3)]).astype(bf16)
    b_plane = summed(b_sum[0], *[swap(b_sum[p], plane=p) for p in (1, 2, 3)]).astype(bf16)
    a_own = summed(a_line[0], *[swap(a_line[p], plane=p) for p in (1, 2, 3)])
    b_own = summed(b_plane[0], *[swap(b_plane[z], z=z) for z in (1, 2, 3)])
    return a_own, b_own


def share_pieces(a_own, b_own):
    a_all, b_all = gather_pieces(a_own, b_own)
    a_near = jnp.stack(a_all)
    b_near = jnp.stack(b_all, axis=1)
    near = jnp.concatenate([a_near, b_near], axis=-1)
    return jnp.stack([near, swap(near, core=1)])


def assemble_kernel(early_ref, late_ref, wqkv_ref, gains_ref, gw_ref, gwout_ref, ggain_ref, col_scr):
    rows = early_ref.shape[3]
    model = gwout_ref.shape[0]
    here = position()
    for core in range(2):
        for z in range(4):
            for plane in range(4):
                owner = here ^ (core * 16 + z * 4 + plane)
                at = pl.ds(pl.multiple_of(owner * rows, rows), rows)
                early = early_ref[core, z, plane].astype(f32)
                late = late_ref[core, z, plane].astype(f32)
                gwout_ref[at, :] = early[:, :model]
                gw_ref[at, 0:model] = early[:, model : 2 * model]
                col_scr[at, :] = early[:, 2 * model :]
                gw_ref[at, model:] = late
    gain_rows(gw_ref, col_scr, wqkv_ref, gains_ref, ggain_ref)


def gain_rows(gw_ref, col_ref, wqkv_ref, gains_ref, ggain_ref):
    along = jnp.sum(gw_ref[...] * wqkv_ref[...].astype(f32), axis=1, keepdims=True)
    wide = jnp.broadcast_to(along, col_ref.shape)
    ggain_ref[0:1, :] = wide.T[0:1, :] / gains_ref[0:1, :]
    ggain_ref[1:2, :] = col_ref[...].T[0:1, :]


def assemble_call(early, late, w_qkv, gains):
    model = w_qkv.shape[0]
    return pl.pallas_call(
        assemble_kernel,
        out_shape=[
            jax.ShapeDtypeStruct(w_qkv.shape, f32),
            jax.ShapeDtypeStruct((model, model), f32),
            jax.ShapeDtypeStruct(gains.shape, f32),
        ],
        scratch_shapes=[pltpu.VMEM((model, 128), f32)],
        compiler_params=params(),
    )(early, late, w_qkv, gains)


def gains_kernel(gw_ref, col_ref, wqkv_ref, gains_ref, ggain_ref):
    gain_rows(gw_ref, col_ref, wqkv_ref, gains_ref, ggain_ref)


def exchange_states(local, backward, fast):
    if not fast:
        everything = lax.all_gather(local, "seq").astype(f32)
        count, place = lax.axis_size("seq"), lax.axis_index("seq")
        at = jnp.arange(count)
        wanted = (at > place) if backward else (at < place)
        total = jnp.sum(jnp.where(wanted[:, None, None, None], everything, 0.0), axis=0)
        return (total.astype(bf16),)
    near = swap(local, core=1)
    half = local.shape[0] // 2
    core = lax.rem(lax.axis_index("seq"), 2)
    total = (local.astype(f32) + near.astype(f32)).astype(bf16)
    mine = jnp.where(core == 0, total[:half], total[half:])
    from_x = 1 if backward else 0
    pairs = [(i, i ^ 2) for i in range(32) if (i >> 1) & 1 == from_x]
    got = lax.ppermute(mine, AXES, pairs)
    other = swap(got, core=1)
    return near, got, other


def ffn_weights_fast(ffn_weight):
    shard = ffn_weight[0]
    unit = shard.shape[1]
    flat = shard.reshape(2 * unit, shard.shape[2])
    a_near, b_near = gather_pieces(flat[:A_ROWS], flat[A_ROWS:])
    a_far = [swap(a, core=1) for a in a_near]
    b_far = [swap(b, core=1) for b in b_near]
    weights = a_far + b_far + a_near + b_near
    copies = []
    tail = unit - A_ROWS
    for group in range(2):
        base = 8 * group
        for z in range(4):
            copies.append(
                (
                    lambda w, i=base + z: w[i],
                    lambda up, down, g=group, z=z: up.at[g, z, :, 0:A_ROWS],
                    group,
                )
            )
        for p in range(4):
            copies.append(
                (
                    lambda w, i=base + 4 + p: w[i].at[:, 0:tail],
                    lambda up, down, g=group, p=p: up.at[g, :, p, A_ROWS:unit],
                    group,
                )
            )
            copies.append(
                (
                    lambda w, i=base + 4 + p: w[i].at[:, tail:],
                    lambda up, down, g=group, p=p: down.at[g, :, p],
                    group,
                )
            )
    return weights, copies, 2, (2, 4, 4, unit)


def ffn_weights_plain(ffn_weight):
    pair = lax.all_gather(ffn_weight[0], AXES, axis=1, tiled=True)
    hidden, model = pair.shape[1:]
    block = min(256, hidden)
    blocks = pair.reshape(2, hidden // block, block, model)
    copies = [
        (lambda w: w[0].at[0], lambda up, down: up, 0),
        (lambda w: w[0].at[1], lambda up, down: down, 0),
    ]
    return [blocks], copies, 1, (hidden // block, block)


def on_device(inputs, gains, w_qkv, w_out, ffn_weight, omega, cotangent):
    batch, rows, model = inputs.shape
    hd = omega.shape[-1]
    fast = lax.axis_size("dp") == 8 and lax.axis_size("seq") == 4 and ffn_weight.shape[2] == 64
    gain_pair, wqkv, wout = gains[0], w_qkv[0], w_out[0]
    wf = feature_weights(omega[0])
    if fast:
        weights, copies, groups, dims = ffn_weights_fast(ffn_weight)
    else:
        weights, copies, groups, dims = ffn_weights_plain(ffn_weight)

    before = None
    carried = []
    for b in range(batch):
        before = features_call(b, inputs, gain_pair, wqkv, wf, before, hd)
        carried.append(exchange_states(before[4], False, fast))
    qkv, phi_q, phi_k, h1 = before[:4]
    before = None
    for b in range(batch):
        before = mix_call(b, inputs, gain_pair, wout, phi_q, phi_k, qkv, carried[b], before, hd)
    scores, mixed, rden, x1, h2 = before
    result = ffn_call(h2, cotangent, x1, weights, copies, groups, dims, fast)
    outputs, gh2 = result[:2]
    if fast:
        a_far, b_far, a_near, b_near = result[2:]
        a_own, b_own = scatter_pieces(a_near, b_near, a_far, b_far)
        unit = ffn_weight.shape[2]
        grad_ffn = jnp.concatenate([a_own, b_own], axis=0).reshape(1, 2, unit, model)
    else:
        both = jnp.stack([g.reshape(-1, model) for g in result[2:]])
        grad_ffn = lax.psum_scatter(both, AXES, scatter_dimension=1, tiled=True).astype(f32)[None]

    before = None
    later = []
    for b in range(batch):
        before = query_back_call(
            b, gh2, x1, cotangent, mixed, rden, wout, gain_pair, phi_q, phi_k, qkv, wf, carried[b], before, hd
        )
        later.append(exchange_states(before[6], True, fast))
    g1, ga, gcol, gn, gs, gq = before[:6]
    early = weight_call([(mixed, ga), (h1, gq)], gcol, fast)
    before = None
    for b in range(batch):
        before = key_back_call(b, gs, scores, phi_q, phi_k, gn, qkv, wf, later[b], before, hd)
    gk, gv = before
    late = weight_call([(h1, gk), (h1, gv)], None, fast)
    grad_inputs = inputs_back_call(gq, gk, gv, wqkv, inputs, g1, gain_pair)
    if fast:
        early_own = scatter_pieces(*early[:2], *early[2:])
        late_own = scatter_pieces(*late[:2], *late[2:])
        early_all = share_pieces(*[a.astype(bf16) for a in early_own])
        late_all = share_pieces(*[a.astype(bf16) for a in late_own])
        grad_wqkv, grad_wout, grad_gains = assemble_call(early_all, late_all, wqkv, gain_pair)
    else:
        early_sum, late_sum = lax.psum((early[0], late[0]), AXES)
        grad_wout = early_sum[:, :model]
        grad_wqkv = jnp.concatenate([early_sum[:, model : 2 * model], late_sum], axis=1)
        grad_gains = pl.pallas_call(
            gains_kernel,
            out_shape=jax.ShapeDtypeStruct(gain_pair.shape, f32),
            compiler_params=params(),
        )(grad_wqkv, early_sum[:, 2 * model :], wqkv, gain_pair)
    return (outputs, grad_inputs, grad_gains[None], grad_wqkv[None], grad_wout[None], grad_ffn)


def solution(mesh):
    in_specs = (
        P("dp", "seq", None),
        P(),
        P(),
        P(),
        P(None, None, ("dp", "seq"), None),
        P(),
        P("dp", "seq", None),
    )
    out_specs = (
        P("dp", "seq", None),
        P("dp", "seq", None),
        P(),
        P(),
        P(),
        P(None, None, ("dp", "seq"), None),
    )
    return jax.shard_map(
        on_device, mesh=mesh, in_specs=in_specs, out_specs=out_specs, check_vma=False
    )
```

time: 917 us -> 399 us (0.44)
  matrix products: 304 us -> 0 us
  waiting for transfers between devices: 343 us -> 73.7 us
  Pallas kernels: 0 us -> 180 us
  starting transfers between devices: 2.9 us -> 119 us
  local copies, waits for them, and re-layouts: 97.9 us -> 5.02 us
  blocking collectives: 72.6 us -> 0 us
  other arithmetic: 67.4 us -> 11.1 us
  between operations: 16.8 us -> 2.21 us
    dot_general x90 -> x0, matrix products: 304 us -> none  [the longest x12 70.4 us: contract_cols(): lax.dot_general(left, right, (((1,), (1,)), ((), ())), preferred_element_...]
    pallas_call x0 -> x17, Pallas kernels: none -> 180 us  [the longest x12 120 us: stacked_call(): pl.pallas_call(body, grid=grid, in_specs=list(in_specs) + [pl.BlockSpec(m...]
    reduce_scatter x7 -> x0, waiting for transfers between devices: 157 us -> none  [the longest x3 93 us: mlp_forward(): lax.psum_scatter(partial_value.astype(jnp.bfloat16), 'seq', scatter_dimen...]
    ppermute x0 -> x106, starting transfers between devices: none -> 119 us  [the longest x100 104 us: swap(): return lax.ppermute(array, AXES, [(i, i ^ mask) for i in range(32)])]
    all_gather x13 -> x0, waiting for transfers between devices: 96.9 us -> none  [the longest x3 70.5 us: mlp_forward(): rows_in = lax.all_gather(hidden_low, 'seq', axis=0, tiled=True)]
    psum x1 -> x0, waiting for transfers between devices: 87.4 us -> none  [on_device(): lax.psum((acc_gain, acc_qkv, acc_out), ('dp', 'seq'))]
    ppermute x0 -> x106, waiting for transfers between devices: none -> 73.7 us  [the longest x100 66.3 us: swap(): return lax.ppermute(array, AXES, [(i, i ^ mask) for i in range(32)])]
    psum x1 -> x0, blocking collectives: 39.8 us -> none  [on_device(): lax.psum((acc_gain, acc_qkv, acc_out), ('dp', 'seq'))]
  transfers between devices with their start and end apart: 21 -> 106, of which waited for: 11 -> 38; matrix products, arithmetic and copies ran while one was open for 41% -> 3% of each run, Pallas kernels for 0% -> 25%
where the time goes in v1:
time: 399 us; the launch traced here: 391 us
  Pallas kernels  180 us (45%)
  starting transfers between devices  119 us (30%)
  waiting for transfers between devices  73.7 us (18%)
  other arithmetic  11.1 us (3%)
  local copies, waits for them, and re-layouts  5.02 us (1%)
    pallas_call x12, Pallas kernels, stacked_call(): pl.pallas_call(body, grid=grid, in_specs=list(in_specs) + [pl.BlockSpec(m...  120 us
    ppermute x100, starting transfers between devices, swap(): return lax.ppermute(array, AXES, [(i, i ^ mask) for i in range(32)])  104 us
    ppermute x100, waiting for transfers between devices, swap(): return lax.ppermute(array, AXES, [(i, i ^ mask) for i in range(32)])  66.3 us
    pallas_call x1, Pallas kernels, ffn_call(): pl.pallas_call(functools.partial(ffn_kernel, len(weights), copies, groups...  33.7 us
    ppermute x6, starting transfers between devices, exchange_states(): got = lax.ppermute(mine, AXES, pairs)  14.4 us
    pallas_call x2, Pallas kernels, weight_call(): pl.pallas_call(functools.partial(weight_kernel, len(products), int(column...  12.8 us
    pallas_call x1, Pallas kernels, inputs_back_call(): pl.pallas_call(inputs_back_kernel, grid=(batch,), in_specs=[whole, whole,...  8.5 us
  transfers between devices with their start and end apart: 106, of which 38 were waited for; matrix products, arithmetic and copies ran while one was open for 3% of the time, Pallas kernels for 25%

profile of v1, /device:TPU:0, one launch (start us, length us, event | category | flops | bytes accessed | tf_op | source)
XLA Modules:
  0.0 391.1 jit_solution(4196354611017545165)
XLA Ops:
  1.4 3.0 collective-permute-start.10
  9.0 7.6 %shard_map.118 = (bf16[3,512,1536]{2,1,0:T(8,128)(2,1)}, bf16[3,512,2048]{2,1,0:T(8,128)(2,1)}, bf16[3,512,2048]{2,1,0:T(8,128)(2,1)}, bf16[3,512,512]{2,1,0:T(8,128)(2,1)}, bf16[4,144,256]{2,1,0:T(8,128)(2,1)}) custom-call(bf16[3,512,512]{2,1,0:T(8,128)(2,1)} %x_ref.1, f32[2,512]{1,0:T(2,128)} %bitcast.236, bf16[512,1536]{1,0:T(8,128)(2,1)} %bitcast.221, ...), custom_call_target="tpu_custom_call" | custom-call | flops 1879048192 | bytes 8388608 | tf_op jit(solution)/shard_map/pallas_call | solution.py:61
  16.7 8.2 %shard_map.119 = (bf16[3,512,1536]{2,1,0:T(8,128)(2,1)}, bf16[3,512,2048]{2,1,0:T(8,128)(2,1)}, bf16[3,512,2048]{2,1,0:T(8,128)(2,1)}, bf16[3,512,512]{2,1,0:T(8,128)(2,1)}, bf16[4,144,256]{2,1,0:T(8,128)(2,1)}) custom-call(bf16[3,512,512]{2,1,0:T(8,128)(2,1)} %x_ref.1, ...), custom_call_target="tpu_custom_call", output_to_operand_aliasing={{0}: (4, {}), {1}: (5, {}), {2}: (6, {}), {3}: (7, {})} | custom-call | flops 1879048192 | bytes 8388608 | tf_op jit(solution)/shard_map/pallas_call | solution.py:61
  24.9 8.2 %shard_map.120 = (bf16[3,512,1536]{2,1,0:T(8,128)(2,1)}, bf16[3,512,2048]{2,1,0:T(8,128)(2,1)}, bf16[3,512,2048]{2,1,0:T(8,128)(2,1)}, bf16[3,512,512]{2,1,0:T(8,128)(2,1)}, bf16[4,144,256]{2,1,0:T(8,128)(2,1)}) custom-call(bf16[3,512,512]{2,1,0:T(8,128)(2,1)} %x_ref.1, ...), custom_call_target="tpu_custom_call", output_to_operand_aliasing={{0}: (4, {}), {1}: (5, {}), {2}: (6, {}), {3}: (7, {})} | custom-call | flops 1879048192 | bytes 8388608 | tf_op jit(solution)/shard_map/pallas_call | solution.py:61
  33.2 3.1 collective-permute-start.20
  38.0 3.3 collective-permute-done.20
  41.4 3.8 collective-permute-start.17
  48.8 2.5 collective-permute-start.27
  51.5 3.2 collective-permute-start.7
  54.7 6.8 %collective-permute-done.15.refs_13_ = bf16[4,48,512]{2,1,0:T(8,128)(2,1)S(1)} collective-permute-done((bf16[4,48,512]{2,1,0:T(8,128)(2,1)S(1)}, bf16[4,48,512]{2,1,0:T(8,128)(2,1)S(1)}, u32[]{:S(2)}, u32[]{:S(2)}) %collective-permute-start.15) | collective-permute-done | bytes 196640 | tf_op jit(solution)/shard_map/ppermute | solution.py:786
  64.6 2.4 collective-permute-start.4
  67.4 5.6 %collective-permute-done.4.refs_7_.refs_13_ = bf16[2,144,256]{2,1,0:T(8,128)(2,1)S(1)} collective-permute-done((bf16[2,144,256]{2,1,0:T(8,128)(2,1)S(1)}, bf16[2,144,256]{2,1,0:T(8,128)(2,1)S(1)}, u32[]{:S(2)}, u32[]{:S(2)}) %collective-permute-start.4) | collective-permute-done | bytes 147488 | tf_op jit(solution)/shard_map/ppermute | solution.py:878
  73.0 4.9 %collective-permute-start.1 = (bf16[2,144,256]{2,1,0:T(8,128)(2,1)S(1)}, bf16[2,144,256]{2,1,0:T(8,128)(2,1)S(1)}, u32[]{:S(2)}, u32[]{:S(2)}) collective-permute-start(bf16[2,144,256]{2,1,0:T(8,128)(2,1)S(1)} %slice_select_fusion.5), channel_id=1, source_target_pairs={{0,2},{1,3},{4,6},{5,7},{8,10},{9,11},{12,14},{13,15},{16,18},{17,... | collective-permute-start | bytes 442376 | tf_op jit(solution)/shard_map/ppermute | solution.py:878
  78.6 8.8 %shard_map.121 = (bf16[3,8,512,512]{3,2,1,0:T(8,128)(2,1)}, bf16[3,512,512]{2,1,0:T(8,128)(2,1)}, f32[3,512,512]{2,1,0:T(8,128)}, f32[3,512,512]{2,1,0:T(8,128)}, bf16[3,512,512]{2,1,0:T(8,128)(2,1)}) custom-call(bf16[3,512,512]{2,1,0:T(8,128)(2,1)} %x_ref.1, f32[2,512]{1,0:T(2,128)} %bitcast.239, bf16[512,512]{1,0:T(8,128)(2,1)} %bitcast.226, ...), custom_call_target="tpu_custom_call" | custom-call | flops 2415919104 | bytes 12582912 | tf_op jit(solution)/shard_map/pallas_call | solution.py:61
  89.3 8.8 %shard_map.122 = (bf16[3,8,512,512]{3,2,1,0:T(8,128)(2,1)}, bf16[3,512,512]{2,1,0:T(8,128)(2,1)}, f32[3,512,512]{2,1,0:T(8,128)}, f32[3,512,512]{2,1,0:T(8,128)}, bf16[3,512,512]{2,1,0:T(8,128)(2,1)}) custom-call(bf16[3,512,512]{2,1,0:T(8,128)(2,1)} %x_ref.1, ...), custom_call_target="tpu_custom_call", output_to_operand_aliasing={{0}: (9, {}), {1}: (10, {}), {2}: (11, {}), {3}: (12, {}), ... | custom-call | flops 2415919104 | bytes 12582912 | tf_op jit(solution)/shard_map/pallas_call | solution.py:61
  99.1 8.8 %shard_map.123 = (bf16[3,8,512,512]{3,2,1,0:T(8,128)(2,1)}, bf16[3,512,512]{2,1,0:T(8,128)(2,1)}, f32[3,512,512]{2,1,0:T(8,128)}, f32[3,512,512]{2,1,0:T(8,128)}, bf16[3,512,512]{2,1,0:T(8,128)(2,1)}) custom-call(bf16[3,512,512]{2,1,0:T(8,128)(2,1)} %x_ref.1, ...), custom_call_target="tpu_custom_call", output_to_operand_aliasing={{0}: (9, {}), {1}: (10, {}), {2}: (11, {}), {3}: (12, {}), ... | custom-call | flops 2415919104 | bytes 12582912 | tf_op jit(solution)/shard_map/pallas_call | solution.py:61
  109.1 33.7 %shard_map.124 = (bf16[3,512,512]{2,1,0:T(8,128)(2,1)}, f32[3,512,512]{2,1,0:T(8,128)}, bf16[4,4,48,512]{3,2,1,0:T(8,128)(2,1)}, bf16[4,4,80,512]{3,2,1,0:T(8,12...) custom-call(bf16[3,512,512]{2,1,0:T(8,128)(2,1)} %get-tuple-element.104.refs_0_, ...), custom_call_target="tpu_custom_call" | custom-call | flops 19327352832 | bytes 18874368 | tf_op jit(solution)/shard_map/pallas_call | solution.py:440
  142.7 14.2 %shard_map.125 = (f32[3,512,512]{2,1,0:T(8,128)}, bf16[3,512,512]{2,1,0:T(8,128)(2,1)}, f32[3,512,128]{2,1,0:T(8,128)}, bf16[3,512,512]{2,1,0:T(8,128)(2,1)}, bf...) custom-call(f32[3,512,512]{2,1,0:T(8,128)} %get-tuple-element.107.refs_0_, ...), custom_call_target="tpu_custom_call" | custom-call | flops 4294967296 | bytes 18874368 | tf_op jit(solution)/shard_map/pallas_call | solution.py:61
  156.9 14.4 %shard_map.126 = (f32[3,512,512]{2,1,0:T(8,128)}, bf16[3,512,512]{2,1,0:T(8,128)(2,1)}, f32[3,512,128]{2,1,0:T(8,128)}, bf16[3,512,512]{2,1,0:T(8,128)(2,1)}, bf...) custom-call(f32[3,512,512]{2,1,0:T(8,128)} %get-tuple-element.107.re, ...), custom_call_target="tpu_custom_call", output_to_operand_aliasing={{0}: (15, {}), {1}: (16, {}), {2}: (17, {}), {3}: (18, {}),... | custom-call | flops 4294967296 | bytes 18874368 | tf_op jit(solution)/shard_map/pallas_call | solution.py:61
  171.3 14.3 %shard_map.127 = (f32[3,512,512]{2,1,0:T(8,128)}, bf16[3,512,512]{2,1,0:T(8,128)(2,1)}, f32[3,512,128]{2,1,0:T(8,128)}, bf16[3,512,512]{2,1,0:T(8,128)(2,1)}, bf...) custom-call(f32[3,512,512]{2,1,0:T(8,128)} %get-tuple-element.107.re, ...), custom_call_target="tpu_custom_call", output_to_operand_aliasing={{0}: (15, {}), {1}: (16, {}), {2}: (17, {}), {3}: (18, {}),... | custom-call | flops 4294967296 | bytes 18874368 | tf_op jit(solution)/shard_map/pallas_call | solution.py:61
  185.7 6.3 %shard_map.132 = (bf16[4,4,16,384]{3,2,1,0:T(8,128)(2,1)}, bf16[4,4,16,768]{3,2,1,0:T(8,128)(2,1)}, bf16[4,4,16,384]{3,2,1,0:T(8,128)(2,1)}, bf16[4,4,16,768]{3,2,1,0:T(8,128)(2,1)}) custom-call(bf16[3,512,512]{2,1,0:T(8,128)(2,1)} %get-tuple-element.108.refs_3_.refs_0_, bf16[3,512,512]{2,1,0:T(8,128)(2,1)} %get-tuple-element.136.refs_1_, ...), custom_call_target="tpu_custom_call" | custom-call | flops 1811939328 | bytes 10485760 | tf_op jit(solution)/shard_map/pallas_call | solution.py:772
  194.6 2.8 collective-permute-start.39
  197.4 2.5 collective-permute-start.41
  200.4 3.0 collective-permute-done.41
  203.3 2.2 collective-permute-done.40
  206.5 2.7 collective-permute-start.44
  218.6 2.2 collective-permute-done.52
  224.0 2.3 collective-permute-start.57
  231.0 2.3 collective-permute-start.60
  247.7 9.2 %shard_map.128 = (bf16[3,512,512]{2,1,0:T(8,128)(2,1)}, bf16[3,512,512]{2,1,0:T(8,128)(2,1)}) custom-call(bf16[3,8,512,512]{3,2,1,0:T(8,128)(2,1)} %get-tuple-element.123.refs_0_, bf16[3,8,512,512]{3,2,1,0:T(8,128)(2,1)} %get-tuple-element.124.refs_1_, bf16[3,512,2048]{2,1,0:T(8,128)(2,1)} %get-tuple-element.88.refs_3_.refs_7_.refs_2_, ...), custom_call_target="tpu_custom_call" | custom-call | flops 4294967296 | bytes 14680064 | tf_op jit(solution)/shard_map/pallas_call | solution.py:61
  258.3 8.9 %shard_map.129 = (bf16[3,512,512]{2,1,0:T(8,128)(2,1)}, bf16[3,512,512]{2,1,0:T(8,128)(2,1)}) custom-call(bf16[3,8,512,512]{3,2,1,0:T(8,128)(2,1)} %get-tuple-element.123.refs_0_, bf16[3,8,512,512]{3,2,1,0:T(8,128)(2,1)} %get-tuple-element.124.refs_1_, ...), custom_call_target="tpu_custom_call", output_to_operand_aliasing={{0}: (11, {}), {1}: (12, {})} | custom-call | flops 4294967296 | bytes 14680064 | tf_op jit(solution)/shard_map/pallas_call | solution.py:61
  268.2 8.9 %shard_map.130 = (bf16[3,512,512]{2,1,0:T(8,128)(2,1)}, bf16[3,512,512]{2,1,0:T(8,128)(2,1)}) custom-call(bf16[3,8,512,512]{3,2,1,0:T(8,128)(2,1)} %get-tuple-element.123.refs_0_, bf16[3,8,512,512]{3,2,1,0:T(8,128)(2,1)} %get-tuple-element.124.refs_1_, ...), custom_call_target="tpu_custom_call", output_to_operand_aliasing={{0}: (11, {}), {1}: (12, {})} | custom-call | flops 4294967296 | bytes 14680064 | tf_op jit(solution)/shard_map/pallas_call | solution.py:61
  277.1 8.5 %shard_map.131 = f32[3,512,512]{2,1,0:T(8,128)} custom-call(bf16[3,512,512]{2,1,0:T(8,128)(2,1)} %get-tuple-element.122.gq_ref.refs_3_, bf16[3,512,512]{2,1,0:T(8,128)(2,1)} %get-tuple-element.133.gk_ref.refs_1_, bf16[3,512,512]{2,1,0:T(8,128)(2,1)} %get-tuple-element.134.gv_ref.refs_3_, bf16[512,1536]{1,0:T(8,128)(2,1)} %bitcast.224, ...), custom_call_target="tpu_custom_call" | custom-call | flops 2415919104 | bytes 14680064 | tf_op jit(solution)/shard_map/pallas_call | solution.py:698
  287.0 6.5 %shard_map.133 = (bf16[4,4,16,384]{3,2,1,0:T(8,128)(2,1)}, bf16[4,4,16,640]{3,2,1,0:T(8,128)(2,1)}, bf16[4,4,16,384]{3,2,1,0:T(8,128)(2,1)}, bf16[4,4,16,640]{3,2,1,0:T(8,128)(2,1)}) custom-call(bf16[3,512,512]{2,1,0:T(8,128)(2,1)} %get-tuple-element.137.refs_2_.refs_0_, bf16[3,512,512]{2,1,0:T(8,128)(2,1)} %get-tuple-element.133.gk_ref.refs_1_, ...), custom_call_target="tpu_custom_call" | custom-call | flops 1610612736 | bytes 10485760 | tf_op jit(solution)/shard_map/pallas_call | solution.py:772
  294.3 2.4 collective-permute-done.65
  298.2 2.1 collective-permute-start.68
  301.7 2.6 collective-permute-done.68
  322.4 2.6 collective-permute-start.95
  325.1 2.8 collective-permute-start.76
  330.1 2.7 collective-permute-start.84
  332.8 7.0 %collective-permute-done.94 = bf16[4,48,512]{2,1,0:T(8,128)(2,1)S(1)} collective-permute-done((bf16[4,48,512]{2,1,0:T(8,128)(2,1)S(1)}, bf16[4,48,512]{2,1,0:T(8,128)(2,1)S(1)}, u32[]{:S(2)}, u32[]{:S(2)}) %collective-permute-start.94) | collective-permute-done | bytes 196640 | tf_op jit(solution)/shard_map/ppermute | solution.py:786
  339.9 3.1 collective-permute-start.75
  344.5 2.5 collective-permute-start.87
  348.9 2.5 collective-permute-start.77
  369.1 5.6 %collective-permute-done.100 = bf16[4,80,512]{2,1,0:T(8,128)(2,1)S(1)} collective-permute-done((bf16[4,80,512]{2,1,0:T(8,128)(2,1)S(1)}, bf16[4,80,512]{2,1,0:T(8,128)(2,1)S(1)}, u32[]{:S(2)}, u32[]{:S(2)}) %collective-permute-start.100) | collective-permute-done | bytes 327712 | tf_op jit(solution)/shard_map/ppermute | solution.py:786
  374.7 4.3 %collective-permute-done.102 = bf16[4,80,512]{2,1,0:T(8,128)(2,1)S(1)} collective-permute-done((bf16[4,80,512]{2,1,0:T(8,128)(2,1)S(1)}, bf16[4,80,512]{2,1,0:T(8,128)(2,1)S(1)}, u32[]{:S(2)}, u32[]{:S(2)}) %collective-permute-start.102) | collective-permute-done | bytes 327712 | tf_op jit(solution)/shard_map/ppermute | solution.py:786
  380.7 2.5 collective-permute-start.105
  385.3 4.8 %shard_map.134 = (f32[512,1536]{1,0:T(8,128)}, f32[512,512]{1,0:T(8,128)}, f32[2,512]{1,0:T(2,128)}) custom-call(bf16[2,4,4,16,1152]{4,3,2,1,0:T(8,128)(2,1)} %pad_maximum_fusion.early_ref, bf16[2,4,4,16,1024]{4,3,2,1,0:T(8,128)(2,1)} %pad_maximum_fusion.2.late_ref, bf16[512,1536]{1,0:T(8,128)(2,1)} %bitcast.225, f32[2,512]{1,0:T(2,128)} %bitcast.246), custom_call_target="tpu_custom_call" | custom-call | tf_op jit(solution)/shard_map/pallas_call | solution.py:847
  (335 shorter events, 107.6 us)
Async XLA Ops:
  1.4 34.8 %collective-permute-start.10 = (bf16[48,512]{1,0:T(8,128)(2,1)S(1)}, bf16[48,512]{1,0:T(8,128)(2,1)S(1)}, u32[]{:S(2)}, u32[]{:S(2)}) collective-permute-start(bf16[48,512]{1,0:T(8,128)(2,1)S(1)} %get-tuple-element.185), channel_id=1, source_target_pairs={{0,4},{1,5},{2,6},{3,7},{4,0},{5,1},{6,2},{7,3},{8,12},{9,13},{10,... | collective-permute-start | bytes 147464 | tf_op jit(solution)/shard_map/ppermute | solution.py:786
  4.4 33.4 %collective-permute-start.9 = (bf16[48,512]{1,0:T(8,128)(2,1)S(1)}, bf16[48,512]{1,0:T(8,128)(2,1)S(1)}, u32[]{:S(2)}, u32[]{:S(2)}) collective-permute-start(bf16[48,512]{1,0:T(8,128)(2,1)S(1)} %get-tuple-element.185), channel_id=1, source_target_pairs={{0,2},{1,3},{2,0},{3,1},{4,6},{5,7},{6,4},{7,5},{8,10},{9,11},{10,... | collective-permute-start | bytes 147464 | tf_op jit(solution)/shard_map/ppermute | solution.py:786
  5.9 31.9 %collective-permute-start.11 = (bf16[48,512]{1,0:T(8,128)(2,1)S(1)}, bf16[48,512]{1,0:T(8,128)(2,1)S(1)}, u32[]{:S(2)}, u32[]{:S(2)}) collective-permute-start(bf16[48,512]{1,0:T(8,128)(2,1)S(1)} %get-tuple-element.185), channel_id=1, source_target_pairs={{0,6},{1,7},{2,4},{3,5},{4,2},{5,3},{6,0},{7,1},{8,14},{9,15},{10,... | collective-permute-start | bytes 147464 | tf_op jit(solution)/shard_map/ppermute | solution.py:786
  33.1 14.3 %collective-permute-start = (bf16[4,144,256]{2,1,0:T(8,128)(2,1)}, bf16[4,144,256]{2,1,0:T(8,128)(2,1)S(1)}, u32[]{:S(2)}, u32[]{:S(2)}) collective-permute-start(bf16[4,144,256]{2,1,0:T(8,128)(2,1)} %get-tuple-element.91), channel_id=1, source_target_pairs={{0,1},{1,0},{2,3},{3,2},{4,5},{5,4},{6,7},{7,6},{8,9},{9,8},{10,11... | collective-permute-start | bytes 884744 | tf_op jit(solution)/shard_map/ppermute | solution.py:786
  37.9 10.8 %collective-permute-start.3 = (bf16[4,144,256]{2,1,0:T(8,128)(2,1)S(1)}, bf16[4,144,256]{2,1,0:T(8,128)(2,1)S(1)}, u32[]{:S(2)}, u32[]{:S(2)}) collective-permute-start(bf16[4,144,256]{2,1,0:T(8,128)(2,1)S(1)} %copy-done.21), channel_id=1, source_target_pairs={{0,1},{1,0},{2,3},{3,2},{4,5},{5,4},{6,7},{7,6},{8,9},{9,8},{10,11... | collective-permute-start | bytes 884744 | tf_op jit(solution)/shard_map/ppermute | solution.py:786
  41.4 10.0 %collective-permute-start.17 = (bf16[4,48,512]{2,1,0:T(8,128)(2,1)S(1)}, bf16[4,48,512]{2,1,0:T(8,128)(2,1)S(1)}, u32[]{:S(2)}, u32[]{:S(2)}) collective-permute-start(bf16[4,48,512]{2,1,0:T(8,128)(2,1)S(1)} %pad_maximum_fusion.5.refs_11_), channel_id=1, source_target_pairs={{0,24},{1,25},{2,26},{3,27},{4,28},{5,29},{6,30},{7,31},{8,16},{9,... | collective-permute-start | bytes 589832 | tf_op jit(solution)/shard_map/ppermute | solution.py:786
  45.2 16.3 %collective-permute-start.15 = (bf16[4,48,512]{2,1,0:T(8,128)(2,1)S(1)}, bf16[4,48,512]{2,1,0:T(8,128)(2,1)S(1)}, u32[]{:S(2)}, u32[]{:S(2)}) collective-permute-start(bf16[4,48,512]{2,1,0:T(8,128)(2,1)S(1)} %pad_maximum_fusion.5.refs_11_), channel_id=1, source_target_pairs={{0,16},{1,17},{2,18},{3,19},{4,20},{5,21},{6,22},{7,23},{8,24},{9,... | collective-permute-start | bytes 589832 | tf_op jit(solution)/shard_map/ppermute | solution.py:786
  47.4 15.7 %collective-permute-start.13 = (bf16[4,48,512]{2,1,0:T(8,128)(2,1)S(1)}, bf16[4,48,512]{2,1,0:T(8,128)(2,1)S(1)}, u32[]{:S(2)}, u32[]{:S(2)}) collective-permute-start(bf16[4,48,512]{2,1,0:T(8,128)(2,1)S(1)} %pad_maximum_fusion.5.refs_11_), channel_id=1, source_target_pairs={{0,8},{1,9},{2,10},{3,11},{4,12},{5,13},{6,14},{7,15},{8,0},{9,1},... | collective-permute-start | bytes 589832 | tf_op jit(solution)/shard_map/ppermute | solution.py:786
  48.6 15.9 %collective-permute-start.12 = (bf16[4,48,512]{2,1,0:T(8,128)(2,1)S(1)}, bf16[4,48,512]{2,1,0:T(8,128)(2,1)S(1)}, u32[]{:S(2)}, u32[]{:S(2)}) collective-permute-start(bf16[4,48,512]{2,1,0:T(8,128)(2,1)S(1)} %pad_maximum_fusion.5.refs_11_), channel_id=1, source_target_pairs={{0,1},{1,0},{2,3},{3,2},{4,5},{5,4},{6,7},{7,6},{8,9},{9,8},{10,11... | collective-permute-start | bytes 589832 | tf_op jit(solution)/shard_map/ppermute | solution.py:786
  48.8 15.8 %collective-permute-start.27 = (bf16[4,80,512]{2,1,0:T(8,128)(2,1)S(1)}, bf16[4,80,512]{2,1,0:T(8,128)(2,1)S(1)}, u32[]{:S(2)}, u32[]{:S(2)}) collective-permute-start(bf16[4,80,512]{2,1,0:T(8,128)(2,1)S(1)} %pad_maximum_fusion.3.refs_15_), channel_id=1, source_target_pairs={{0,6},{1,7},{2,4},{3,5},{4,2},{5,3},{6,0},{7,1},{8,14},{9,15},{10,... | collective-permute-start | bytes 983048 | tf_op jit(solution)/shard_map/ppermute | solution.py:786
  51.5 15.6 %collective-permute-start.7 = (bf16[2,144,256]{2,1,0:T(8,128)(2,1)S(1)}, bf16[2,144,256]{2,1,0:T(8,128)(2,1)S(1)}, u32[]{:S(2)}, u32[]{:S(2)}) collective-permute-start(bf16[2,144,256]{2,1,0:T(8,128)(2,1)S(1)} %slice_select_fusion.3), channel_id=1, source_target_pairs={{0,2},{1,3},{4,6},{5,7},{8,10},{9,11},{12,14},{13,15},{16,18},{17,... | collective-permute-start | bytes 442376 | tf_op jit(solution)/shard_map/ppermute | solution.py:878
  61.5 26.0 %collective-permute-start.25 = (bf16[4,80,512]{2,1,0:T(8,128)(2,1)S(1)}, bf16[4,80,512]{2,1,0:T(8,128)(2,1)S(1)}, u32[]{:S(2)}, u32[]{:S(2)}) collective-permute-start(bf16[4,80,512]{2,1,0:T(8,128)(2,1)S(1)} %pad_maximum_fusion.3.refs_15_), channel_id=1, source_target_pairs={{0,4},{1,5},{2,6},{3,7},{4,0},{5,1},{6,2},{7,3},{8,12},{9,13},{10,... | collective-permute-start | bytes 983048 | tf_op jit(solution)/shard_map/ppermute | solution.py:786
  63.0 24.6 %collective-permute-start.23 = (bf16[4,80,512]{2,1,0:T(8,128)(2,1)S(1)}, bf16[4,80,512]{2,1,0:T(8,128)(2,1)S(1)}, u32[]{:S(2)}, u32[]{:S(2)}) collective-permute-start(bf16[4,80,512]{2,1,0:T(8,128)(2,1)S(1)} %pad_maximum_fusion.3.refs_15_), channel_id=1, source_target_pairs={{0,2},{1,3},{2,0},{3,1},{4,6},{5,7},{6,4},{7,5},{8,10},{9,11},{10,... | collective-permute-start | bytes 983048 | tf_op jit(solution)/shard_map/ppermute | solution.py:786
  64.5 23.6 %collective-permute-start.22 = (bf16[4,80,512]{2,1,0:T(8,128)(2,1)S(1)}, bf16[4,80,512]{2,1,0:T(8,128)(2,1)S(1)}, u32[]{:S(2)}, u32[]{:S(2)}) collective-permute-start(bf16[4,80,512]{2,1,0:T(8,128)(2,1)S(1)} %pad_maximum_fusion.3.refs_15_), channel_id=1, source_target_pairs={{0,1},{1,0},{2,3},{3,2},{4,5},{5,4},{6,7},{7,6},{8,9},{9,8},{10,11... | collective-permute-start | bytes 983048 | tf_op jit(solution)/shard_map/ppermute | solution.py:786
  67.1 10.8 %collective-permute-start.8 = (bf16[2,144,256]{2,1,0:T(8,128)(2,1)S(1)}, bf16[2,144,256]{2,1,0:T(8,128)(2,1)S(1)}, u32[]{:S(2)}, u32[]{:S(2)}) collective-permute-start(bf16[2,144,256]{2,1,0:T(8,128)(2,1)S(1)} %collective-permute-done.7.refs_7_.refs_13_), channel_id=1, source_target_pairs={{0,1},{1,0},{2,3},{3,2},{4,5},{5,4},{6,7},{7,6},{8,9},{9,8},{10,11... | collective-permute-start | bytes 442376 | tf_op jit(solution)/shard_map/ppermute | solution.py:786
  73.0 15.3 %collective-permute-start.1 = (bf16[2,144,256]{2,1,0:T(8,128)(2,1)S(1)}, bf16[2,144,256]{2,1,0:T(8,128)(2,1)S(1)}, u32[]{:S(2)}, u32[]{:S(2)}) collective-permute-start(bf16[2,144,256]{2,1,0:T(8,128)(2,1)S(1)} %slice_select_fusion.5), channel_id=1, source_target_pairs={{0,2},{1,3},{4,6},{5,7},{8,10},{9,11},{12,14},{13,15},{16,18},{17,... | collective-permute-start | bytes 442376 | tf_op jit(solution)/shard_map/ppermute | solution.py:878
  77.9 10.7 %collective-permute-start.5 = (bf16[2,144,256]{2,1,0:T(8,128)(2,1)S(1)}, bf16[2,144,256]{2,1,0:T(8,128)(2,1)S(1)}, u32[]{:S(2)}, u32[]{:S(2)}) collective-permute-start(bf16[2,144,256]{2,1,0:T(8,128)(2,1)S(1)} %collective-permute-done.4.refs_7_.refs_13_), channel_id=1, source_target_pairs={{0,1},{1,0},{2,3},{3,2},{4,5},{5,4},{6,7},{7,6},{8,9},{9,8},{10,11... | collective-permute-start | bytes 442376 | tf_op jit(solution)/shard_map/ppermute | solution.py:786
  87.5 10.7 %collective-permute-start.18 = (bf16[4,48,512]{2,1,0:T(8,128)(2,1)S(1)}, bf16[4,48,512]{2,1,0:T(8,128)(2,1)S(1)}, u32[]{:S(2)}, u32[]{:S(2)}) collective-permute-start(bf16[4,48,512]{2,1,0:T(8,128)(2,1)S(1)} %collective-permute-done.17.refs_14_), channel_id=1, source_target_pairs={{0,1},{1,0},{2,3},{3,2},{4,5},{5,4},{6,7},{7,6},{8,9},{9,8},{10,11... | collective-permute-start | bytes 589832 | tf_op jit(solution)/shard_map/ppermute | solution.py:786
  87.6 20.4 %collective-permute-start.28 = (bf16[4,80,512]{2,1,0:T(8,128)(2,1)S(1)}, bf16[4,80,512]{2,1,0:T(8,128)(2,1)S(1)}, u32[]{:S(2)}, u32[]{:S(2)}) collective-permute-start(bf16[4,80,512]{2,1,0:T(8,128)(2,1)S(1)} %collective-permute-done.27.refs_18_), channel_id=1, source_target_pairs={{0,1},{1,0},{2,3},{3,2},{4,5},{5,4},{6,7},{7,6},{8,9},{9,8},{10,11... | collective-permute-start | bytes 983048 | tf_op jit(solution)/shard_map/ppermute | solution.py:786
  88.2 19.8 %collective-permute-start.26 = (bf16[4,80,512]{2,1,0:T(8,128)(2,1)S(1)}, bf16[4,80,512]{2,1,0:T(8,128)(2,1)S(1)}, u32[]{:S(2)}, u32[]{:S(2)}) collective-permute-start(bf16[4,80,512]{2,1,0:T(8,128)(2,1)S(1)} %collective-permute-done.25.refs_17_), channel_id=1, source_target_pairs={{0,1},{1,0},{2,3},{3,2},{4,5},{5,4},{6,7},{7,6},{8,9},{9,8},{10,11... | collective-permute-start | bytes 983048 | tf_op jit(solution)/shard_map/ppermute | solution.py:786
  88.3 19.8 %collective-permute-start.24 = (bf16[4,80,512]{2,1,0:T(8,128)(2,1)S(1)}, bf16[4,80,512]{2,1,0:T(8,128)(2,1)S(1)}, u32[]{:S(2)}, u32[]{:S(2)}) collective-permute-start(bf16[4,80,512]{2,1,0:T(8,128)(2,1)S(1)} %collective-permute-done.23.refs_16_), channel_id=1, source_target_pairs={{0,1},{1,0},{2,3},{3,2},{4,5},{5,4},{6,7},{7,6},{8,9},{9,8},{10,11... | collective-permute-start | bytes 983048 | tf_op jit(solution)/shard_map/ppermute | solution.py:786
  88.7 9.7 %collective-permute-start.2 = (bf16[2,144,256]{2,1,0:T(8,128)(2,1)S(1)}, bf16[2,144,256]{2,1,0:T(8,128)(2,1)S(1)}, u32[]{:S(2)}, u32[]{:S(2)}) collective-permute-start(bf16[2,144,256]{2,1,0:T(8,128)(2,1)S(1)} %collective-permute-done.1.refs_7_.refs_13_), channel_id=1, source_target_pairs={{0,1},{1,0},{2,3},{3,2},{4,5},{5,4},{6,7},{7,6},{8,9},{9,8},{10,11... | collective-permute-start | bytes 442376 | tf_op jit(solution)/shard_map/ppermute | solution.py:786
  200.3 13.5 %collective-permute-start.29 = (bf16[4,144,256]{2,1,0:T(8,128)(2,1)S(1)}, bf16[4,144,256]{2,1,0:T(8,128)(2,1)S(1)}, u32[]{:S(2)}, u32[]{:S(2)}) collective-permute-start(bf16[4,144,256]{2,1,0:T(8,128)(2,1)S(1)} %copy-done.20), channel_id=1, source_target_pairs={{0,1},{1,0},{2,3},{3,2},{4,5},{5,4},{6,7},{7,6},{8,9},{9,8},{10,11... | collective-permute-start | bytes 884744 | tf_op jit(solution)/shard_map/ppermute | solution.py:786
  212.9 20.5 %collective-permute-start.47 = (bf16[16,384]{1,0:T(8,128)(2,1)S(1)}, bf16[16,384]{1,0:T(8,128)(2,1)S(1)}, u32[]{:S(2)}, u32[]{:S(2)}) collective-permute-start(bf16[16,384]{1,0:T(8,128)(2,1)S(1)} %fusion.57), channel_id=1, source_target_pairs={{0,6},{1,7},{2,4},{3,5},{4,2},{5,3},{6,0},{7,1},{8,14},{9,15},{10,... | collective-permute-start | bytes 36872 | tf_op jit(solution)/shard_map/ppermute | solution.py:786
  213.8 20.8 %collective-permute-start.46 = (bf16[16,384]{1,0:T(8,128)(2,1)S(1)}, bf16[16,384]{1,0:T(8,128)(2,1)S(1)}, u32[]{:S(2)}, u32[]{:S(2)}) collective-permute-start(bf16[16,384]{1,0:T(8,128)(2,1)S(1)} %fusion.57), channel_id=1, source_target_pairs={{0,4},{1,5},{2,6},{3,7},{4,0},{5,1},{6,2},{7,3},{8,12},{9,13},{10,... | collective-permute-start | bytes 36872 | tf_op jit(solution)/shard_map/ppermute | solution.py:786
  227.8 9.9 %collective-permute-start.45 = (bf16[16,384]{1,0:T(8,128)(2,1)S(1)}, bf16[16,384]{1,0:T(8,128)(2,1)S(1)}, u32[]{:S(2)}, u32[]{:S(2)}) collective-permute-start(bf16[16,384]{1,0:T(8,128)(2,1)S(1)} %fusion.57), channel_id=1, source_target_pairs={{0,2},{1,3},{2,0},{3,1},{4,6},{5,7},{6,4},{7,5},{8,10},{9,11},{10,... | collective-permute-start | bytes 36872 | tf_op jit(solution)/shard_map/ppermute | solution.py:786
  233.3 12.4 %collective-permute-start.30 = (bf16[2,144,256]{2,1,0:T(8,128)(2,1)S(1)}, bf16[2,144,256]{2,1,0:T(8,128)(2,1)S(1)}, u32[]{:S(2)}, u32[]{:S(2)}) collective-permute-start(bf16[2,144,256]{2,1,0:T(8,128)(2,1)S(1)} %slice_select_fusion.2), channel_id=1, source_target_pairs={{2,0},{3,1},{6,4},{7,5},{10,8},{11,9},{14,12},{15,13},{18,16},{19,... | collective-permute-start | bytes 442376 | tf_op jit(solution)/shard_map/ppermute | solution.py:878
  234.7 12.4 %collective-permute-start.33 = (bf16[2,144,256]{2,1,0:T(8,128)(2,1)S(1)}, bf16[2,144,256]{2,1,0:T(8,128)(2,1)S(1)}, u32[]{:S(2)}, u32[]{:S(2)}) collective-permute-start(bf16[2,144,256]{2,1,0:T(8,128)(2,1)S(1)} %slice_select_fusion.1), channel_id=1, source_target_pairs={{2,0},{3,1},{6,4},{7,5},{10,8},{11,9},{14,12},{15,13},{18,16},{19,... | collective-permute-start | bytes 442376 | tf_op jit(solution)/shard_map/ppermute | solution.py:878
  242.5 43.1 %collective-permute-start.49 = (bf16[4,16,384]{2,1,0:T(8,128)(2,1)S(1)}, bf16[4,16,384]{2,1,0:T(8,128)(2,1)S(1)}, u32[]{:S(2)}, u32[]{:S(2)}) collective-permute-start(bf16[4,16,384]{2,1,0:T(8,128)(2,1)S(1)} %get-tuple-element.202), channel_id=1, source_target_pairs={{0,16},{1,17},{2,18},{3,19},{4,20},{5,21},{6,22},{7,23},{8,24},{9,... | collective-permute-start | bytes 147464 | tf_op jit(solution)/shard_map/ppermute | solution.py:786
  243.9 49.6 %collective-permute-start.48 = (bf16[4,16,384]{2,1,0:T(8,128)(2,1)S(1)}, bf16[4,16,384]{2,1,0:T(8,128)(2,1)S(1)}, u32[]{:S(2)}, u32[]{:S(2)}) collective-permute-start(bf16[4,16,384]{2,1,0:T(8,128)(2,1)S(1)} %get-tuple-element.202), channel_id=1, source_target_pairs={{0,8},{1,9},{2,10},{3,11},{4,12},{5,13},{6,14},{7,15},{8,0},{9,1},... | collective-permute-start | bytes 147464 | tf_op jit(solution)/shard_map/ppermute | solution.py:786
  245.7 47.9 %collective-permute-start.50 = (bf16[4,16,384]{2,1,0:T(8,128)(2,1)S(1)}, bf16[4,16,384]{2,1,0:T(8,128)(2,1)S(1)}, u32[]{:S(2)}, u32[]{:S(2)}) collective-permute-start(bf16[4,16,384]{2,1,0:T(8,128)(2,1)S(1)} %get-tuple-element.202), channel_id=1, source_target_pairs={{0,24},{1,25},{2,26},{3,27},{4,28},{5,29},{6,30},{7,31},{8,16},{9,... | collective-permute-start | bytes 147464 | tf_op jit(solution)/shard_map/ppermute | solution.py:786
  247.0 20.2 %collective-permute-start.31 = (bf16[2,144,256]{2,1,0:T(8,128)(2,1)S(1)}, bf16[2,144,256]{2,1,0:T(8,128)(2,1)S(1)}, u32[]{:S(2)}, u32[]{:S(2)}) collective-permute-start(bf16[2,144,256]{2,1,0:T(8,128)(2,1)S(1)} %collective-permute-done.30.refs_9_), channel_id=1, source_target_pairs={{0,1},{1,0},{2,3},{3,2},{4,5},{5,4},{6,7},{7,6},{8,9},{9,8},{10,11... | collective-permute-start | bytes 442376 | tf_op jit(solution)/shard_map/ppermute | solution.py:786
  247.0 9.8 %collective-permute-start.34 = (bf16[2,144,256]{2,1,0:T(8,128)(2,1)S(1)}, bf16[2,144,256]{2,1,0:T(8,128)(2,1)S(1)}, u32[]{:S(2)}, u32[]{:S(2)}) collective-permute-start(bf16[2,144,256]{2,1,0:T(8,128)(2,1)S(1)} %collective-permute-done.33.refs_9_), channel_id=1, source_target_pairs={{0,1},{1,0},{2,3},{3,2},{4,5},{5,4},{6,7},{7,6},{8,9},{9,8},{10,11... | collective-permute-start | bytes 442376 | tf_op jit(solution)/shard_map/ppermute | solution.py:786
  256.9 37.2 %collective-permute-start.62 = (bf16[4,16,768]{2,1,0:T(8,128)(2,1)S(1)}, bf16[4,16,768]{2,1,0:T(8,128)(2,1)S(1)}, u32[]{:S(2)}, u32[]{:S(2)}) collective-permute-start(bf16[4,16,768]{2,1,0:T(8,128)(2,1)S(1)} %get-tuple-element.187), channel_id=1, source_target_pairs={{0,4},{1,5},{2,6},{3,7},{4,0},{5,1},{6,2},{7,3},{8,12},{9,13},{10,... | collective-permute-start | bytes 294920 | tf_op jit(solution)/shard_map/ppermute | solution.py:786
  267.3 27.0 %collective-permute-start.61 = (bf16[4,16,768]{2,1,0:T(8,128)(2,1)S(1)}, bf16[4,16,768]{2,1,0:T(8,128)(2,1)S(1)}, u32[]{:S(2)}, u32[]{:S(2)}) collective-permute-start(bf16[4,16,768]{2,1,0:T(8,128)(2,1)S(1)} %get-tuple-element.187), channel_id=1, source_target_pairs={{0,2},{1,3},{2,0},{3,1},{4,6},{5,7},{6,4},{7,5},{8,10},{9,11},{10,... | collective-permute-start | bytes 294920 | tf_op jit(solution)/shard_map/ppermute | solution.py:786
  293.5 16.1 %collective-permute-start.92 = (bf16[4,4,48,512]{3,2,1,0:T(8,128)(2,1)S(1)}, bf16[4,4,48,512]{3,2,1,0:T(8,128)(2,1)S(1)}, u32[]{:S(2)}, u32[]{:S(2)}) collective-permute-start(bf16[4,4,48,512]{3,2,1,0:T(8,128)(2,1)S(1)} %copy-done.31), channel_id=1, source_target_pairs={{0,1},{1,0},{2,3},{3,2},{4,5},{5,4},{6,7},{7,6},{8,9},{9,8},{10,11... | collective-permute-start | bytes 2359304 | tf_op jit(solution)/shard_map/ppermute | solution.py:786
  293.6 70.3 %collective-permute-start.99 = (bf16[4,4,80,512]{3,2,1,0:T(8,128)(2,1)S(1)}, bf16[4,4,80,512]{3,2,1,0:T(8,128)(2,1)S(1)}, u32[]{:S(2)}, u32[]{:S(2)}) collective-permute-start(bf16[4,4,80,512]{3,2,1,0:T(8,128)(2,1)S(1)} %copy-done.30), channel_id=1, source_target_pairs={{0,1},{1,0},{2,3},{3,2},{4,5},{5,4},{6,7},{7,6},{8,9},{9,8},{10,11... | collective-permute-start | bytes 3932168 | tf_op jit(solution)/shard_map/ppermute | solution.py:786
  301.7 14.0 %collective-permute-start.78 = (bf16[4,4,16,640]{3,2,1,0:T(8,128)(2,1)S(1)}, bf16[4,4,16,640]{3,2,1,0:T(8,128)(2,1)S(1)}, u32[]{:S(2)}, u32[]{:S(2)}) collective-permute-start(bf16[4,4,16,640]{3,2,1,0:T(8,128)(2,1)S(1)} %copy-done.36), channel_id=1, source_target_pairs={{0,1},{1,0},{2,3},{3,2},{4,5},{5,4},{6,7},{7,6},{8,9},{9,8},{10,11... | collective-permute-start | bytes 983048 | tf_op jit(solution)/shard_map/ppermute | solution.py:786
  310.9 17.1 %collective-permute-start.93 = (bf16[4,48,512]{2,1,0:T(8,128)(2,1)S(1)}, bf16[4,48,512]{2,1,0:T(8,128)(2,1)S(1)}, u32[]{:S(2)}, u32[]{:S(2)}) collective-permute-start(bf16[4,48,512]{2,1,0:T(8,128)(2,1)S(1)} %get-tuple-element.157), channel_id=1, source_target_pairs={{0,8},{1,9},{2,10},{3,11},{4,12},{5,13},{6,14},{7,15},{8,0},{9,1},... | collective-permute-start | bytes 589832 | tf_op jit(solution)/shard_map/ppermute | solution.py:786
  325.0 14.8 %collective-permute-start.94 = (bf16[4,48,512]{2,1,0:T(8,128)(2,1)S(1)}, bf16[4,48,512]{2,1,0:T(8,128)(2,1)S(1)}, u32[]{:S(2)}, u32[]{:S(2)}) collective-permute-start(bf16[4,48,512]{2,1,0:T(8,128)(2,1)S(1)} %get-tuple-element.159), channel_id=1, source_target_pairs={{0,16},{1,17},{2,18},{3,19},{4,20},{5,21},{6,22},{7,23},{8,24},{9,... | collective-permute-start | bytes 589832 | tf_op jit(solution)/shard_map/ppermute | solution.py:786
  325.1 21.9 %collective-permute-start.76 = (bf16[4,16,384]{2,1,0:T(8,128)(2,1)S(1)}, bf16[4,16,384]{2,1,0:T(8,128)(2,1)S(1)}, u32[]{:S(2)}, u32[]{:S(2)}) collective-permute-start(bf16[4,16,384]{2,1,0:T(8,128)(2,1)S(1)} %get-tuple-element.197), channel_id=1, source_target_pairs={{0,16},{1,17},{2,18},{3,19},{4,20},{5,21},{6,22},{7,23},{8,24},{9,... | collective-permute-start | bytes 147464 | tf_op jit(solution)/shard_map/ppermute | solution.py:786
  328.0 11.9 %collective-permute-start.82 = (bf16[16,640]{1,0:T(8,128)(2,1)S(1)}, bf16[16,640]{1,0:T(8,128)(2,1)S(1)}, u32[]{:S(2)}, u32[]{:S(2)}) collective-permute-start(bf16[16,640]{1,0:T(8,128)(2,1)S(1)} %get-tuple-element.193), channel_id=1, source_target_pairs={{0,8},{1,9},{2,10},{3,11},{4,12},{5,13},{6,14},{7,15},{8,0},{9,1},... | collective-permute-start | bytes 61448 | tf_op jit(solution)/shard_map/ppermute | solution.py:786
  330.1 12.8 %collective-permute-start.84 = (bf16[16,640]{1,0:T(8,128)(2,1)S(1)}, bf16[16,640]{1,0:T(8,128)(2,1)S(1)}, u32[]{:S(2)}, u32[]{:S(2)}) collective-permute-start(bf16[16,640]{1,0:T(8,128)(2,1)S(1)} %get-tuple-element.194), channel_id=1, source_target_pairs={{0,24},{1,25},{2,26},{3,27},{4,28},{5,29},{6,30},{7,31},{8,16},{9,... | collective-permute-start | bytes 61448 | tf_op jit(solution)/shard_map/ppermute | solution.py:786
  355.0 13.0 %collective-permute-start.64 = (bf16[4,4,16,1152]{3,2,1,0:T(8,128)(2,1)S(1)}, bf16[4,4,16,1152]{3,2,1,0:T(8,128)(2,1)S(1)}, u32[]{:S(2)}, u32[]{:S(2)}) collective-permute-start(bf16[4,4,16,1152]{3,2,1,0:T(8,128)(2,1)S(1)} %maximum_maximum_fusion), channel_id=1, source_target_pairs={{0,1},{1,0},{2,3},{3,2},{4,5},{5,4},{6,7},{7,6},{8,9},{9,8},{10,11... | collective-permute-start | bytes 1769480 | tf_op jit(solution)/shard_map/ppermute | solution.py:786
  364.2 10.4 %collective-permute-start.100 = (bf16[4,80,512]{2,1,0:T(8,128)(2,1)S(1)}, bf16[4,80,512]{2,1,0:T(8,128)(2,1)S(1)}, u32[]{:S(2)}, u32[]{:S(2)}) collective-permute-start(bf16[4,80,512]{2,1,0:T(8,128)(2,1)S(1)} %get-tuple-element.154), channel_id=1, source_target_pairs={{0,2},{1,3},{2,0},{3,1},{4,6},{5,7},{6,4},{7,5},{8,10},{9,11},{10,... | collective-permute-start | bytes 983048 | tf_op jit(solution)/shard_map/ppermute | solution.py:786
  365.1 13.9 %collective-permute-start.102 = (bf16[4,80,512]{2,1,0:T(8,128)(2,1)S(1)}, bf16[4,80,512]{2,1,0:T(8,128)(2,1)S(1)}, u32[]{:S(2)}, u32[]{:S(2)}) collective-permute-start(bf16[4,80,512]{2,1,0:T(8,128)(2,1)S(1)} %get-tuple-element.155), channel_id=1, source_target_pairs={{0,6},{1,7},{2,4},{3,5},{4,2},{5,3},{6,0},{7,1},{8,14},{9,15},{10,... | collective-permute-start | bytes 983048 | tf_op jit(solution)/shard_map/ppermute | solution.py:786
  366.9 13.5 %collective-permute-start.101 = (bf16[4,80,512]{2,1,0:T(8,128)(2,1)S(1)}, bf16[4,80,512]{2,1,0:T(8,128)(2,1)S(1)}, u32[]{:S(2)}, u32[]{:S(2)}) collective-permute-start(bf16[4,80,512]{2,1,0:T(8,128)(2,1)S(1)} %get-tuple-element.156), channel_id=1, source_target_pairs={{0,4},{1,5},{2,6},{3,7},{4,0},{5,1},{6,2},{7,3},{8,12},{9,13},{10,... | collective-permute-start | bytes 983048 | tf_op jit(solution)/shard_map/ppermute | solution.py:786
  367.9 16.4 %collective-permute-start.91 = (bf16[4,4,16,1024]{3,2,1,0:T(8,128)(2,1)S(1)}, bf16[4,4,16,1024]{3,2,1,0:T(8,128)(2,1)S(1)}, u32[]{:S(2)}, u32[]{:S(2)}) collective-permute-start(bf16[4,4,16,1024]{3,2,1,0:T(8,128)(2,1)S(1)} %maximum_maximum_fusion.1), channel_id=1, source_target_pairs={{0,1},{1,0},{2,3},{3,2},{4,5},{5,4},{6,7},{7,6},{8,9},{9,8},{10,11... | collective-permute-start | bytes 1572872 | tf_op jit(solution)/shard_map/ppermute | solution.py:786
  (105 other events, 938.0 us)

commit v2 on v1

v2 whole, which is shorter than its diff:
```python
import functools
import math

import jax
import jax.numpy as jnp
from jax import lax
from jax.experimental import pallas as pl
from jax.experimental.pallas import tpu as pltpu
from jax.sharding import PartitionSpec as P

epsilon = 1e-05
bf16 = jnp.bfloat16
f32 = jnp.float32
AXES = ("dp", "seq")
MIB = 2**20


def nn(a, b):
    return lax.dot_general(a, b, (((1,), (0,)), ((), ())), preferred_element_type=f32)


def nt(a, b):
    return lax.dot_general(a, b, (((1,), (1,)), ((), ())), preferred_element_type=f32)


def tn(a, b):
    return lax.dot_general(a, b, (((0,), (0,)), ((), ())), preferred_element_type=f32)


def lanes_of(shape):
    return lax.broadcasted_iota(jnp.int32, shape, len(shape) - 1)


def params(mib=56):
    return pltpu.CompilerParams(vmem_limit_bytes=mib * MIB)


def cost(flops, nbytes, trans=0):
    return pl.CostEstimate(flops=int(flops), bytes_accessed=int(nbytes), transcendentals=int(trans))


def const_block(shape):
    return pl.BlockSpec(shape, lambda *_: (0,) * len(shape))


def stacked_call(kernel, grid, in_specs, out_specs, out_shapes, stacked, before, args, scratch, estimate, after=()):
    n_in = len(args)
    aliases = {}
    extra = list(after)
    if before is not None:
        for at, (flag, buffer) in enumerate(zip(stacked, before)):
            if flag:
                aliases[n_in + len(extra)] = at
                extra.append(buffer)
    n_extra = len(extra)

    def body(*refs):
        kernel(*refs[:n_in], *refs[n_in + n_extra :])

    return pl.pallas_call(
        body,
        grid=grid,
        in_specs=list(in_specs) + [pl.BlockSpec(memory_space=pl.ANY)] * n_extra,
        out_specs=out_specs,
        out_shape=out_shapes,
        scratch_shapes=scratch,
        input_output_aliases=aliases,
        compiler_params=params(),
        cost_estimate=estimate,
    )(*args, *extra)


def normed(values):
    center = values - jnp.mean(values, axis=-1, keepdims=True)
    spread = jnp.mean(center * center, axis=-1, keepdims=True)
    scale = lax.rsqrt(spread + epsilon)
    return center * scale, scale


def norm_back(grad, xhat, scale, gain):
    gy = grad * gain
    return scale * (
        gy - jnp.mean(gy, axis=-1, keepdims=True) - xhat * jnp.mean(gy * xhat, axis=-1, keepdims=True)
    )


def causal_tile(rows):
    return lax.broadcasted_iota(jnp.int32, (rows, rows), 0) >= lax.broadcasted_iota(
        jnp.int32, (rows, rows), 1
    )


def feature_weights(omega, odd):
    ones = jnp.full(omega.shape, -1.0, omega.dtype)
    zeros = jnp.zeros_like(ones)
    parts = [ones, omega, zeros, ones] if odd else [omega, ones, ones, zeros]
    return jnp.concatenate(parts, axis=1)


def features_kernel(hd, x_ref, gains_ref, w_ref, omega_ref, qkv_ref, phiq_ref, phik_ref, h1_ref, state_ref, qkv_scr):
    pair = pl.program_id(0)
    width = 2 * hd
    model = x_ref.shape[-1]
    s = hd ** (-0.25)
    feats = omega_ref.shape[1]

    @pl.when(pair == 0)
    def _():
        xhat, _ = normed(x_ref[0].astype(f32))
        hidden = (xhat * gains_ref[0:1, :]).astype(bf16)
        h1_ref[0] = hidden
        for part in range(3):
            cols = slice(part * model, (part + 1) * model)
            made = nn(hidden, w_ref[:, cols]).astype(bf16)
            qkv_ref[0, :, cols] = made
            qkv_scr[part] = made

    column = pl.ds(pl.multiple_of(pair * width, width), width)
    rows = x_ref.shape[1]
    low = lanes_of((rows, width)) < hd
    weights = [feature_weights(omega_ref[odd], odd) for odd in range(2)]

    def phi_pair(part, out_ref):
        points = qkv_scr[part, :, column].astype(f32)
        energy = points * points * (0.5 * s)
        high = energy.astype(bf16).astype(f32)
        rest = (energy - high).astype(bf16)
        turned = pltpu.roll(high, hd, 1)
        made = []
        for odd in range(2):
            first = jnp.where(low, turned, points) if odd else jnp.where(low, points, turned)
            left = jnp.concatenate([first.astype(bf16), rest], axis=1)
            proj = nt(left, weights[odd])
            phi = jnp.exp2(proj * (s * math.log2(math.e)) - 0.5 * math.log2(feats))
            phi_low = phi.astype(bf16)
            out_ref[0, :, odd * feats : (odd + 1) * feats] = phi_low
            made.append(phi_low)
        return made

    phi_pair(0, phiq_ref)
    even_k, odd_k = phi_pair(1, phik_ref)
    values = qkv_scr[2, :, column]
    state_ref[0, 0:hd, :] = tn(values, even_k)[0:hd].astype(bf16)
    state_ref[0, hd:width, :] = tn(values, odd_k)[hd:width].astype(bf16)
    sums = jnp.concatenate(
        [
            jnp.sum(even_k.astype(f32), axis=0, keepdims=True),
            jnp.sum(odd_k.astype(f32), axis=0, keepdims=True),
            jnp.zeros((14, feats), f32),
        ],
        axis=0,
    )
    state_ref[0, width : width + 16, :] = sums.astype(bf16)


def features_call(index, at, count, inputs, gains, w_qkv, omega, before, after=()):
    batch, rows, model = inputs.shape
    heads, feats, hd = omega.shape
    pairs = heads // 2
    width = 2 * hd
    n_rows = width + 16
    phi_spec = pl.BlockSpec((1, rows, 2 * feats), lambda p: (index, 0, p))
    return stacked_call(
        functools.partial(features_kernel, hd),
        (pairs,),
        [
            pl.BlockSpec((1, rows, model), lambda p: (index, 0, 0)),
            const_block(gains.shape),
            const_block(w_qkv.shape),
            pl.BlockSpec((2, feats, hd), lambda p: (p, 0, 0)),
        ],
        [
            pl.BlockSpec((1, rows, 3 * model), lambda p: (index, 0, 0)),
            phi_spec,
            phi_spec,
            pl.BlockSpec((1, rows, model), lambda p: (index, 0, 0)),
            pl.BlockSpec((1, n_rows, feats), lambda p: (at * pairs + p, 0, 0)),
        ],
        [
            jax.ShapeDtypeStruct((batch, rows, 3 * model), bf16),
            jax.ShapeDtypeStruct((batch, rows, heads * feats), bf16),
            jax.ShapeDtypeStruct((batch, rows, heads * feats), bf16),
            jax.ShapeDtypeStruct((batch, rows, model), bf16),
            jax.ShapeDtypeStruct((count * pairs, n_rows, feats), bf16),
        ],
        (True, True, True, True, at > 0),
        before,
        (inputs, gains, w_qkv, omega),
        [pltpu.VMEM((3, rows, model), bf16)],
        cost(2 * rows * model * 3 * model + 4 * heads * rows * 256 * feats, 9 * MIB, 2 * rows * heads * feats),
        after,
    )


def state_block(state_refs, backward, pair, hd, first, count):
    if len(state_refs) == 1:
        total = state_refs[0][0].astype(f32)
    else:
        near, got, other = state_refs
        core = lax.rem(lax.axis_index("seq"), 2)
        own_half = (first + pair) // (count // 2) == core
        own = jnp.where(own_half, 1.0, 0.0)
        beside = jnp.where(core == (0 if backward else 1), 1.0, 0.0)
        total = (
            got[0].astype(f32) * own + other[0].astype(f32) * (1.0 - own) + near[0].astype(f32) * beside
        )
    feats = total.shape[-1]
    width = 2 * hd
    zeros = jnp.zeros((hd, feats), bf16)
    low = total.astype(bf16)
    even_norm = jnp.broadcast_to(total[width : width + 1], (hd, feats)).astype(bf16)
    odd_norm = jnp.broadcast_to(total[width + 1 : width + 2], (hd, feats)).astype(bf16)
    even = jnp.concatenate([low[0:hd], zeros, even_norm, zeros], axis=0)
    odd = jnp.concatenate([zeros, low[hd:width], zeros, odd_norm], axis=0)
    return even, odd


def state_specs(carried, pairs):
    states, at, count = carried
    shape = (1,) + states[0].shape[1:]
    first = at * pairs
    specs = [pl.BlockSpec(shape, lambda g: (first + g, 0, 0))]
    if len(states) > 1:
        specs += [pl.BlockSpec(shape, lambda g: (lax.rem(first + g, count // 2), 0, 0))] * 2
    return specs


def mix_kernel(hd, n_states, first, count, tile, *refs):
    x_ref, gains_ref, wout_ref, phiq_ref, phik_ref, v_ref = refs[:6]
    state_refs = refs[6 : 6 + n_states]
    mixed_ref, rden_ref, x1_ref, h2_ref, mixed_scr = refs[6 + n_states :]
    step = pl.program_id(0)
    width = 2 * hd
    pairs = wout_ref.shape[0] // width
    pair = lax.rem(step, pairs)
    rows = x_ref.shape[1]
    feats = phiq_ref.shape[-1] // 2
    column = pl.ds(pl.multiple_of(pair * width, width), width)
    even_state, odd_state = state_block(state_refs, False, step, hd, first, count)
    both_state = jnp.concatenate([even_state, odd_state], axis=1)
    low = lanes_of((rows, width)) < hd
    values = v_ref[0].astype(f32)
    ones = jnp.where(low, 1.0, 0.0)
    sides = [
        jnp.concatenate([jnp.where(low, values, 0.0), ones], axis=1).astype(bf16),
        jnp.concatenate([jnp.where(low, 0.0, values), 1.0 - ones], axis=1).astype(bf16),
    ]
    causal = causal_tile(tile)
    for at in range(rows // tile):
        here = slice(at * tile, (at + 1) * tile)
        end = (at + 1) * tile
        total = nt(phiq_ref[0, here, :], both_state)
        for odd in range(2):
            cols = slice(odd * feats, (odd + 1) * feats)
            made = masked(nt(phiq_ref[0, here, cols], phik_ref[0, 0:end, cols]), causal, at, tile)
            total = total + nn(made, sides[odd][0:end])
        rden = 1.0 / total[:, width:]
        mixed = (total[:, :width] * rden).astype(bf16)
        rden_ref[0, here, :] = rden
        mixed_ref[0, here, :] = mixed
        mixed_scr[here, column] = mixed

    @pl.when(pair == pairs - 1)
    def _():
        x1 = x_ref[0].astype(f32) + nn(mixed_scr[...], wout_ref[...])
        x1_ref[0] = x1
        xhat, _ = normed(x1)
        h2_ref[0] = (xhat * gains_ref[1:2, :]).astype(bf16)


def masked(made, causal, at, tile):
    last = jnp.where(causal, made[:, at * tile :], 0.0)
    if at > 0:
        last = jnp.concatenate([made[:, : at * tile], last], axis=1)
    return last.astype(bf16)


def mix_call(index, members, inputs, gains, w_out, phi_q, phi_k, qkv, carried, before, hd, after=()):
    batch, rows, model = inputs.shape
    width = 2 * hd
    pairs = model // width
    states, at, count = carried
    heads = 2 * pairs
    feats = phi_q.shape[-1] // heads
    tile = min(256, rows)
    whole = pl.BlockSpec((1, rows, model), lambda g: (index + g // pairs, 0, 0))
    narrow = pl.BlockSpec((1, rows, width), lambda g: (index + g // pairs, 0, lax.rem(g, pairs)))
    phi_spec = pl.BlockSpec((1, rows, 2 * feats), lambda g: (index + g // pairs, 0, lax.rem(g, pairs)))
    return stacked_call(
        functools.partial(mix_kernel, hd, len(states), at * pairs, count, tile),
        (members * pairs,),
        [
            whole,
            const_block(gains.shape),
            const_block(w_out.shape),
            phi_spec,
            phi_spec,
            pl.BlockSpec((1, rows, width), lambda g: (index + g // pairs, 0, 2 * pairs + lax.rem(g, pairs))),
        ]
        + state_specs(carried, pairs),
        [narrow, narrow, whole, whole],
        [
            jax.ShapeDtypeStruct((batch, rows, model), bf16),
            jax.ShapeDtypeStruct((batch, rows, model), f32),
            jax.ShapeDtypeStruct((batch, rows, model), f32),
            jax.ShapeDtypeStruct((batch, rows, model), bf16),
        ],
        (True,) * 4,
        before,
        (inputs, gains, w_out, phi_q, phi_k, qkv) + tuple(states),
        [pltpu.VMEM((rows, model), bf16)],
        cost(members * (heads * 2 * rows * rows * 512 + 2 * rows * model * model), members * 9 * MIB),
        after,
    )


def ffn_kernel(groups, batch, hd, *refs):
    h2_ref, gf_ref, x1_ref, mixed_ref, rden_ref, phiq_ref, wout_ref, gains_ref = refs[:8]
    weights = refs[8 : 8 + groups]
    act_ref, pre_ref, g1_ref, ga_ref, gain_ref, side_ref, gstate_ref = refs[8 + groups : 15 + groups]
    up_scr, down_scr, pre_scr, sems = refs[15 + groups :]
    step = pl.program_id(0)
    n_blocks = pl.num_programs(0) - batch
    each = n_blocks // groups
    block = act_ref.shape[-1]
    rows = h2_ref.shape[1]
    model = h2_ref.shape[2]
    shards, unit = up_scr.shape[1:3]
    taken = block // unit
    started = []
    for group in range(groups):
        started.append(pltpu.make_async_copy(weights[group].at[:, 0], up_scr.at[group], sems.at[2 * group]))
        started.append(pltpu.make_async_copy(weights[group].at[:, 1], down_scr.at[group], sems.at[2 * group + 1]))

    @pl.when(step == 0)
    def _():
        for copy in started:
            copy.start()

    for group in range(groups):

        @pl.when(step == group * each)
        def _():
            started[2 * group].wait()
            started[2 * group + 1].wait()

    @pl.when(step < n_blocks)
    def _():
        here = pl.ds(pl.multiple_of(lax.rem(step, each) * taken, taken), taken)
        up = up_scr[step // each, here].reshape(block, model)
        down = down_scr[step // each, here].reshape(block, model)
        cols = pl.ds(pl.multiple_of(step * block, block), block)
        for b in range(batch):
            pre = nt(h2_ref[b], up)
            part = 0.5 * lax.erf(pre * math.sqrt(0.5)) + 0.5
            act_ref[b] = (pre * part).astype(bf16)
            slope = part + pre * (
                jnp.exp2(pre * pre * (-0.5 * math.log2(math.e))) * (1.0 / math.sqrt(2.0 * math.pi))
            )
            grad_pre = (nt(gf_ref[b], down) * slope).astype(bf16)
            pre_ref[b] = grad_pre
            pre_scr[b, :, cols] = grad_pre

    @pl.when(step >= n_blocks)
    def _():
        b = step - n_blocks
        grad = nn(pre_scr[b], up_scr[...].reshape(n_blocks * block, model))
        xhat, scale = normed(x1_ref[0])
        g1 = gf_ref[b].astype(f32) + norm_back(grad, xhat, scale, gains_ref[1:2, :])
        g1_ref[0] = g1
        gain = jnp.sum(grad * xhat, axis=0, keepdims=True)

        @pl.when(b == 0)
        def _():
            gain_ref[...] = jnp.zeros_like(gain_ref)

        gain_ref[0:1] += gain
        ga = g1.astype(bf16)
        ga_ref[0] = ga
        gn_full = nt(ga, wout_ref[...]) * rden_ref[0]
        gn_low = gn_full.astype(bf16)
        product = gn_full * mixed_ref[0].astype(f32)
        high = product.astype(bf16)
        rest = (product - high.astype(f32)).astype(bf16)
        width = 2 * hd
        same = lax.div(lax.rem(lax.broadcasted_iota(jnp.int32, (2 * width, width), 0), width), hd) == lax.div(
            lax.broadcasted_iota(jnp.int32, (2 * width, width), 1), hd
        )
        minus = jnp.where(same, -1.0, 0.0).astype(bf16)
        inner = lax.rem(lanes_of((rows, width)), hd)
        feats = phiq_ref.shape[-1] // (model // hd)
        for at in range(model // width):
            cols = slice(at * width, (at + 1) * width)
            gd = nn(jnp.concatenate([high[:, cols], rest[:, cols]], axis=1), minus)
            gd_high = gd.astype(bf16).astype(f32)
            gdx = jnp.where(inner == 0, gd_high, jnp.where(inner == 1, gd - gd_high, 0.0))
            side = jnp.concatenate([gn_low[:, cols], gdx.astype(bf16)], axis=1)
            side_ref[0, at] = side
            even = tn(side, phiq_ref[0, :, 2 * at * feats : (2 * at + 1) * feats])
            odd = tn(side, phiq_ref[0, :, (2 * at + 1) * feats : (2 * at + 2) * feats])
            gstate_ref[at, 0:hd] = even[0:hd].astype(bf16)
            gstate_ref[at, hd:width] = odd[hd:width].astype(bf16)
            norms = jnp.concatenate(
                [
                    even[width : width + 1] + even[width + 1 : width + 2],
                    odd[width + hd : width + hd + 1] + odd[width + hd + 1 : width + hd + 2],
                    jnp.zeros((14, feats), f32),
                ],
                axis=0,
            )
            gstate_ref[at, width : width + 16] = norms.astype(bf16)


def ffn_call(h2, gf, x1, mixed, rden, phi_q, w_out, gains, weights, hd):
    batch, rows, model = h2.shape
    groups = len(weights)
    shards, _, unit, _ = weights[0].shape
    hidden = groups * shards * unit
    block = min(512, shards * unit)
    n_blocks = hidden // block
    pairs = model // (2 * hd)
    feats = phi_q.shape[-1] // (2 * pairs)
    n_rows = 2 * hd + 16
    here = lambda j: jnp.clip(j - n_blocks, 0, batch - 1)
    late = pl.BlockSpec((1, rows, model), lambda j: (here(j), 0, 0))
    wide = pl.BlockSpec((batch, rows, block), lambda j: (0, 0, jnp.minimum(j, n_blocks - 1)))
    scratch = (groups, shards, unit, model)
    return pl.pallas_call(
        functools.partial(ffn_kernel, groups, batch, hd),
        grid=(n_blocks + batch,),
        in_specs=[
            const_block(h2.shape),
            const_block(gf.shape),
            late,
            late,
            late,
            pl.BlockSpec((1, rows, phi_q.shape[-1]), lambda j: (here(j), 0, 0)),
            const_block(w_out.shape),
            const_block(gains.shape),
        ]
        + [pl.BlockSpec(memory_space=pl.ANY)] * groups,
        out_specs=[
            wide,
            wide,
            late,
            late,
            const_block((16, model)),
            pl.BlockSpec((1, pairs, rows, 4 * hd), lambda j: (here(j), 0, 0, 0)),
            pl.BlockSpec((pairs, n_rows, feats), lambda j: (here(j), 0, 0)),
        ],
        out_shape=[
            jax.ShapeDtypeStruct((batch, rows, hidden), bf16),
            jax.ShapeDtypeStruct((batch, rows, hidden), bf16),
            jax.ShapeDtypeStruct((batch, rows, model), f32),
            jax.ShapeDtypeStruct((batch, rows, model), bf16),
            jax.ShapeDtypeStruct((16, model), f32),
            jax.ShapeDtypeStruct((batch, pairs, rows, 4 * hd), bf16),
            jax.ShapeDtypeStruct((batch * pairs, n_rows, feats), bf16),
        ],
        scratch_shapes=[
            pltpu.VMEM(scratch, bf16),
            pltpu.VMEM(scratch, bf16),
            pltpu.VMEM((batch, rows, hidden), bf16),
            pltpu.SemaphoreType.DMA((2 * groups,)),
        ],
        compiler_params=params(),
        cost_estimate=cost(6 * batch * rows * hidden * model, 30 * MIB, 2 * batch * rows * hidden),
    )(h2, gf, x1, mixed, rden, phi_q, w_out, gains, *weights)


def row_owner(far, first, second):
    seq = lax.axis_index("seq")
    y, x = lax.rem(lax.axis_index("dp"), 2), seq // 2
    core = lax.rem(seq, 2) ^ far
    turned = core == 1
    y = y ^ jnp.where(turned, second, first)
    x = x ^ jnp.where(turned, first, second)
    return core * 4 + y * 2 + x


EXTRA = 16


def ffn_weight_kernel(groups, fast, n_after, *refs):
    act_ref, pre_ref, gf_ref, h2_ref, gain_ref, mixed_any, ga_any = refs[:7]
    outs = refs[7 + n_after : 9 + n_after]
    mixed_scr, ga_scr, sum_scr, sems = refs[9 + n_after :]
    step = pl.program_id(0)
    n_blocks = pl.num_programs(0) - 1
    batch, rows, block = act_ref.shape
    model = gf_ref.shape[2]
    copies = [
        pltpu.make_async_copy(mixed_any, mixed_scr, sems.at[0]),
        pltpu.make_async_copy(ga_any, ga_scr, sems.at[1]),
    ]

    @pl.when(step == 0)
    def _():
        for copy in copies:
            copy.start()

    @pl.when(step < n_blocks)
    def _():
        down = tn(act_ref[...].reshape(batch * rows, block), gf_ref[...].reshape(batch * rows, model)).astype(bf16)
        up = tn(pre_ref[...].reshape(batch * rows, block), h2_ref[...].reshape(batch * rows, model)).astype(bf16)
        if not fast:
            outs[0][0, 0] = up
            outs[0][0, 1] = down
            return
        unit = block // 8
        held = outs[0].shape[0] // 2
        for group in range(groups):

            @pl.when(step == group)
            def _():
                out = outs[group // 2]
                first = (group % 2) * held
                for at in range(8):
                    row = first + 2 * at * unit
                    here = slice(at * unit, (at + 1) * unit)
                    out[row : row + unit] = up[here]
                    out[row + unit : row + 2 * unit] = down[here]

    @pl.when(step == n_blocks)
    def _():
        for copy in copies:
            copy.wait()
        total = tn(mixed_scr[...].reshape(batch * rows, model), ga_scr[...].reshape(batch * rows, model))
        if not fast:
            outs[1][...] = total
            return
        sum_scr[...] = total
        piece = model // 8
        held = outs[0].shape[0] // 2
        gain = gain_ref[...].astype(bf16)
        for far in range(2):
            for first in range(2):
                for second in range(2):
                    owner = row_owner(far, first, second)
                    taken = sum_scr[pl.ds(pl.multiple_of(owner * piece, piece), piece), :].astype(bf16)
                    out = outs[0 if far else 1]
                    row = (first + 1) * held - (2 - second) * (piece + EXTRA)
                    out[row : row + piece] = taken
                    out[row + piece : row + piece + EXTRA] = gain


def ffn_weight_call(act, pre, gf, h2, gain, mixed, ga, weights, fast, after=()):
    batch, rows, model = h2.shape
    groups = len(weights)
    shards, _, unit, _ = weights[0].shape
    hidden = act.shape[-1]
    block = min(512, shards * unit)
    n_blocks = hidden // block
    wide = pl.BlockSpec((batch, rows, block), lambda j: (0, 0, jnp.minimum(j, n_blocks - 1)))
    if fast:
        shape = (4 * shards * unit + 4 * (model // 8 + EXTRA), model)
        out_specs = [const_block(shape)] * 2
        out_shapes = [jax.ShapeDtypeStruct(shape, bf16)] * 2
    else:
        out_specs = [
            pl.BlockSpec((1, 2, block, model), lambda j: (jnp.minimum(j, n_blocks - 1), 0, 0, 0)),
            const_block((model, model)),
        ]
        out_shapes = [
            jax.ShapeDtypeStruct((n_blocks, 2, block, model), bf16),
            jax.ShapeDtypeStruct((model, model), f32),
        ]
    anywhere = pl.BlockSpec(memory_space=pl.ANY)
    return pl.pallas_call(
        functools.partial(ffn_weight_kernel, groups, fast, len(after)),
        grid=(n_blocks + 1,),
        in_specs=[wide, wide, const_block(gf.shape), const_block(h2.shape), const_block(gain.shape), anywhere, anywhere]
        + [anywhere] * len(after),
        out_specs=out_specs,
        out_shape=out_shapes,
        scratch_shapes=[
            pltpu.VMEM(mixed.shape, bf16),
            pltpu.VMEM(ga.shape, bf16),
            pltpu.VMEM((model, model), f32),
            pltpu.SemaphoreType.DMA((2,)),
        ],
        compiler_params=params(),
        cost_estimate=cost(4 * batch * rows * hidden * model, 22 * MIB),
    )(act, pre, gf, h2, gain, mixed, ga, *after)


def attention_back_kernel(hd, n_prev, n_later, spots, tile, *refs):
    side_ref, phiq_ref, phik_ref, q_ref, k_ref, v_ref, omega_ref = refs[:7]
    prev_refs = refs[7 : 7 + n_prev]
    later_refs = refs[7 + n_prev : 7 + n_prev + n_later]
    out_ref, scores_scr, back_scr = refs[7 + n_prev + n_later :]
    pair = pl.program_id(0)
    width = 2 * hd
    rows = q_ref.shape[1]
    feats = phiq_ref.shape[-1] // 2
    tiles = rows // tile
    s = hd ** (-0.25)
    low = lanes_of((rows, width)) < hd
    low_tile = low[0:tile]
    inner = lax.rem(lanes_of((rows, width)), hd)
    weights = [feature_weights(omega_ref[odd], odd) for odd in range(2)]
    prev = state_block(prev_refs, False, pair, hd, *spots[0])
    later = state_block(later_refs, True, pair, hd, *spots[1])
    both = jnp.concatenate([later[0][0:width], later[1][0:width]], axis=1)
    side = side_ref[0, 0]
    values = v_ref[0].astype(f32)
    ones = jnp.where(inner < 2, 1.0, 0.0)
    sides = [
        jnp.concatenate([jnp.where(low, values, 0.0), jnp.where(low, ones, 0.0)], axis=1).astype(bf16),
        jnp.concatenate([jnp.where(low, 0.0, values), jnp.where(low, 0.0, ones)], axis=1).astype(bf16),
    ]
    one = jnp.where(inner == 0, 1.0, 0.0).astype(bf16)
    gn_pair = side[:, :width].astype(f32)
    gn_sides = [jnp.where(low, gn_pair, 0.0).astype(bf16), jnp.where(low, 0.0, gn_pair).astype(bf16)]
    causal = causal_tile(tile)

    def to_points(back, point_ref, here):
        along = jnp.where(low_tile, back[0][:, :width], back[1][:, :width])
        total = jnp.where(low_tile, back[0][:, width:], back[1][:, width:])
        return (s * along + (s * s) * point_ref[0, here, :].astype(f32) * total).astype(bf16)

    for at in range(tiles):
        here = slice(at * tile, (at + 1) * tile)
        end = (at + 1) * tile
        back = []
        for odd in range(2):
            cols = slice(odd * feats, (odd + 1) * feats)
            scores_scr[odd, here, 0:end] = masked(
                nt(phiq_ref[0, here, cols], phik_ref[0, 0:end, cols]), causal, at, tile
            )
            made = masked(nt(side[here], sides[odd][0:end]), causal, at, tile)
            back_scr[odd, here, 0:end] = made
            grad_phi = nn(side[here], prev[odd]) + nn(made, phik_ref[0, 0:end, cols])
            grad_proj = (grad_phi * phiq_ref[0, here, cols].astype(f32)).astype(bf16)
            back.append(nn(grad_proj, weights[odd]))
        out_ref[0, 0, here, :] = to_points(back, q_ref, here)
    for at in range(tiles):
        here = slice(at * tile, (at + 1) * tile)
        start = at * tile
        beside = jnp.concatenate([v_ref[0, here, :], one[here]], axis=1)
        grad_v = nt(phik_ref[0, here, :], both)
        back = []
        for odd in range(2):
            cols = slice(odd * feats, (odd + 1) * feats)
            grad_phi = nn(beside, later[odd]) + tn(back_scr[odd, start:, here], phiq_ref[0, start:, cols])
            grad_proj = (grad_phi * phik_ref[0, here, cols].astype(f32)).astype(bf16)
            back.append(nn(grad_proj, weights[odd]))
            grad_v = grad_v + tn(scores_scr[odd, start:, here], gn_sides[odd][start:])
        out_ref[0, 1, here, :] = to_points(back, k_ref, here)
        out_ref[0, 2, here, :] = grad_v.astype(bf16)


def attention_back_call(index, side, phi_q, phi_k, qkv, omega, carried, later, before, after=()):
    batch, pairs, rows, wide = side.shape
    heads, feats, hd = omega.shape
    width = 2 * hd
    model = pairs * width
    tile = min(256, rows)
    phi_spec = pl.BlockSpec((1, rows, 2 * feats), lambda p: (index, 0, p))
    spots = tuple((at * pairs, count) for _, at, count in (carried, later))

    def part(n):
        return pl.BlockSpec((1, rows, width), lambda p: (index, 0, n * pairs + p))

    return stacked_call(
        functools.partial(attention_back_kernel, hd, len(carried[0]), len(later[0]), spots, tile),
        (pairs,),
        [
            pl.BlockSpec((1, 1, rows, wide), lambda p: (index, p, 0, 0)),
            phi_spec,
            phi_spec,
            part(0),
            part(1),
            part(2),
            pl.BlockSpec((2, feats, hd), lambda p: (p, 0, 0)),
        ]
        + state_specs(carried, pairs)
        + state_specs(later, pairs),
        [pl.BlockSpec((1, 3, rows, width), lambda p: (index, 0, 0, p))],
        [jax.ShapeDtypeStruct((batch, 3, rows, model), bf16)],
        (True,),
        before,
        (side, phi_q, phi_k, qkv, qkv, qkv, omega) + tuple(carried[0]) + tuple(later[0]),
        [pltpu.VMEM((2, rows, rows), bf16), pltpu.VMEM((2, rows, rows), bf16)],
        cost(heads * 2 * rows * (rows * 1024 + 6 * 65536), 12 * MIB),
        after,
    )


def qkv_weight_kernel(fast, n_after, *refs):
    h1_ref, grad_ref = refs[:2]
    outs = refs[2 + n_after :]
    batch, rows, model = h1_ref.shape
    total = tn(h1_ref[...].reshape(batch * rows, model), grad_ref[...].reshape(batch * rows, model))
    if not fast:
        outs[0][...] = total
        return
    far_ref, low_ref, high_ref, sum_scr = outs
    sum_scr[...] = total
    piece = model // 8
    for far in range(2):
        for first in range(2):
            for second in range(2):
                owner = row_owner(far, first, second)
                taken = sum_scr[pl.ds(pl.multiple_of(owner * piece, piece), piece), :].astype(bf16)
                if far:
                    far_ref[2 * first + second, 0] = taken
                else:
                    (high_ref if first else low_ref)[second, 0] = taken


def qkv_weight_call(h1, grads, fast, after=()):
    batch, rows, model = h1.shape
    if fast:
        sizes = (4, 2, 2)
        out_specs = [pl.BlockSpec((n, 1, model // 8, model), lambda p: (0, p, 0, 0)) for n in sizes]
        out_shapes = [jax.ShapeDtypeStruct((n, 3, model // 8, model), bf16) for n in sizes]
    else:
        out_specs = [pl.BlockSpec((model, model), lambda p: (0, p))]
        out_shapes = [jax.ShapeDtypeStruct((model, 3 * model), f32)]
    return pl.pallas_call(
        functools.partial(qkv_weight_kernel, fast, len(after)),
        grid=(3,),
        in_specs=[const_block(h1.shape), pl.BlockSpec((batch, 1, rows, model), lambda p: (0, p, 0, 0))]
        + [pl.BlockSpec(memory_space=pl.ANY)] * len(after),
        out_specs=out_specs,
        out_shape=out_shapes,
        scratch_shapes=[pltpu.VMEM((model, model), f32)] if fast else [],
        compiler_params=params(),
        cost_estimate=cost(6 * batch * rows * model * model, 8 * MIB),
    )(h1, grads, *after)


def finish_kernel(groups, *refs):
    grads_ref, w_ref, x_ref, g1_ref, gains_ref, act_ref, x1_ref = refs[:7]
    weights = refs[7 : 7 + groups]
    grad_ref, out_ref, token_ref, down_scr, sems = refs[7 + groups :]
    copies = [
        pltpu.make_async_copy(weights[group].at[:, 1], down_scr.at[group], sems.at[group]) for group in range(groups)
    ]
    for copy in copies:
        copy.start()
    model = x_ref.shape[2]
    grad = nt(grads_ref[0, 0], w_ref[:, :model])
    for part in (1, 2):
        grad = grad + nt(grads_ref[0, part], w_ref[:, part * model : (part + 1) * model])
    xhat, scale = normed(x_ref[0].astype(f32))
    grad_ref[0] = g1_ref[0] + norm_back(grad, xhat, scale, gains_ref[0:1, :])
    token_ref[...] = jnp.zeros_like(token_ref)
    for copy in copies:
        copy.wait()
    down = down_scr[...].reshape(act_ref.shape[2], model)
    out_ref[0] = (x1_ref[0] + nn(act_ref[0], down)).astype(bf16)


def finish_call(index, grads, w_qkv, inputs, g1, gains, act, x1, weights, before, after=()):
    batch, rows, model = inputs.shape
    hidden = act.shape[2]
    groups = len(weights)
    shards, _, unit, _ = weights[0].shape
    one = lambda j: (index, 0, 0)
    whole = pl.BlockSpec((1, rows, model), one)
    return stacked_call(
        functools.partial(finish_kernel, groups),
        (1,),
        [
            pl.BlockSpec((1, 3, rows, model), lambda j: (index, 0, 0, 0)),
            const_block(w_qkv.shape),
            whole,
            whole,
            const_block(gains.shape),
            pl.BlockSpec((1, rows, hidden), one),
            whole,
        ]
        + [pl.BlockSpec(memory_space=pl.ANY)] * groups,
        [whole, whole, const_block((8, 128))],
        [
            jax.ShapeDtypeStruct((batch, rows, model), f32),
            jax.ShapeDtypeStruct((batch, rows, model), bf16),
            jax.ShapeDtypeStruct((8, 128), f32),
        ],
        (True, True, False),
        before,
        (grads, w_qkv, inputs, g1, gains, act, x1) + tuple(weights),
        [pltpu.VMEM((groups, shards, unit, model), bf16), pltpu.SemaphoreType.DMA((groups,))],
        cost(2 * rows * model * (3 * model + hidden), 12 * MIB),
        after,
    )


CORE = (1, 1)
GATHER = ((16, 8), (8, 16), (2, 4), (4, 2))
PLANE = ((4, 2), (2, 4))
LINE = ((16, 8), (8, 16))


def swap(array, masks):
    return lax.ppermute(array, AXES, [(i, i ^ masks[i & 1]) for i in range(32)])


def summed(*arrays):
    return functools.reduce(lambda a, b: a + b, [a.astype(f32) for a in arrays])


def summed_low(*arrays):
    return summed(*arrays).astype(bf16)


def exchange_states(local, backward, fast):
    if not fast:
        everything = lax.all_gather(local, "seq").astype(f32)
        count, place = lax.axis_size("seq"), lax.axis_index("seq")
        at = jnp.arange(count)
        wanted = (at > place) if backward else (at < place)
        total = jnp.sum(jnp.where(wanted[:, None, None, None], everything, 0.0), axis=0)
        return (total.astype(bf16),)
    near = swap(local, CORE)
    core = lax.rem(lax.axis_index("seq"), 2)
    half = local.shape[0] // 2
    mine = jnp.where(core == 0, summed_low(local[:half], near[:half]), summed_low(local[half:], near[half:]))
    from_x = 1 if backward else 0
    pairs = [(i, i ^ 2) for i in range(32) if (i >> 1) & 1 == from_x]
    got = lax.ppermute(mine, AXES, pairs)
    other = swap(got, CORE)
    return near, got, other


def assemble_kernel(near_ref, ahead_ref, far_ref, wqkv_ref, gains_ref, gw_ref, gwout_ref, ggain_ref):
    model = gwout_ref.shape[0]
    rows = model // 8
    for far in range(2):
        for first in range(2):
            for second in range(2):
                owner = row_owner(far, first, second)
                at = pl.ds(pl.multiple_of(owner * rows, rows), rows)
                if far:
                    piece = far_ref[2 * first + second]
                else:
                    piece = (ahead_ref if first else near_ref)[second]
                for part in range(3):
                    gw_ref[at, part * model : (part + 1) * model] = piece[part * rows : (part + 1) * rows].astype(f32)
                gwout_ref[at, :] = piece[3 * rows : 4 * rows].astype(f32)

                @pl.when(owner == 0)
                def _():
                    ggain_ref[1:2, :] = piece[4 * rows : 4 * rows + EXTRA].astype(f32)[0:1]

    ggain_ref[0:1, :] = first_gain(gw_ref, wqkv_ref, gains_ref)


def first_gain(gw_ref, wqkv_ref, gains_ref):
    along = jnp.sum(gw_ref[...] * wqkv_ref[...].astype(f32), axis=1, keepdims=True)
    return jnp.broadcast_to(along, (along.shape[0], 128)).T[0:1, :] / gains_ref[0:1, :]


def assemble_call(near, ahead, far, w_qkv, gains):
    model = w_qkv.shape[0]
    return pl.pallas_call(
        assemble_kernel,
        out_shape=[
            jax.ShapeDtypeStruct(w_qkv.shape, f32),
            jax.ShapeDtypeStruct((model, model), f32),
            jax.ShapeDtypeStruct(gains.shape, f32),
        ],
        compiler_params=params(),
    )(near, ahead, far, w_qkv, gains)


def gains_kernel(gw_ref, gain_ref, wqkv_ref, gains_ref, ggain_ref):
    ggain_ref[0:1, :] = first_gain(gw_ref, wqkv_ref, gains_ref)
    ggain_ref[1:2, :] = gain_ref[0:1, :]


def halves(array):
    cut = array.shape[0] // 2
    return array[:cut], array[cut:]


def gather_shards(shard):
    held = shard[None]
    steps = []
    for masks in GATHER:
        got = swap(held, masks)
        steps.append(got)
        low, held = held, jnp.concatenate([held, got])
    return [swap(low, CORE), swap(got, CORE), low, got], steps


def scatter_sums(far, near, n_shard, n_piece):
    got = swap(far, CORE)
    steps = [got]
    (low, high), (got_low, got_high) = halves(near), halves(got)
    low, high = summed_low(low, got_low), summed_low(high, got_high)
    for at, masks in enumerate(reversed(GATHER)):
        got = swap(high, masks)
        steps.append(got)
        shards = (8 >> at) * n_shard
        shard, shard_got = low[:shards], got[:shards]
        piece, piece_got = low[shards:], got[shards:]
        if at == 3:
            return summed(shard, shard_got), summed_low(piece, piece_got), steps
        (shard_low, shard_high), (got_low, got_high) = halves(shard), halves(shard_got)
        if at == 0:
            (low_p, high_p), (low_g, high_g) = halves(piece), halves(piece_got)
        else:
            low_p, low_g = piece, piece_got
            high_p, high_g = piece, piece_got
        low = summed_low(jnp.concatenate([shard_low, low_p]), jnp.concatenate([got_low, low_g]))
        high = summed_low(jnp.concatenate([shard_high, high_p]), jnp.concatenate([got_high, high_g]))


def on_device(inputs, gains, w_qkv, w_out, ffn_weight, omega, cotangent):
    batch, rows, model = inputs.shape
    heads, feats, hd = omega.shape[1:]
    fast = lax.axis_size("dp") == 8 and lax.axis_size("seq") == 4 and batch == 3
    gain_pair, wqkv, wout, omegas = gains[0], w_qkv[0], w_out[0], omega[0]
    pairs = heads // 2
    unit = ffn_weight.shape[2]

    def only_fast(*arrays):
        return arrays if fast else ()

    if fast:
        weights, steps = gather_shards(ffn_weight[0])
        groups = [(0, 2), (2, 1)]
    else:
        pair = lax.all_gather(ffn_weight[0], AXES, axis=1, tiled=True)
        hidden = pair.shape[1]
        block = min(512, hidden)
        weights = [jnp.swapaxes(pair.reshape(2, hidden // block, block, model), 0, 1)]
        steps = [None] * 4
        groups = [(0, batch)]

    before = None
    carried = []
    for first, members in groups:
        for at in range(members):
            b = first + at
            waits = []
            if fast and b > 0:
                waits.append(steps[b - 1])
            if fast and b == 2:
                waits.append(carried[0][0][0])
            before = features_call(b, at, members, inputs, gain_pair, wqkv, omegas, before, tuple(waits))
        carried.append((exchange_states(before[4], False, fast), 0, members * pairs))
    qkv, phi_q, phi_k, h1 = before[:4]
    before = None
    for (first, members), sums in zip(groups, carried):
        waits = only_fast(steps[2], carried[-1][0][0]) if first == 0 else ()
        before = mix_call(
            first, members, inputs, gain_pair, wout, phi_q, phi_k, qkv, sums, before, hd, waits
        )
    mixed, rden, x1, h2 = before
    carried = [(sums, at, members * pairs) for (first, members), (sums, _, _) in zip(groups, carried) for at in range(members)]

    act, pre, g1, ga, gain, side, gstate = ffn_call(
        h2, cotangent, x1, mixed, rden, phi_q, wout, gain_pair, weights, hd
    )
    sums = exchange_states(gstate, True, fast)
    far, near = ffn_weight_call(act, pre, cotangent, h2, gain, mixed, ga, weights, fast, only_fast(sums[0]))
    if fast:
        shard, piece, steps = scatter_sums(far, near, 2 * unit, model // 8 + EXTRA)
        grad_ffn = shard.reshape(1, 2, unit, model)
    else:
        both = jnp.swapaxes(far, 0, 1).reshape(2, -1, model)
        grad_ffn = lax.psum_scatter(both, AXES, scatter_dimension=1, tiled=True).astype(f32)[None]

    before = None
    for b in range(batch):
        waits = only_fast(steps[b - 1]) if b > 0 else ()
        before = attention_back_call(
            b, side, phi_q, phi_k, qkv, omegas, carried[b], (sums, b, batch * pairs), before, waits
        )
    (grads,) = before
    late = qkv_weight_call(h1, grads, fast, only_fast(steps[2]))

    before = None
    tokens = []
    for b in range(batch):
        before = finish_call(b, grads, wqkv, inputs, g1, gain_pair, act, x1, weights, before)
        tokens.append(before[2][0, 0])
    grad_inputs, outputs = before[:2]
    if fast:
        far, low, high = [a.reshape(a.shape[0], -1, model) for a in late]
        got_low, got_high = halves(swap(far, CORE))
        high = summed_low(high, got_high)
        low = summed_low(low, got_low)
        got = swap(high, PLANE[0])
        high = summed(low[1], got[1])
        low = summed_low(low[0], got[0])
        low = summed_low(low, swap((high + tokens[0]).astype(bf16), PLANE[1]))
        for at, masks in enumerate(LINE):
            low = (summed(low, swap(low, masks)) + tokens[1 + at]).astype(bf16)
        low = jnp.concatenate([low, piece])
        near = jnp.stack([low, swap(low, PLANE[1])])
        ahead = swap(near, PLANE[0])
        far = swap(jnp.concatenate([near, ahead]), CORE)
        grad_wqkv, grad_wout, grad_gains = assemble_call(near, ahead, far, wqkv, gain_pair)
    else:
        grad_wqkv, grad_wout, gain = lax.psum((late[0], near, gain), AXES)
        grad_gains = pl.pallas_call(
            gains_kernel,
            out_shape=jax.ShapeDtypeStruct(gain_pair.shape, f32),
            compiler_params=params(),
        )(grad_wqkv, gain, wqkv, gain_pair)
    return (outputs, grad_inputs, grad_gains[None], grad_wqkv[None], grad_wout[None], grad_ffn)


def solution(mesh):
    in_specs = (
        P("dp", "seq", None),
        P(),
        P(),
        P(),
        P(None, None, ("dp", "seq"), None),
        P(),
        P("dp", "seq", None),
    )
    out_specs = (
        P("dp", "seq", None),
        P("dp", "seq", None),
        P(),
        P(),
        P(),
        P(None, None, ("dp", "seq"), None),
    )
    return jax.shard_map(
        on_device, mesh=mesh, in_specs=in_specs, out_specs=out_specs, check_vma=False
    )
```

time: 399 us -> 290 us (0.73); the launches traced: 391 us -> 286 us
  starting transfers between devices: 119 us -> 36.8 us
  waiting for transfers between devices: 73.7 us -> 57.3 us
  Pallas kernels: 180 us -> 166 us
  local copies, waits for them, and re-layouts: 5.02 us -> 13.7 us
    ppermute x100 -> x25, starting transfers between devices: 104 us -> 28.1 us  [swap(): return lax.ppermute(array, AXES, [(i, i ^ masks[i & 1]) for i in range(32)])]
    ppermute x100 -> x25, waiting for transfers between devices: 66.3 us -> 41.3 us  [swap(): return lax.ppermute(array, AXES, [(i, i ^ masks[i & 1]) for i in range(32)])]
    ppermute x6 -> x3, waiting for transfers between devices: 7.37 us -> 16 us  [exchange_states(): got = lax.ppermute(mine, AXES, pairs)]
    pallas_call x4 -> x3, Pallas kernels: 54.9 us -> 47.9 us  [the longest x1 27.4 us: ffn_call(): pl.pallas_call(functools.partial(ffn_kernel, groups, batch, hd), grid=(n_...]
    unnamed x96 -> x62, local copies, waits for them, and re-layouts: 3 us -> 9.82 us
    pallas_call x12 -> x11, Pallas kernels: 120 us -> 114 us  [stacked_call(): pl.pallas_call(body, grid=grid, in_specs=list(in_specs) + [pl.BlockSpec(m...]
    ppermute x6 -> x3, starting transfers between devices: 14.4 us -> 8.66 us  [exchange_states(): got = lax.ppermute(mine, AXES, pairs)]
  transfers between devices with their start and end apart: 106 -> 28, of which waited for: 38 -> 12; matrix products, arithmetic and copies ran while one was open for 3% -> 5% of each run, Pallas kernels for 25% -> 40%
where the time goes in v2:
time: 290 us; the launch traced here: 286 us
  Pallas kernels  166 us (57%)
  waiting for transfers between devices  57.3 us (20%)
  starting transfers between devices  36.8 us (13%)
  local copies, waits for them, and re-layouts  13.7 us (5%)
  other arithmetic  11.3 us (4%)
    pallas_call x11, Pallas kernels, stacked_call(): pl.pallas_call(body, grid=grid, in_specs=list(in_specs) + [pl.BlockSpec(m...  114 us
    ppermute x25, waiting for transfers between devices, swap(): return lax.ppermute(array, AXES, [(i, i ^ masks[i & 1]) for i in range(32)])  41.3 us
    ppermute x25, starting transfers between devices, swap(): return lax.ppermute(array, AXES, [(i, i ^ masks[i & 1]) for i in range(32)])  28.1 us
    pallas_call x1, Pallas kernels, ffn_call(): pl.pallas_call(functools.partial(ffn_kernel, groups, batch, hd), grid=(n_...  27.4 us
    ppermute x3, waiting for transfers between devices, exchange_states(): got = lax.ppermute(mine, AXES, pairs)  16 us
    pallas_call x1, Pallas kernels, ffn_weight_call(): pl.pallas_call(functools.partial(ffn_weight_kernel, groups, fast, len(aft...  14.1 us
    unnamed x62, local copies, waits for them, and re-layouts  9.82 us
    ppermute x3, starting transfers between devices, exchange_states(): got = lax.ppermute(mine, AXES, pairs)  8.66 us
  transfers between devices with their start and end apart: 28, of which 12 were waited for; matrix products, arithmetic and copies ran while one was open for 5% of the time, Pallas kernels for 40%

profile of v2, /device:TPU:0, one launch (start us, length us, event | category | flops | bytes accessed | tf_op | source)
XLA Modules:
  0.0 286.3 jit_solution(8584832636602622210)
XLA Ops:
  0.6 4.1 %collective-permute-start = (bf16[1,2,64,512]{3,2,1,0:T(8,128)(2,1)}, bf16[1,2,64,512]{3,2,1,0:T(8,128)(2,1)S(1)}, u32[]{:S(2)}, u32[]{:S(2)}) collective-permute-start(bf16[1,2,64,512]{3,2,1,0:T(8,128)(2,1)} %param.11), channel_id=1, source_target_pairs={{0,16},{1,9},{2,18},{3,11},{4,20},{5,13},{6,22},{7,15},{8,24},{9,1... | collective-permute-start | bytes 393224 | tf_op jit(solution)/shard_map/ppermute | solution.py:798
  4.7 3.2 %collective-permute-done.refs_4_ = bf16[1,2,64,512]{3,2,1,0:T(8,128)(2,1)S(1)} collective-permute-done((bf16[1,2,64,512]{3,2,1,0:T(8,128)(2,1)}, bf16[1,2,64,512]{3,2,1,0:T(8,128)(2,1)S(1)}, u32[]{:S(2)}, u32[]{:S(2)}) %collective-permute-start) | collective-permute-done | bytes 131104 | tf_op jit(solution)/shard_map/ppermute | solution.py:798
  8.0 1.0 pad_maximum_fusion.4
  8.9 2.5 collective-permute-start.1
  11.4 1.9 copy.32
  13.4 7.7 %shard_map.118 = (bf16[3,512,1536]{2,1,0:T(8,128)(2,1)}, bf16[3,512,2048]{2,1,0:T(8,128)(2,1)}, bf16[3,512,2048]{2,1,0:T(8,128)(2,1)}, bf16[3,512,512]{2,1,0:T(8,128)(2,1)}, bf16[8,144,256]{2,1,0:T(8,128)(2,1)}) custom-call(bf16[3,512,512]{2,1,0:T(8,128)(2,1)} %refs_2_.7, f32[2,512]{1,0:T(2,128)} %bitcast.47, bf16[512,1536]{1,0:T(8,128)(2,1)} %bitcast.28, ...), custom_call_target="tpu_custom_call" | custom-call | flops 1879048192 | bytes 9437184 | tf_op jit(solution)/shard_map/pallas_call | solution.py:60
  21.2 1.6 collective-permute-start.8
  22.8 8.1 %shard_map.119 = (bf16[3,512,1536]{2,1,0:T(8,128)(2,1)}, bf16[3,512,2048]{2,1,0:T(8,128)(2,1)}, bf16[3,512,2048]{2,1,0:T(8,128)(2,1)}, bf16[3,512,512]{2,1,0:T(8,128)(2,1)}, bf16[8,144,256]{2,1,0:T(8,128)(2,1)}) custom-call(bf16[3,512,512]{2,1,0:T(8,128)(2,1)} %refs_2_.7, ...), custom_call_target="tpu_custom_call", output_to_operand_aliasing={{0}: (5, {}), {1}: (6, {}), {2}: (7, {}), {3}: (8, {}), {4}... | custom-call | flops 1879048192 | bytes 9437184 | tf_op jit(solution)/shard_map/pallas_call | solution.py:60
  31.8 1.6 collective-permute-start.10
  33.6 2.9 collective-permute-start.6
  36.4 8.1 %shard_map.120 = (bf16[3,512,1536]{2,1,0:T(8,128)(2,1)}, bf16[3,512,2048]{2,1,0:T(8,128)(2,1)}, bf16[3,512,2048]{2,1,0:T(8,128)(2,1)}, bf16[3,512,512]{2,1,0:T(8,128)(2,1)}, bf16[4,144,256]{2,1,0:T(8,128)(2,1)}) custom-call(bf16[3,512,512]{2,1,0:T(8,128)(2,1)} %refs_2_.7, ...), custom_call_target="tpu_custom_call", output_to_operand_aliasing={{0}: (6, {}), {1}: (7, {}), {2}: (8, {}), {3}: (9, {})} | custom-call | flops 1879048192 | bytes 9437184 | tf_op jit(solution)/shard_map/pallas_call | solution.py:60
  45.1 5.6 %collective-permute-start.7 = (bf16[4,144,256]{2,1,0:T(8,128)(2,1)S(1)}, bf16[4,144,256]{2,1,0:T(8,128)(2,1)S(1)}, u32[]{:S(2)}, u32[]{:S(2)}) collective-permute-start(bf16[4,144,256]{2,1,0:T(8,128)(2,1)S(1)} %collective-permute-done.6.refs_7_.refs_8_), channel_id=1, source_target_pairs={{0,1},{1,0},{2,3},{3,2},{4,5},{5,4},{6,7},{7,6},{8,9},{9,8},{10,11... | collective-permute-start | bytes 884744 | tf_op jit(solution)/shard_map/ppermute | solution.py:798
  50.8 1.4 fusion.7
  52.2 4.3 %collective-permute-start.4 = (bf16[2,144,256]{2,1,0:T(8,128)(2,1)S(1)}, bf16[2,144,256]{2,1,0:T(8,128)(2,1)S(1)}, u32[]{:S(2)}, u32[]{:S(2)}) collective-permute-start(bf16[2,144,256]{2,1,0:T(8,128)(2,1)S(1)} %fusion.7), channel_id=1, source_target_pairs={{0,2},{1,3},{4,6},{5,7},{8,10},{9,11},{12,14},{13,15},{16,18},{17,... | collective-permute-start | bytes 442376 | tf_op jit(solution)/shard_map/ppermute | solution.py:823
  56.5 3.3 %collective-permute-done.4.refs_7_.refs_8_ = bf16[2,144,256]{2,1,0:T(8,128)(2,1)S(1)} collective-permute-done((bf16[2,144,256]{2,1,0:T(8,128)(2,1)S(1)}, bf16[2,144,256]{2,1,0:T(8,128)(2,1)S(1)}, u32[]{:S(2)}, u32[]{:S(2)}) %collective-permute-start.4) | collective-permute-done | bytes 147488 | tf_op jit(solution)/shard_map/ppermute | solution.py:823
  60.5 14.2 %shard_map.121 = (bf16[3,512,512]{2,1,0:T(8,128)(2,1)}, f32[3,512,512]{2,1,0:T(8,128)}, f32[3,512,512]{2,1,0:T(8,128)}, bf16[3,512,512]{2,1,0:T(8,128)(2,1)}) custom-call(bf16[3,512,512]{2,1,0:T(8,128)(2,1)} %refs_2_.7, f32[2,512]{1,0:T(2,128)} %bitcast.50, bf16[512,512]{1,0:T(8,128)(2,1)} %bitcast.41, ...), custom_call_target="tpu_custom_call" | custom-call | flops 4831838208 | bytes 18874368 | tf_op jit(solution)/shard_map/pallas_call | solution.py:60
  75.4 8.2 %shard_map.122 = (bf16[3,512,512]{2,1,0:T(8,128)(2,1)}, f32[3,512,512]{2,1,0:T(8,128)}, f32[3,512,512]{2,1,0:T(8,128)}, bf16[3,512,512]{2,1,0:T(8,128)(2,1)}) custom-call(bf16[3,512,512]{2,1,0:T(8,128)(2,1)} %refs_2_.7, f32[2,512]{1,0:T(2,128)} %bitcast.51, ...), custom_call_target="tpu_custom_call", output_to_operand_aliasing={{0}: (9, {}), {1}: (10, {}), {2}: (11, {}), {3}: (12, {})} | custom-call | flops 2415919104 | bytes 9437184 | tf_op jit(solution)/shard_map/pallas_call | solution.py:60
  83.6 0.9 copy-done.5
  85.0 27.4 %shard_map.123 = (bf16[3,512,2048]{2,1,0:T(8,128)(2,1)}, bf16[3,512,2048]{2,1,0:T(8,128)(2,1)}, f32[3,512,512]{2,1,0:T(8,128)}, bf16[3,512,512]{2,1,0:T(8,128)(2...) custom-call(bf16[3,512,512]{2,1,0:T(8,128)(2,1)} %get-tuple-element.71.refs_0_.refs_3_, ...), custom_call_target="tpu_custom_call" | custom-call | flops 9663676416 | bytes 31457280 | tf_op jit(solution)/shard_map/pallas_call | solution.py:428
  112.9 2.3 collective-permute-done.12.refs_7_.refs_10_
  116.1 14.1 %shard_map.124 = (bf16[2368,512]{1,0:T(8,128)(2,1)}, bf16[2368,512]{1,0:T(8,128)(2,1)}) custom-call(bf16[3,512,2048]{2,1,0:T(8,128)(2,1)} %get-tuple-element.77.refs_0_.refs_5_, bf16[3,512,2048]{2,1,0:T(8,128)(2,1)} %get-tuple-element.78.refs_1_, bf16[3,512,512]{2,1,0:T(8,128)(2,1)} %refs_2_.4, bf16[3,512,512]{2,1,0:T(8,128)(2,1)} %get-tuple-element.71.refs_0_.refs_3_, ...), custom_call_target="tpu_custom_call" | custom-call | flops 6442450944 | bytes 23068672 | tf_op jit(solution)/shard_map/pallas_call | solution.py:569
  130.6 1.4 fusion.2
  132.0 1.5 collective-permute-start.13
  133.5 12.7 %collective-permute-done.13.refs_11_ = bf16[6,144,256]{2,1,0:T(8,128)(2,1)S(1)} collective-permute-done((bf16[6,144,256]{2,1,0:T(8,128)(2,1)S(1)}, bf16[6,144,256]{2,1,0:T(8,128)(2,1)S(1)}, u32[]{:S(2)}, u32[]{:S(2)}) %collective-permute-start.13) | collective-permute-done | bytes 442400 | tf_op jit(solution)/shard_map/ppermute | solution.py:823
  146.2 3.4 %add_convert_fusion = (bf16[1184,512]{1,0:T(8,128)(2,1)S(1)}, bf16[1184,512]{1,0:T(8,128)(2,1)S(1)}) fusion(bf16[2368,512]{1,0:T(8,128)(2,1)S(1)} %collective-permute-done.15.refs_13_, bf16[2368,512]{1,0:T(8,128)(2,1)} %get-tuple-element.81), kind=kLoop, calls=%fused_computation | loop fusion | flops 4849664 | bytes 7274496 | tf_op jit(solution)/shard_map/convert_element_type | solution.py:806
  149.6 1.6 collective-permute-start.16
  152.0 15.6 %shard_map.125.refs_14_ = bf16[3,3,512,512]{3,2,1,0:T(8,128)(2,1)} custom-call(bf16[3,4,512,256]{3,2,1,0:T(8,128)(2,1)} %get-tuple-element.75.refs_0_, bf16[3,512,2048]{2,1,0:T(8,128)(2,1)} %get-tuple-element.63.refs_3_.refs_5_.refs_1_, bf16[3,512,2048]{2,1,0:T(8,128)(2,1)} %get-tuple-element.64.refs_4_.refs_2_, ...), custom_call_target="tpu_custom_call" | custom-call | flops 7516192768 | bytes 12582912 | tf_op jit(solution)/shard_map/pallas_call | solution.py:60
  167.7 15.6 %shard_map.126.refs_14_ = bf16[3,3,512,512]{3,2,1,0:T(8,128)(2,1)} custom-call(bf16[3,4,512,256]{3,2,1,0:T(8,128)(2,1)} %get-tuple-element.75.refs_0_, bf16[3,512,2048]{2,1,0:T(8,128)(2,1)} %get-tuple-element.63.refs_3_.refs_5_.refs_1_, bf16[3,512,2048]{2,1,0:T(8,128)(2,1)} %get-tuple-element.64.refs_4_.refs_2_, ...), custom_call_target="tpu_custom_call", output_to_operand_aliasing={{}: (14, {})} | custom-call | flops 7516192768 | bytes 12582912 | tf_op jit(solution)/shard_map/pallas_call | solution.py:60
  184.3 15.6 %shard_map.127.refs_0_.refs_1_ = bf16[3,3,512,512]{3,2,1,0:T(8,128)(2,1)} custom-call(bf16[3,4,512,256]{3,2,1,0:T(8,128)(2,1)} %get-tuple-element.75.refs_0_, bf16[3,512,2048]{2,1,0:T(8,128)(2,1)} %get-tuple-element.63.refs_3_.refs_5_.refs_1_, bf16[3,512,2048]{2,1,0:T(8,128)(2,1)} %get-tuple-element.64.refs_4_.refs_2_, ...), custom_call_target="tpu_custom_call", output_to_operand_aliasing={{}: (14, {})} | custom-call | flops 7516192768 | bytes 12582912 | tf_op jit(solution)/shard_map/pallas_call | solution.py:60
  200.8 6.4 %shard_map.131 = (bf16[4,3,64,512]{3,2,1,0:T(8,128)(2,1)}, bf16[2,3,64,512]{3,2,1,0:T(8,128)(2,1)}, bf16[2,3,64,512]{3,2,1,0:T(8,128)(2,1)}) custom-call(bf16[3,512,512]{2,1,0:T(8,128)(2,1)} %get-tuple-element.90.refs_0_, bf16[3,3,512,512]{3,2,1,0:T(8,128)(2,1)} %shard_map.127.refs_0_.refs_1_, bf16[592,512]{1,0:T(8,128)(2,1)} %copy-done.23), custom_call_target="tpu_custom_call" | custom-call | flops 2415919104 | bytes 8388608 | tf_op jit(solution)/shard_map/pallas_call | solution.py:721
  207.2 6.9 %shard_map.128 = (f32[3,512,512]{2,1,0:T(8,128)}, bf16[3,512,512]{2,1,0:T(8,128)(2,1)}, f32[8,128]{1,0:T(8,128)}) custom-call(bf16[3,3,512,512]{3,2,1,0:T(8,128)(2,1)} %shard_map.127.refs_0_.refs_1_, bf16[512,1536]{1,0:T(8,128)(2,1)} %bitcast.31, bf16[3,512,512]{2,1,0:T(8,128)(2,1)} %refs_2_.7, f32[3,512,512]{2,1,0:T(8,128)} %get-tuple-element.83.refs_3_, ...), custom_call_target="tpu_custom_call" | custom-call | flops 1879048192 | bytes 12582912 | tf_op jit(solution)/shard_map/pallas_call | solution.py:60
  214.1 6.9 %shard_map.129 = (f32[3,512,512]{2,1,0:T(8,128)}, bf16[3,512,512]{2,1,0:T(8,128)(2,1)}, f32[8,128]{1,0:T(8,128)}) custom-call(bf16[3,3,512,512]{3,2,1,0:T(8,128)(2,1)} %shard_map.127.refs_0_.refs_1_, bf16[512,1536]{1,0:T(8,128)(2,1)} %bitcast.32, bf16[3,512,512]{2,1,0:T(8,128)(2,1)} %refs_2_.7, ...), custom_call_target="tpu_custom_call", output_to_operand_aliasing={{0}: (11, {}), {1}: (12, {})} | custom-call | flops 1879048192 | bytes 12582912 | tf_op jit(solution)/shard_map/pallas_call | solution.py:60
  221.0 6.9 %shard_map.130 = (f32[3,512,512]{2,1,0:T(8,128)}, bf16[3,512,512]{2,1,0:T(8,128)(2,1)}, f32[8,128]{1,0:T(8,128)}) custom-call(bf16[3,3,512,512]{3,2,1,0:T(8,128)(2,1)} %shard_map.127.refs_0_.refs_1_, bf16[512,1536]{1,0:T(8,128)(2,1)} %bitcast.33, bf16[3,512,512]{2,1,0:T(8,128)(2,1)} %refs_2_.7, ...), custom_call_target="tpu_custom_call", output_to_operand_aliasing={{0}: (11, {}), {1}: (12, {})} | custom-call | flops 1879048192 | bytes 12582912 | tf_op jit(solution)/shard_map/pallas_call | solution.py:60
  229.1 1.2 slice.193
  230.3 1.2 slice.194
  231.5 1.2 slice.195
  232.9 3.2 %collective-permute-done.19 = bf16[2,192,512]{2,1,0:T(8,128)(2,1)S(1)} collective-permute-done((bf16[2,192,512]{2,1,0:T(8,128)(2,1)S(1)}, bf16[2,192,512]{2,1,0:T(8,128)(2,1)S(1)}, u32[]{:S(2)}, u32[]{:S(2)}) %collective-permute-start.19) | collective-permute-done | bytes 393248 | tf_op jit(solution)/shard_map/ppermute | solution.py:798
  236.8 2.0 collective-permute-start.20
  239.0 3.6 %collective-permute-done.20 = bf16[192,512]{1,0:T(8,128)(2,1)S(1)} collective-permute-done((bf16[192,512]{1,0:T(8,128)(2,1)S(1)}, bf16[192,512]{1,0:T(8,128)(2,1)S(1)}, u32[]{:S(2)}, u32[]{:S(2)}) %collective-permute-start.20) | collective-permute-done | bytes 196640 | tf_op jit(solution)/shard_map/ppermute | solution.py:798
  242.7 3.3 %collective-permute-start.21 = (bf16[192,512]{1,0:T(8,128)(2,1)S(1)}, bf16[192,512]{1,0:T(8,128)(2,1)S(1)}, u32[]{:S(2)}, u32[]{:S(2)}) collective-permute-start(bf16[192,512]{1,0:T(8,128)(2,1)S(1)} %fusion.3), channel_id=1, source_target_pairs={{0,16},{1,9},{2,18},{3,11},{4,20},{5,13},{6,22},{7,15},{8,24},{9,1... | collective-permute-start | bytes 589832 | tf_op jit(solution)/shard_map/ppermute | solution.py:798
  246.2 5.6 %collective-permute-done.21 = bf16[192,512]{1,0:T(8,128)(2,1)S(1)} collective-permute-done((bf16[192,512]{1,0:T(8,128)(2,1)S(1)}, bf16[192,512]{1,0:T(8,128)(2,1)S(1)}, u32[]{:S(2)}, u32[]{:S(2)}) %collective-permute-start.21) | collective-permute-done | bytes 196640 | tf_op jit(solution)/shard_map/ppermute | solution.py:798
  252.5 7.0 %collective-permute-done.24 = bf16[208,512]{1,0:T(8,128)(2,1)S(1)} collective-permute-done((bf16[208,512]{1,0:T(8,128)(2,1)S(1)}, bf16[208,512]{1,0:T(8,128)(2,1)S(1)}, u32[]{:S(2)}, u32[]{:S(2)}) %collective-permute-start.24) | collective-permute-done | bytes 213024 | tf_op jit(solution)/shard_map/ppermute | solution.py:798
  261.2 2.6 collective-permute-start.25
  263.8 4.5 %collective-permute-done.25 = bf16[272,512]{1,0:T(8,128)(2,1)S(1)} collective-permute-done((bf16[272,512]{1,0:T(8,128)(2,1)S(1)}, bf16[272,512]{1,0:T(8,128)(2,1)S(1)}, u32[]{:S(2)}, u32[]{:S(2)}) %collective-permute-start.25) | collective-permute-done | bytes 278560 | tf_op jit(solution)/shard_map/ppermute | solution.py:798
  268.9 9.0 %collective-permute-done.26.ahead_ref = bf16[2,272,512]{2,1,0:T(8,128)(2,1)S(1)} collective-permute-done((bf16[2,272,512]{2,1,0:T(8,128)(2,1)S(1)}, bf16[2,272,512]{2,1,0:T(8,128)(2,1)S(1)}, u32[]{:S(2)}, u32[]{:S(2)}) %collective-permute-start.26) | collective-permute-done | bytes 557088 | tf_op jit(solution)/shard_map/ppermute | solution.py:798
  278.9 2.0 collective-permute-done.27.far_ref
  280.9 1.0 copy-done.21
  281.9 4.4 %shard_map.132 = (f32[512,1536]{1,0:T(8,128)}, f32[512,512]{1,0:T(8,128)}, f32[2,512]{1,0:T(2,128)}) custom-call(bf16[2,272,512]{2,1,0:T(8,128)(2,1)} %copy-done.15, bf16[2,272,512]{2,1,0:T(8,128)(2,1)} %copy-done.16, bf16[4,272,512]{2,1,0:T(8,128)(2,1)} %copy-done.21, bf16[512,1536]{1,0:T(8,128)(2,1)} %bitcast.34, f32[2,512]{1,0:T(2,128)} %bitcast.56), custom_call_target="tpu_custom_call" | custom-call | tf_op jit(solution)/shard_map/pallas_call | solution.py:858
  (122 shorter events, 14.6 us)
Async XLA Ops:
  0.6 7.3 %collective-permute-start = (bf16[1,2,64,512]{3,2,1,0:T(8,128)(2,1)}, bf16[1,2,64,512]{3,2,1,0:T(8,128)(2,1)S(1)}, u32[]{:S(2)}, u32[]{:S(2)}) collective-permute-start(bf16[1,2,64,512]{3,2,1,0:T(8,128)(2,1)} %param.11), channel_id=1, source_target_pairs={{0,16},{1,9},{2,18},{3,11},{4,20},{5,13},{6,22},{7,15},{8,24},{9,1... | collective-permute-start | bytes 393224 | tf_op jit(solution)/shard_map/ppermute | solution.py:798
  7.9 13.1 %copy-start.17 = (bf16[1,2,64,512]{3,2,1,0:T(8,128)(2,1)}, bf16[1,2,64,512]{3,2,1,0:T(8,128)(2,1)S(1)}, u32[]{:S(2)}) copy-start(bf16[1,2,64,512]{3,2,1,0:T(8,128)(2,1)S(1)} %collective-permute-done.refs_4_) | copy-start | bytes 393220
  8.9 12.2 %collective-permute-start.1 = (bf16[2,2,64,512]{3,2,1,0:T(8,128)(2,1)S(1)}, bf16[2,2,64,512]{3,2,1,0:T(8,128)(2,1)S(1)}, u32[]{:S(2)}, u32[]{:S(2)}) collective-permute-start(bf16[2,2,64,512]{3,2,1,0:T(8,128)(2,1)S(1)} %pad_maximum_fusion.4), channel_id=1, source_target_pairs={{0,8},{1,17},{2,10},{3,19},{4,12},{5,21},{6,14},{7,23},{8,0},{9,25... | collective-permute-start | bytes 786440 | tf_op jit(solution)/shard_map/ppermute | solution.py:798
  13.4 7.7 %copy-start.20 = (bf16[1,2,64,512]{3,2,1,0:T(8,128)(2,1)S(1)}, bf16[1,2,64,512]{3,2,1,0:T(8,128)(2,1)}, u32[]{:S(2)}) copy-start(bf16[1,2,64,512]{3,2,1,0:T(8,128)(2,1)} %param.11) | copy-start | bytes 393220
  21.1 9.8 %copy-start.13 = (bf16[2,2,64,512]{3,2,1,0:T(8,128)(2,1)}, bf16[2,2,64,512]{3,2,1,0:T(8,128)(2,1)S(1)}, u32[]{:S(2)}) copy-start(bf16[2,2,64,512]{3,2,1,0:T(8,128)(2,1)S(1)} %collective-permute-done.1.refs_4_) | copy-start | bytes 786436
  21.2 9.8 %collective-permute-start.8 = (bf16[4,2,64,512]{3,2,1,0:T(8,128)(2,1)S(1)}, bf16[4,2,64,512]{3,2,1,0:T(8,128)(2,1)S(1)}, u32[]{:S(2)}, u32[]{:S(2)}) collective-permute-start(bf16[4,2,64,512]{3,2,1,0:T(8,128)(2,1)S(1)} %pad_maximum_fusion.2), channel_id=1, source_target_pairs={{0,2},{1,5},{2,0},{3,7},{4,6},{5,1},{6,4},{7,3},{8,10},{9,13},{10,... | collective-permute-start | bytes 1572872 | tf_op jit(solution)/shard_map/ppermute | solution.py:798
  22.7 8.2 %copy-start.18 = (bf16[1,2,64,512]{3,2,1,0:T(8,128)(2,1)S(1)}, bf16[1,2,64,512]{3,2,1,0:T(8,128)(2,1)}, u32[]{:S(2)}) copy-start(bf16[1,2,64,512]{3,2,1,0:T(8,128)(2,1)} %copy-done.17) | copy-start | bytes 393220
  30.8 2.6 copy-start.14
  30.8 2.6 collective-permute-start.2
  31.8 12.8 %copy-start.2 = (bf16[8,2,64,512]{3,2,1,0:T(8,128)(2,1)}, bf16[8,2,64,512]{3,2,1,0:T(8,128)(2,1)S(1)}, u32[]{:S(2)}) copy-start(bf16[8,2,64,512]{3,2,1,0:T(8,128)(2,1)S(1)} %constant_dynamic-update-slice_fusion.refs_10_.refs_9_) | copy-start | bytes 3145732
  31.8 18.9 %collective-permute-start.10 = (bf16[8,2,64,512]{3,2,1,0:T(8,128)(2,1)S(1)}, bf16[8,2,64,512]{3,2,1,0:T(8,128)(2,1)S(1)}, u32[]{:S(2)}, u32[]{:S(2)}) collective-permute-start(bf16[8,2,64,512]{3,2,1,0:T(8,128)(2,1)S(1)} %constant_dynamic-update-slice_fusion.refs_10_.refs_9_), channel_id=1, source_target_pairs={{0,4},{1,3},{2,6},{3,1},{4,0},{5,7},{6,2},{7,5},{8,12},{9,11},{10,... | collective-permute-start | bytes 3145736 | tf_op jit(solution)/shard_map/ppermute | solution.py:798
  33.4 3.0 %copy-start = (bf16[8,144,256]{2,1,0:T(8,128)(2,1)}, bf16[8,144,256]{2,1,0:T(8,128)(2,1)S(1)}, u32[]{:S(2)}) copy-start(bf16[8,144,256]{2,1,0:T(8,128)(2,1)S(1)} %collective-permute-done.2.refs_5_.refs_6_.refs_7_) | copy-start | bytes 1769476
  33.6 11.5 %collective-permute-start.6 = (bf16[4,144,256]{2,1,0:T(8,128)(2,1)S(1)}, bf16[4,144,256]{2,1,0:T(8,128)(2,1)S(1)}, u32[]{:S(2)}, u32[]{:S(2)}) collective-permute-start(bf16[4,144,256]{2,1,0:T(8,128)(2,1)S(1)} %fusion.4), channel_id=1, source_target_pairs={{0,2},{1,3},{4,6},{5,7},{8,10},{9,11},{12,14},{13,15},{16,18},{17,... | collective-permute-start | bytes 884744 | tf_op jit(solution)/shard_map/ppermute | solution.py:823
  44.5 6.3 %collective-permute-start.3 = (bf16[4,144,256]{2,1,0:T(8,128)(2,1)}, bf16[4,144,256]{2,1,0:T(8,128)(2,1)S(1)}, u32[]{:S(2)}, u32[]{:S(2)}) collective-permute-start(bf16[4,144,256]{2,1,0:T(8,128)(2,1)} %get-tuple-element.66), channel_id=1, source_target_pairs={{0,1},{1,0},{2,3},{3,2},{4,5},{5,4},{6,7},{7,6},{8,9},{9,8},{10,11... | collective-permute-start | bytes 884744 | tf_op jit(solution)/shard_map/ppermute | solution.py:798
  44.6 39.0 %collective-permute-start.9 = (bf16[8,2,64,512]{3,2,1,0:T(8,128)(2,1)S(1)}, bf16[8,2,64,512]{3,2,1,0:T(8,128)(2,1)S(1)}, u32[]{:S(2)}, u32[]{:S(2)}) collective-permute-start(bf16[8,2,64,512]{3,2,1,0:T(8,128)(2,1)S(1)} %constant_dynamic-update-slice_fusion.refs_10_.refs_9_), channel_id=1, source_target_pairs={{0,1},{1,0},{2,3},{3,2},{4,5},{5,4},{6,7},{7,6},{8,9},{9,8},{10,11... | collective-permute-start | bytes 3145736 | tf_op jit(solution)/shard_map/ppermute | solution.py:798
  45.1 14.7 %copy-start.11 = (bf16[4,144,256]{2,1,0:T(8,128)(2,1)}, bf16[4,144,256]{2,1,0:T(8,128)(2,1)S(1)}, u32[]{:S(2)}) copy-start(bf16[4,144,256]{2,1,0:T(8,128)(2,1)S(1)} %collective-permute-done.6.refs_7_.refs_8_) | copy-start | bytes 884740
  45.1 14.7 %collective-permute-start.7 = (bf16[4,144,256]{2,1,0:T(8,128)(2,1)S(1)}, bf16[4,144,256]{2,1,0:T(8,128)(2,1)S(1)}, u32[]{:S(2)}, u32[]{:S(2)}) collective-permute-start(bf16[4,144,256]{2,1,0:T(8,128)(2,1)S(1)} %collective-permute-done.6.refs_7_.refs_8_), channel_id=1, source_target_pairs={{0,1},{1,0},{2,3},{3,2},{4,5},{5,4},{6,7},{7,6},{8,9},{9,8},{10,11... | collective-permute-start | bytes 884744 | tf_op jit(solution)/shard_map/ppermute | solution.py:798
  50.7 24.0 %copy-start.4 = (bf16[8,2,64,512]{3,2,1,0:T(8,128)(2,1)}, bf16[8,2,64,512]{3,2,1,0:T(8,128)(2,1)S(1)}, u32[]{:S(2)}) copy-start(bf16[8,2,64,512]{3,2,1,0:T(8,128)(2,1)S(1)} %collective-permute-done.10.refs_11_.refs_10_) | copy-start | bytes 3145732
  50.7 32.9 %collective-permute-start.11 = (bf16[8,2,64,512]{3,2,1,0:T(8,128)(2,1)S(1)}, bf16[8,2,64,512]{3,2,1,0:T(8,128)(2,1)S(1)}, u32[]{:S(2)}, u32[]{:S(2)}) collective-permute-start(bf16[8,2,64,512]{3,2,1,0:T(8,128)(2,1)S(1)} %collective-permute-done.10.refs_11_.refs_10_), channel_id=1, source_target_pairs={{0,1},{1,0},{2,3},{3,2},{4,5},{5,4},{6,7},{7,6},{8,9},{9,8},{10,11... | collective-permute-start | bytes 3145736 | tf_op jit(solution)/shard_map/ppermute | solution.py:798
  50.8 9.0 %copy-start.8 = (bf16[4,144,256]{2,1,0:T(8,128)(2,1)}, bf16[4,144,256]{2,1,0:T(8,128)(2,1)S(1)}, u32[]{:S(2)}) copy-start(bf16[4,144,256]{2,1,0:T(8,128)(2,1)S(1)} %collective-permute-done.3.refs_10_.refs_6_.refs_7_) | copy-start | bytes 884740
  52.2 7.6 %collective-permute-start.4 = (bf16[2,144,256]{2,1,0:T(8,128)(2,1)S(1)}, bf16[2,144,256]{2,1,0:T(8,128)(2,1)S(1)}, u32[]{:S(2)}, u32[]{:S(2)}) collective-permute-start(bf16[2,144,256]{2,1,0:T(8,128)(2,1)S(1)} %fusion.7), channel_id=1, source_target_pairs={{0,2},{1,3},{4,6},{5,7},{8,10},{9,11},{12,14},{13,15},{16,18},{17,... | collective-permute-start | bytes 442376 | tf_op jit(solution)/shard_map/ppermute | solution.py:823
  59.7 15.0 %copy-start.25 = (bf16[2,144,256]{2,1,0:T(8,128)(2,1)}, bf16[2,144,256]{2,1,0:T(8,128)(2,1)S(1)}, u32[]{:S(2)}) copy-start(bf16[2,144,256]{2,1,0:T(8,128)(2,1)S(1)} %collective-permute-done.4.refs_7_.refs_8_) | copy-start | bytes 442372
  59.7 15.0 %collective-permute-start.5 = (bf16[2,144,256]{2,1,0:T(8,128)(2,1)S(1)}, bf16[2,144,256]{2,1,0:T(8,128)(2,1)S(1)}, u32[]{:S(2)}, u32[]{:S(2)}) collective-permute-start(bf16[2,144,256]{2,1,0:T(8,128)(2,1)S(1)} %collective-permute-done.4.refs_7_.refs_8_), channel_id=1, source_target_pairs={{0,1},{1,0},{2,3},{3,2},{4,5},{5,4},{6,7},{7,6},{8,9},{9,8},{10,11... | collective-permute-start | bytes 442376 | tf_op jit(solution)/shard_map/ppermute | solution.py:798
  83.6 1.3 copy-start.6
  112.4 2.8 collective-permute-start.12
  116.1 14.5 %copy-start.22 = (bf16[12,144,256]{2,1,0:T(8,128)(2,1)S(1)}, bf16[12,144,256]{2,1,0:T(8,128)(2,1)}, u32[]{:S(2)}) copy-start(bf16[12,144,256]{2,1,0:T(8,128)(2,1)} %get-tuple-element.76) | copy-start | bytes 2654212
  130.2 16.0 %collective-permute-start.15 = (bf16[2368,512]{1,0:T(8,128)(2,1)}, bf16[2368,512]{1,0:T(8,128)(2,1)S(1)}, u32[]{:S(2)}, u32[]{:S(2)}) collective-permute-start(bf16[2368,512]{1,0:T(8,128)(2,1)} %get-tuple-element.82), channel_id=1, source_target_pairs={{0,1},{1,0},{2,3},{3,2},{4,5},{5,4},{6,7},{7,6},{8,9},{9,8},{10,11... | collective-permute-start | bytes 7274504 | tf_op jit(solution)/shard_map/ppermute | solution.py:798
  132.0 14.2 %collective-permute-start.13 = (bf16[6,144,256]{2,1,0:T(8,128)(2,1)S(1)}, bf16[6,144,256]{2,1,0:T(8,128)(2,1)S(1)}, u32[]{:S(2)}, u32[]{:S(2)}) collective-permute-start(bf16[6,144,256]{2,1,0:T(8,128)(2,1)S(1)} %fusion.2), channel_id=1, source_target_pairs={{2,0},{3,1},{6,4},{7,5},{10,8},{11,9},{14,12},{15,13},{18,16},{19,... | collective-permute-start | bytes 1327112 | tf_op jit(solution)/shard_map/ppermute | solution.py:823
  146.2 3.4 %copy-start.9 = (bf16[6,144,256]{2,1,0:T(8,128)(2,1)}, bf16[6,144,256]{2,1,0:T(8,128)(2,1)S(1)}, u32[]{:S(2)}) copy-start(bf16[6,144,256]{2,1,0:T(8,128)(2,1)S(1)} %collective-permute-done.13.refs_11_) | copy-start | bytes 1327108
  146.2 5.0 %collective-permute-start.14 = (bf16[6,144,256]{2,1,0:T(8,128)(2,1)S(1)}, bf16[6,144,256]{2,1,0:T(8,128)(2,1)S(1)}, u32[]{:S(2)}, u32[]{:S(2)}) collective-permute-start(bf16[6,144,256]{2,1,0:T(8,128)(2,1)S(1)} %collective-permute-done.13.refs_11_), channel_id=1, source_target_pairs={{0,1},{1,0},{2,3},{3,2},{4,5},{5,4},{6,7},{7,6},{8,9},{9,8},{10,11... | collective-permute-start | bytes 1327112 | tf_op jit(solution)/shard_map/ppermute | solution.py:798
  146.2 3.4 %copy-start.3 = (bf16[2368,512]{1,0:T(8,128)(2,1)}, bf16[2368,512]{1,0:T(8,128)(2,1)S(1)}, u32[]{:S(2)}) copy-start(bf16[2368,512]{1,0:T(8,128)(2,1)S(1)} %collective-permute-done.15.refs_13_) | copy-start | bytes 7274500
  149.6 33.7 %collective-permute-start.16 = (bf16[1184,512]{1,0:T(8,128)(2,1)S(1)}, bf16[1184,512]{1,0:T(8,128)(2,1)S(1)}, u32[]{:S(2)}, u32[]{:S(2)}) collective-permute-start(bf16[1184,512]{1,0:T(8,128)(2,1)S(1)} %get-tuple-element.101), channel_id=1, source_target_pairs={{0,4},{1,3},{2,6},{3,1},{4,0},{5,7},{6,2},{7,5},{8,12},{9,11},{10,... | collective-permute-start | bytes 3637256 | tf_op jit(solution)/shard_map/ppermute | solution.py:798
  184.3 15.6 %collective-permute-start.17 = (bf16[592,512]{1,0:T(8,128)(2,1)S(1)}, bf16[592,512]{1,0:T(8,128)(2,1)S(1)}, u32[]{:S(2)}, u32[]{:S(2)}) collective-permute-start(bf16[592,512]{1,0:T(8,128)(2,1)S(1)} %add_convert_fusion.3), channel_id=1, source_target_pairs={{0,2},{1,5},{2,0},{3,7},{4,6},{5,1},{6,4},{7,3},{8,10},{9,13},{10,... | collective-permute-start | bytes 1818632 | tf_op jit(solution)/shard_map/ppermute | solution.py:798
  207.2 20.8 %collective-permute-start.18 = (bf16[4,192,512]{2,1,0:T(8,128)(2,1)}, bf16[4,192,512]{2,1,0:T(8,128)(2,1)S(1)}, u32[]{:S(2)}, u32[]{:S(2)}) collective-permute-start(bf16[4,192,512]{2,1,0:T(8,128)(2,1)} %bitcast.59), channel_id=1, source_target_pairs={{0,1},{1,0},{2,3},{3,2},{4,5},{5,4},{6,7},{7,6},{8,9},{9,8},{10,11... | collective-permute-start | bytes 2359304 | tf_op jit(solution)/shard_map/ppermute | solution.py:798
  221.0 7.0 %copy-start.27 = (bf16[2,3,64,512]{3,2,1,0:T(8,128)(2,1)S(1)}, bf16[2,3,64,512]{3,2,1,0:T(8,128)(2,1)}, u32[]{:S(2)}) copy-start(bf16[2,3,64,512]{3,2,1,0:T(8,128)(2,1)} %get-tuple-element.91) | copy-start | bytes 1179652
  221.0 7.0 %copy-start.28 = (bf16[2,3,64,512]{3,2,1,0:T(8,128)(2,1)S(1)}, bf16[2,3,64,512]{3,2,1,0:T(8,128)(2,1)}, u32[]{:S(2)}) copy-start(bf16[2,3,64,512]{3,2,1,0:T(8,128)(2,1)} %get-tuple-element.93) | copy-start | bytes 1179652
  228.3 7.8 %collective-permute-start.19 = (bf16[2,192,512]{2,1,0:T(8,128)(2,1)S(1)}, bf16[2,192,512]{2,1,0:T(8,128)(2,1)S(1)}, u32[]{:S(2)}, u32[]{:S(2)}) collective-permute-start(bf16[2,192,512]{2,1,0:T(8,128)(2,1)S(1)} %get-tuple-element.111), channel_id=1, source_target_pairs={{0,4},{1,3},{2,6},{3,1},{4,0},{5,7},{6,2},{7,5},{8,12},{9,11},{10,... | collective-permute-start | bytes 1179656 | tf_op jit(solution)/shard_map/ppermute | solution.py:798
  228.9 3.8 %copy-start.24 = (bf16[592,512]{1,0:T(8,128)(2,1)S(1)}, bf16[592,512]{1,0:T(8,128)(2,1)}, u32[]{:S(2)}) copy-start(bf16[592,512]{1,0:T(8,128)(2,1)} %copy-done.23) | copy-start | bytes 1818628
  232.8 13.2 %collective-permute-start.23 = (bf16[336,512]{1,0:T(8,128)(2,1)S(1)}, bf16[336,512]{1,0:T(8,128)(2,1)S(1)}, u32[]{:S(2)}, u32[]{:S(2)}) collective-permute-start(bf16[336,512]{1,0:T(8,128)(2,1)S(1)} %add_convert_fusion.6), channel_id=1, source_target_pairs={{0,8},{1,17},{2,10},{3,19},{4,12},{5,21},{6,14},{7,23},{8,0},{9,25... | collective-permute-start | bytes 1032200 | tf_op jit(solution)/shard_map/ppermute | solution.py:798
  236.8 5.7 %collective-permute-start.20 = (bf16[192,512]{1,0:T(8,128)(2,1)S(1)}, bf16[192,512]{1,0:T(8,128)(2,1)S(1)}, u32[]{:S(2)}, u32[]{:S(2)}) collective-permute-start(bf16[192,512]{1,0:T(8,128)(2,1)S(1)} %fusion.6), channel_id=1, source_target_pairs={{0,2},{1,5},{2,0},{3,7},{4,6},{5,1},{6,4},{7,3},{8,10},{9,13},{10,... | collective-permute-start | bytes 589832 | tf_op jit(solution)/shard_map/ppermute | solution.py:798
  242.7 9.1 %collective-permute-start.21 = (bf16[192,512]{1,0:T(8,128)(2,1)S(1)}, bf16[192,512]{1,0:T(8,128)(2,1)S(1)}, u32[]{:S(2)}, u32[]{:S(2)}) collective-permute-start(bf16[192,512]{1,0:T(8,128)(2,1)S(1)} %fusion.3), channel_id=1, source_target_pairs={{0,16},{1,9},{2,18},{3,11},{4,20},{5,13},{6,22},{7,15},{8,24},{9,1... | collective-permute-start | bytes 589832 | tf_op jit(solution)/shard_map/ppermute | solution.py:798
  246.1 13.5 %collective-permute-start.24 = (bf16[208,512]{1,0:T(8,128)(2,1)S(1)}, bf16[208,512]{1,0:T(8,128)(2,1)S(1)}, u32[]{:S(2)}, u32[]{:S(2)}) collective-permute-start(bf16[208,512]{1,0:T(8,128)(2,1)S(1)} %add_convert_fusion.10), channel_id=1, source_target_pairs={{0,16},{1,9},{2,18},{3,11},{4,20},{5,13},{6,22},{7,15},{8,24},{9,1... | collective-permute-start | bytes 638984 | tf_op jit(solution)/shard_map/ppermute | solution.py:798
  252.5 8.0 %collective-permute-start.22 = (bf16[192,512]{1,0:T(8,128)(2,1)S(1)}, bf16[192,512]{1,0:T(8,128)(2,1)S(1)}, u32[]{:S(2)}, u32[]{:S(2)}) collective-permute-start(bf16[192,512]{1,0:T(8,128)(2,1)S(1)} %add_convert_fusion.12), channel_id=1, source_target_pairs={{0,8},{1,17},{2,10},{3,19},{4,12},{5,21},{6,14},{7,23},{8,0},{9,25... | collective-permute-start | bytes 589832 | tf_op jit(solution)/shard_map/ppermute | solution.py:798
  261.2 7.1 %collective-permute-start.25 = (bf16[272,512]{1,0:T(8,128)(2,1)S(1)}, bf16[272,512]{1,0:T(8,128)(2,1)S(1)}, u32[]{:S(2)}, u32[]{:S(2)}) collective-permute-start(bf16[272,512]{1,0:T(8,128)(2,1)S(1)} %get-tuple-element.113), channel_id=1, source_target_pairs={{0,2},{1,5},{2,0},{3,7},{4,6},{5,1},{6,4},{7,3},{8,10},{9,13},{10,... | collective-permute-start | bytes 835592 | tf_op jit(solution)/shard_map/ppermute | solution.py:798
  268.4 12.5 %copy-start.15 = (bf16[2,272,512]{2,1,0:T(8,128)(2,1)}, bf16[2,272,512]{2,1,0:T(8,128)(2,1)S(1)}, u32[]{:S(2)}) copy-start(bf16[2,272,512]{2,1,0:T(8,128)(2,1)S(1)} %pad_maximum_fusion.1.near_ref) | copy-start | bytes 1671172
  268.4 9.6 %collective-permute-start.26 = (bf16[2,272,512]{2,1,0:T(8,128)(2,1)S(1)}, bf16[2,272,512]{2,1,0:T(8,128)(2,1)S(1)}, u32[]{:S(2)}, u32[]{:S(2)}) collective-permute-start(bf16[2,272,512]{2,1,0:T(8,128)(2,1)S(1)} %pad_maximum_fusion.1.near_ref), channel_id=1, source_target_pairs={{0,4},{1,3},{2,6},{3,1},{4,0},{5,7},{6,2},{7,5},{8,12},{9,11},{10,... | collective-permute-start | bytes 1671176 | tf_op jit(solution)/shard_map/ppermute | solution.py:798
  278.0 2.9 %copy-start.16 = (bf16[2,272,512]{2,1,0:T(8,128)(2,1)}, bf16[2,272,512]{2,1,0:T(8,128)(2,1)S(1)}, u32[]{:S(2)}) copy-start(bf16[2,272,512]{2,1,0:T(8,128)(2,1)S(1)} %collective-permute-done.26.ahead_ref) | copy-start | bytes 1671172
  278.1 2.8 collective-permute-start.27
  (9 other events, 7.7 us)
